TPU v7x, 256 devices: a whole 4x4x8 slice. The times are simulated.
256 devices in a mesh: dp: 16 (over x_hi, y, core), tile: 16 (over x_lo, z).
Axes of the slice: x: 4 (x_hi: 2, x_lo: 2; x = x_hi * 2 + x_lo), y: 4, z: 8, core: 2. Of those that a mesh axis runs over, the one named last changes fastest.
Arguments:
- fields_in: bfloat16 [16, 16, 2, 32, 32, 256], P('dp', 'tile'), may hold values from -6 to 6
- state_start: float32 [16, 16, 32, 32, 256], P('dp', 'tile'), may hold values from -0.9 to 0.9
- state_adjoint: float32 [16, 16, 32, 32, 256], P('dp', 'tile'), may hold values from -12 to 12
- output_grad: bfloat16 [16, 16, 2, 8, 1024], P('dp', 'tile'), may hold values from -12 to 12
- conv_weight: bfloat16 [9, 256, 256], replicated, may hold values from -0.125 to 0.125
- w_update: bfloat16 [512, 256], replicated, may hold values from -0.25 to 0.25
- w_reset: bfloat16 [512, 256], replicated, may hold values from -0.25 to 0.25
- w_candidate: bfloat16 [512, 256], replicated, may hold values from -0.25 to 0.25
- head_weight: bfloat16 [8, 256], replicated, may hold values from -0.375 to 0.375
- neighbor_tile: int32 [16, 4], replicated, may hold values from 0 to 15, as said below
- seam_turns: int32 [16, 4], replicated, may hold values from 0 to 2, as said below
Outputs:
- grad_fields: bfloat16 [16, 16, 2, 32, 32, 256], P('dp', 'tile')
- grad_state: float32 [16, 16, 32, 32, 256], P('dp', 'tile')
- grad_conv: float32 [9, 256, 256], P(None, 'tile')
- grad_update: float32 [512, 256], P(None, 'tile')
- grad_reset: float32 [512, 256], P(None, 'tile')
- grad_candidate: float32 [512, 256], P(None, 'tile')
- grad_head: float32 [8, 256], P(None, 'tile')
Inputs may be any that keep to these rules, and one draw needn't show every extreme that they name: The tiles form a closed belt: side 1 of tile s meets side 3 of tile (s + 1) mod 16. The tiles are paired as mates (2 m + o, 2 m + 1 + o) mod 16 for one o in 0, 1; sides 0 and 2 of a tile meet sides 0 or 2 of itself or of its mate. Gluing is mutual: if side k of s meets side j of t = neighbor_tile[s, k], then neighbor_tile[t, j] = s and the side of t that meets s is j. The rotation code of the seam described with neighbor_tile: side k of tile s meets side (k + 2 - seam_turns[s, k]) mod 4 of its neighbour.
All inputs are finite; a program needn't handle non-finite values.
Results may differ from a plain program's by a relative error of at most 0.007.
Values may be sent and summed in bfloat16 or wider, within the bound.
No kernel may reach another device: no remote copies, remote signals or barrier semaphores. Data moves between devices by JAX's collectives and lax.ppermute only.
A program may use at most 128 MiB of HBM per device.

v0:
```python
import math

import jax
import jax.numpy as jnp
from jax import lax
from jax.sharding import PartitionSpec as P

CUBIC = 0.044715
ROOT = math.sqrt(2.0 / math.pi)


def with_halo(block, sides, width):
    for axis, dim in sides:
        count = lax.axis_size(axis)
        forward = [(i, i + 1) for i in range(count - 1)]
        forward.append((count - 1, 0))
        backward = [(target, source) for source, target in forward]
        low = lax.ppermute(
            lax.slice_in_dim(block, block.shape[dim] - width, None, axis=dim), axis, forward
        )
        high = lax.ppermute(lax.slice_in_dim(block, 0, width, axis=dim), axis, backward)
        block = jnp.concatenate([low, block, high], axis=dim)
    return block


def edges_of(field):
    top = field[..., 0, :, :]
    right = field[..., :, -1, :]
    bottom = jnp.flip(field[..., -1, :, :], axis=-2)
    left = jnp.flip(field[..., :, 0, :], axis=-2)
    return jnp.stack([top, right, bottom, left], axis=-3)


def add_edges(field, extra):
    field = field.at[..., 0, :, :].add(extra[..., 0, :, :])
    field = field.at[..., :, -1, :].add(extra[..., 1, :, :])
    field = field.at[..., -1, :, :].add(jnp.flip(extra[..., 2, :, :], axis=-2))
    field = field.at[..., :, 0, :].add(jnp.flip(extra[..., 3, :, :], axis=-2))
    return field


def pad_with(field, halo):
    left = jnp.flip(halo[:, 3], axis=1)[:, :, None, :]
    right = halo[:, 1][:, :, None, :]
    middle = jnp.concatenate([left, field, right], axis=2)
    corner = jnp.zeros_like(halo[:, 0, :1, :])
    top = jnp.concatenate([corner, halo[:, 0], corner], axis=1)[:, None]
    bottom = jnp.concatenate([corner, jnp.flip(halo[:, 2], axis=1), corner], axis=1)[:, None]
    return jnp.concatenate([top, middle, bottom], axis=1)


def cycle_of(grad_pad):
    top = grad_pad[:, 0, 1:-1]
    right = grad_pad[:, 1:-1, -1]
    bottom = jnp.flip(grad_pad[:, -1, 1:-1], axis=1)
    left = jnp.flip(grad_pad[:, 1:-1, 0], axis=1)
    return jnp.stack([top, right, bottom, left], axis=1)


def conv_pre(padded, conv_weight):
    side = padded.shape[1] - 2
    width = padded.shape[-1]
    result = jnp.zeros((padded.shape[0] * side * side, conv_weight.shape[2]), jnp.float32)
    for tap in range(9):
        window = padded[:, tap // 3 : tap // 3 + side, tap % 3 : tap % 3 + side, :].reshape(
            -1, width
        )
        result = result + jnp.dot(window, conv_weight[tap], preferred_element_type=jnp.float32)
    return result


def local_backward(fields, halos, state, adjoint, output_grad, weights):
    conv_weight, w_update, w_reset, w_candidate, head_weight = weights
    tiles_here = fields.shape[0]
    steps = fields.shape[1]
    side = fields.shape[2]
    width = fields.shape[-1]
    hidden = state.reshape(-1, width)
    saved = []
    for step in range(steps):
        padded = pad_with(fields[:, step], halos[:, step])
        raw_conv = conv_pre(padded, conv_weight)
        bend = jnp.tanh(ROOT * (raw_conv + CUBIC * raw_conv * raw_conv * raw_conv))
        feature = (0.5 * raw_conv * (1.0 + bend)).astype(jnp.bfloat16)
        joined = jnp.concatenate([feature, hidden.astype(jnp.bfloat16)], axis=1)
        update = jax.nn.sigmoid(jnp.dot(joined, w_update, preferred_element_type=jnp.float32))
        reset = jax.nn.sigmoid(jnp.dot(joined, w_reset, preferred_element_type=jnp.float32))
        gated = (reset * hidden).astype(jnp.bfloat16)
        joined_gate = jnp.concatenate([feature, gated], axis=1)
        candidate = jnp.tanh(jnp.dot(joined_gate, w_candidate, preferred_element_type=jnp.float32))
        following = hidden + update * (candidate - hidden)
        saved.append(
            (
                padded,
                raw_conv,
                bend,
                joined,
                update,
                reset,
                joined_gate,
                candidate,
                hidden,
                following,
            )
        )
        hidden = following
    carried = adjoint.reshape(-1, width)
    conv_grads = [jnp.zeros(conv_weight.shape[1:], jnp.float32) for tap in range(9)]
    grad_update = jnp.zeros(w_update.shape, jnp.float32)
    grad_reset = jnp.zeros(w_reset.shape, jnp.float32)
    grad_candidate = jnp.zeros(w_candidate.shape, jnp.float32)
    grad_head = jnp.zeros(head_weight.shape, jnp.float32)
    grad_middles = [None] * steps
    cycles = [None] * steps
    for step in reversed(range(steps)):
        padded, raw_conv, bend, joined, update, reset, joined_gate, candidate, hidden, following = (
            saved[step]
        )
        grad_out = jnp.transpose(output_grad[:, step], (1, 0, 2)).reshape(output_grad.shape[2], -1)
        grad_head = grad_head + jnp.dot(
            grad_out, following.astype(jnp.bfloat16), preferred_element_type=jnp.float32
        )
        overall = carried + jnp.dot(grad_out.T, head_weight, preferred_element_type=jnp.float32)
        part_cand = (overall * update * (1.0 - candidate * candidate)).astype(jnp.bfloat16)
        part_update = (overall * (candidate - hidden) * update * (1.0 - update)).astype(
            jnp.bfloat16
        )
        back_cand = jnp.dot(part_cand, w_candidate.T, preferred_element_type=jnp.float32)
        grad_gated = back_cand[:, width:]
        part_reset = (grad_gated * hidden * reset * (1.0 - reset)).astype(jnp.bfloat16)
        back_joined = jnp.dot(
            part_update, w_update.T, preferred_element_type=jnp.float32
        ) + jnp.dot(part_reset, w_reset.T, preferred_element_type=jnp.float32)
        carried = overall * (1.0 - update) + grad_gated * reset + back_joined[:, width:]
        grad_feature = back_cand[:, :width] + back_joined[:, :width]
        slope = 0.5 * (1.0 + bend) + 0.5 * raw_conv * (1.0 - bend * bend) * ROOT * (
            1.0 + 3.0 * CUBIC * raw_conv * raw_conv
        )
        part_conv = (grad_feature * slope).astype(jnp.bfloat16)
        grad_candidate = grad_candidate + jnp.dot(
            joined_gate.T, part_cand, preferred_element_type=jnp.float32
        )
        grad_update = grad_update + jnp.dot(
            joined.T, part_update, preferred_element_type=jnp.float32
        )
        grad_reset = grad_reset + jnp.dot(joined.T, part_reset, preferred_element_type=jnp.float32)
        grad_pad = jnp.zeros(padded.shape, jnp.float32)
        for tap in range(9):
            row_at = tap // 3
            col_at = tap % 3
            window = padded[:, row_at : row_at + side, col_at : col_at + side, :].reshape(-1, width)
            conv_grads[tap] = conv_grads[tap] + jnp.dot(
                window.T, part_conv, preferred_element_type=jnp.float32
            )
            spread = jnp.dot(part_conv, conv_weight[tap].T, preferred_element_type=jnp.float32)
            grad_pad = grad_pad.at[:, row_at : row_at + side, col_at : col_at + side, :].add(
                spread.reshape(tiles_here, side, side, width)
            )
        grad_middles[step] = grad_pad[:, 1:-1, 1:-1]
        cycles[step] = cycle_of(grad_pad).astype(jnp.bfloat16)
    grads = (jnp.stack(conv_grads, axis=0), grad_update, grad_reset, grad_candidate, grad_head)
    return (
        jnp.stack(grad_middles, axis=1),
        jnp.stack(cycles, axis=1),
        carried.reshape(state.shape),
        grads,
    )


def side_match(partner_tile, partner_side, tiles_there):
    sides = jnp.arange(4, dtype=jnp.int32)
    same_tile = partner_tile[:, :, None, None] == tiles_there[None, None, :, None]
    same_side = partner_side[:, :, None, None] == sides[None, None, None, :]
    return (same_tile & same_side).astype(jnp.bfloat16)


def body(
    fields_in,
    state_start,
    state_adjoint,
    output_grad,
    conv_weight,
    w_update,
    w_reset,
    w_candidate,
    head_weight,
    neighbor_tile,
    seam_turns,
):
    weights = (conv_weight, w_update, w_reset, w_candidate, head_weight)
    fields = fields_in[0]
    tiles_here = fields.shape[0]
    tiles_all = tiles_here * lax.axis_size("tile")
    first = lax.axis_index("tile") * tiles_here
    partner_tile = lax.dynamic_slice_in_dim(neighbor_tile, first, tiles_here, 0)
    turns_here = lax.dynamic_slice_in_dim(seam_turns, first, tiles_here, 0)
    partner_side = (jnp.arange(4, dtype=jnp.int32)[None, :] + 2 - turns_here) % 4
    tiles_there = (first - 1 + tiles_all + jnp.arange(tiles_here + 2, dtype=jnp.int32)) % tiles_all
    match = side_match(partner_tile, partner_side, tiles_there)

    def pick(extended):
        flat = extended.reshape(extended.shape[:3] + (-1,))
        return jnp.einsum("kirj,rtjx->ktix", match, flat, preferred_element_type=jnp.float32)

    edges = edges_of(fields)
    extended_edges = with_halo(edges, (("tile", 0),), 1)
    halos = jnp.flip(pick(extended_edges).reshape(edges.shape).astype(jnp.bfloat16), axis=-2)
    grad_middle, cycles, grad_start, grads = local_backward(
        fields, halos, state_start[0], state_adjoint[0], output_grad[0], weights
    )
    extended_cycles = with_halo(cycles, (("tile", 0),), 1)
    arrived = pick(extended_cycles)
    extra = jnp.flip(arrived.reshape(cycles.shape), axis=-2)
    grad_fields = add_edges(grad_middle, extra).astype(jnp.bfloat16)[None]
    conv_part, update_part, reset_part, candidate_part, head_part = grads
    summed = lax.psum((conv_part, update_part, reset_part, candidate_part, head_part), "dp")
    shares = (
        lax.psum_scatter(summed[0], "tile", scatter_dimension=1, tiled=True),
        lax.psum_scatter(summed[1], "tile", scatter_dimension=1, tiled=True),
        lax.psum_scatter(summed[2], "tile", scatter_dimension=1, tiled=True),
        lax.psum_scatter(summed[3], "tile", scatter_dimension=1, tiled=True),
        lax.psum_scatter(summed[4], "tile", scatter_dimension=1, tiled=True),
    )
    return (grad_fields, grad_start[None], shares[0], shares[1], shares[2], shares[3], shares[4])


def solution(mesh):
    return jax.shard_map(
        body,
        mesh=mesh,
        in_specs=(
            P("dp", "tile", None, None, None, None),
            P("dp", "tile", None, None, None),
            P("dp", "tile", None, None, None),
            P("dp", "tile", None, None, None),
            P(),
            P(),
            P(),
            P(),
            P(),
            P(),
            P(),
        ),
        out_specs=(
            P("dp", "tile", None, None, None, None),
            P("dp", "tile", None, None, None),
            P(None, "tile", None),
            P(None, "tile"),
            P(None, "tile"),
            P(None, "tile"),
            P(None, "tile"),
        ),
        check_vma=False,
    )
```

profile of v0, /device:TPU:1, one launch (start us, length us, event | category | flops | bytes accessed | tf_op | source)
XLA Modules:
  0.0 709.7 jit_solution(5768499749983313307)
XLA Ops:
  9.6 7.3 %collective-permute-start.1 = (bf16[1,2,4,32,256]{4,3,1,2,0:T(8,128)(2,1)}, bf16[1,2,4,32,256]{4,3,1,2,0:T(8,128)(2,1)}, u32[]{:S(2)}, u32[]{:S(2)}) collective-permute-start(bf16[1,2,4,32,256]{4,3,1,2,0:T(8,128)(2,1)} %pad_maximum_fusion.17), channel_id=1, source_target_pairs={{1,0},{2,1},{3,2},{4,3},{5,4},{6,5},{7,6},{8,7},{9,8},{10,9},{11,1... | collective-permute-start | bytes 393224 | tf_op jit(solution)/shard_map/ppermute | solution.py:21
  70.2 7.6 %scatter-add.90 = f32[1,34,34,256]{3,1,2,0:T(8,128)} dynamic-update-slice(f32[1,34,34,256]{3,1,2,0:T(8,128)} %scatter-add.89, f32[1,32,32,256]{3,1,2,0:T(8,128)} %fusion.23, s32[]{:T(128)} %constant.594.clone.1, s32[]{:T(128)} %bitcast.64, s32[]{:T(128)} %bitcast.65, s32[]{:T(128)} %constant.594.clone.1) | dynamic-update-slice | bytes 2097156 | tf_op jit(solution)/shard_map/scatter-add | solution.py:156
  77.7 4.8 add_select_fusion
  82.5 7.4 %scatter-add.91 = f32[1,34,34,256]{3,1,2,0:T(8,128)} dynamic-update-slice(f32[1,34,34,256]{3,1,2,0:T(8,128)} %scatter-add.90, f32[1,32,32,256]{3,1,2,0:T(8,128)} %add_select_fusion, s32[]{:T(128)} %constant.594.clone.1, s32[]{:T(128)} %bitcast.68, s32[]{:T(128)} %bitcast.69, s32[]{:T(128)} %constant.594.clone.1) | dynamic-update-slice | bytes 2097156 | tf_op jit(solution)/shard_map/scatter-add | solution.py:156
  89.9 2.8 fusion.24
  92.7 6.2 scatter-add.75
  104.5 6.2 scatter-add.76
  114.3 4.9 scatter-add.80
  121.4 4.9 scatter-add.81
  130.2 6.1 scatter-add.94
  136.3 4.9 scatter-add.85
  144.6 2.8 fusion.25
  152.4 4.9 scatter-add.86
  160.1 6.1 scatter-add.95
  186.6 5.8 scatter-add.96
  194.3 5.8 scatter-add.99
  202.0 5.8 scatter-add.100
  209.7 5.8 scatter-add.101
  220.7 3.6 collective-permute-start.3
  233.8 35.2 %reduce-scatter.14.cloned.1.call-done = f32[512,16]{0,1:T(8,128)} async-done(((f32[512,256]{0,1:T(8,128)}), f32[512,16]{0,1:T(8,128)}) %reduce-scatter.14.cloned.1.call-update) | async-done | bytes 32784 | tf_op jit(solution)/shard_map/reduce_scatter | solution.py:221
  269.0 69.5 %reduce-scatter.12.cloned.1.call-done = f32[512,16]{0,1:T(8,128)} async-done(((f32[512,256]{0,1:T(8,128)}), f32[512,16]{0,1:T(8,128)}) %reduce-scatter.12.cloned.1.call-update) | async-done | bytes 32784 | tf_op jit(solution)/shard_map/reduce_scatter | solution.py:220
  338.6 73.6 %reduce-scatter.8.cloned.1.call-done = f32[9,16,256]{2,1,0:T(8,128)} async-done(((f32[9,256,256]{2,1,0:T(8,128)}), f32[9,16,256]{2,1,0:T(8,128)}) %reduce-scatter.8.cloned.1.call-update) | async-done | bytes 147472 | tf_op jit(solution)/shard_map/reduce_scatter | solution.py:218
  413.9 145.7 %all-reduce.8.cloned.1.call-done = (f32[512,16]{0,1:T(8,128)}, f32[512,16]{0,1:T(8,128)}, f32[512,16]{0,1:T(8,128)}, f32[8,16]{1,0:T(8,128)}) async-done(((f32[512,16]{0,1:T(8,128)}, f32[512,16]{0,1:T(8,128)}, f32[512,16]{0,1:T(8,128)}, f32[8,16]{1,0:T(8,128)}), (f32[512,16]{0,1:T(8,128)}, f32[512,16]{0,1:T(8,128)}, f32[512,16]{0,1:T(8,128)}, f32[8,16]{1,0:T(8,128)})) %all-reduce.8.cloned.1.call-update) | async-done | bytes 98832 | tf_op jit(solution)/shard_map/psum | solution.py:216
  559.6 136.1 %all-reduce.6.cloned.1.call-done = f32[9,16,256]{2,1,0:T(8,128)} async-done(((f32[9,16,256]{2,1,0:T(8,128)}), f32[9,16,256]{2,1,0:T(8,128)}) %all-reduce.6.cloned.1.call-update) | async-done | bytes 147472 | tf_op jit(solution)/shard_map/psum | solution.py:216
  (318 shorter events, 130.1 us)
Async XLA Ops:
  7.2 33.6 %copy-start = (bf16[512,256]{1,0:T(8,128)(2,1)S(1)}, bf16[512,256]{1,0:T(8,128)(2,1)}, u32[]{:S(2)}) copy-start(bf16[512,256]{1,0:T(8,128)(2,1)} %param.60) | copy-start | bytes 786436
  7.2 220.2 %reduce-scatter.16.cloned.1.call-start = ((), (), s32[]{:S(2)}) async-start(), calls=%async_computation.10 | async-start | bytes 139264
  9.6 13.6 %collective-permute-start.1 = (bf16[1,2,4,32,256]{4,3,1,2,0:T(8,128)(2,1)}, bf16[1,2,4,32,256]{4,3,1,2,0:T(8,128)(2,1)}, u32[]{:S(2)}, u32[]{:S(2)}) collective-permute-start(bf16[1,2,4,32,256]{4,3,1,2,0:T(8,128)(2,1)} %pad_maximum_fusion.17), channel_id=1, source_target_pairs={{1,0},{2,1},{3,2},{4,3},{5,4},{6,5},{7,6},{8,7},{9,8},{10,9},{11,1... | collective-permute-start | bytes 393224 | tf_op jit(solution)/shard_map/ppermute | solution.py:21
  16.9 6.3 collective-permute-start
  27.3 10.3 %copy-start.17 = (bf16[1,32,32,256]{3,2,1,0:T(8,128)(2,1)}, bf16[1,32,32,256]{3,2,1,0:T(8,128)(2,1)S(1)}, u32[]{:S(2)}) copy-start(bf16[1,32,32,256]{3,2,1,0:T(8,128)(2,1)S(1)} %get-tuple-element.327) | copy-start | bytes 1572868
  27.8 4.7 copy-start.5
  28.7 5.5 copy-start.12
  28.7 5.8 copy-start.10
  28.7 6.1 copy-start.27
  29.5 5.9 copy-start.20
  29.5 6.2 copy-start.21
  35.3 5.4 copy-start.52
  38.8 5.0 copy-start.42
  41.3 25.0 %copy-start.44 = (bf16[1024,256]{1,0:T(8,128)(2,1)}, bf16[1024,256]{1,0:T(8,128)(2,1)S(1)}, u32[]{:S(2)}) copy-start(bf16[1024,256]{1,0:T(8,128)(2,1)S(1)} %get-tuple-element.303) | copy-start | bytes 1572868
  67.3 166.5 %reduce-scatter.10.cloned.1.call-start = ((), (), s32[]{:S(2)}) async-start(), calls=%async_computation.7 | async-start | bytes 557056 | tf_op jit(solution)/shard_map/reduce_scatter | solution.py:219
  141.2 127.8 %reduce-scatter.14.cloned.1.call-start = ((), (), s32[]{:S(2)}) async-start(), calls=%async_computation.9 | async-start | bytes 557056 | tf_op jit(solution)/shard_map/reduce_scatter | solution.py:221
  149.7 188.8 %reduce-scatter.12.cloned.1.call-start = ((), (), s32[]{:S(2)}) async-start(), calls=%async_computation.8 | async-start | bytes 557056 | tf_op jit(solution)/shard_map/reduce_scatter | solution.py:220
  173.3 238.9 %reduce-scatter.8.cloned.1.call-start = ((), (), s32[]{:S(2)}) async-start(), calls=%async_computation.5 | async-start | bytes 2506752 | tf_op jit(solution)/shard_map/reduce_scatter | solution.py:218
  173.6 4.3 copy-start.6
  184.7 374.9 %all-reduce.8.cloned.1.call-start = ((), (), s32[]{:S(2)}) async-start(), calls=%async_computation.11 | async-start | bytes 204800 | tf_op jit(solution)/shard_map/psum | solution.py:216
  220.7 8.1 %collective-permute-start.3 = (bf16[1,2,4,32,256]{4,3,2,1,0:T(8,128)(2,1)S(1)}, bf16[1,2,4,32,256]{4,3,2,1,0:T(8,128)(2,1)S(1)}, u32[]{:S(2)}, u32[]{:S(2)}) collective-permute-start(bf16[1,2,4,32,256]{4,3,2,1,0:T(8,128)(2,1)S(1)} %maximum_maximum_fusion.2), channel_id=1, source_target_pairs={{1,0},{2,1},{3,2},{4,3},{5,4},{6,5},{7,6},{8,7},{9,8},{10,9},{11,1... | collective-permute-start | bytes 393224 | tf_op jit(solution)/shard_map/ppermute | solution.py:21
  224.3 6.1 collective-permute-start.2
  338.5 357.2 %all-reduce.6.cloned.1.call-start = ((), (), s32[]{:S(2)}) async-start(), calls=%async_computation.6 | async-start | bytes 294912 | tf_op jit(solution)/shard_map/psum | solution.py:216
  412.2 290.5 %copy-start.1 = (bf16[512,256]{1,0:T(8,128)(2,1)S(1)}, bf16[512,256]{1,0:T(8,128)(2,1)}, u32[]{:S(2)}) copy-start(bf16[512,256]{1,0:T(8,128)(2,1)} %param.60) | copy-start | bytes 786436
  (45 other events, 92.9 us)
Sparse Core Ops, SparseCore 0:
  67.4 56.8 reduce-scatter.15
  141.4 58.0 reduce-scatter.9
  202.0 67.0 reduce-scatter.13
  272.1 66.3 reduce-scatter.11
  340.9 71.2 reduce-scatter.7
  415.4 144.1 all-reduce.7
  562.4 133.2 all-reduce.5
where the time goes:
time: 716 us; the launch traced here: 710 us
  waiting for transfers between devices  462 us (65%)
  local copies, waits for them, and re-layouts  122 us (17%)
  matrix products  87 us (12%)
  between operations  15.8 us (2%)
  other arithmetic  11.6 us (2%)
  starting transfers between devices  11.4 us (2%)
    psum x2, waiting for transfers between devices, body(): lax.psum((conv_part, update_part, reset_part, candidate_part, head_part),...  282 us
    scatter-add x18, local copies, waits for them, and re-layouts, local_backward(): grad_pad.at[:, row_at:row_at + side, col_at:col_at + side, :]  86.5 us
    reduce_scatter x1, waiting for transfers between devices, body(): lax.psum_scatter(summed[0], 'tile', scatter_dimension=1, tiled=True)  73.6 us
    reduce_scatter x1, waiting for transfers between devices, body(): lax.psum_scatter(summed[2], 'tile', scatter_dimension=1, tiled=True)  69.5 us
    dot_general x18, matrix products, local_backward(): jnp.dot(part_conv, conv_weight[tap].T, preferred_element_type=jnp.float32)  38.1 us
    reduce_scatter x1, waiting for transfers between devices, body(): lax.psum_scatter(summed[3], 'tile', scatter_dimension=1, tiled=True)  35.2 us
    dot_general x18, matrix products, local_backward(): jnp.dot(window.T, part_conv, preferred_element_type=jnp.float32)  22.4 us
    unnamed x130, local copies, waits for them, and re-layouts  18 us
  transfers between devices with their start and end apart: 11, of which 6 were waited for; matrix products, arithmetic and copies ran while one was open for 24% of the time, Pallas kernels for 0%

commit v1 on v0

v1 whole, which is shorter than its diff:
```python
import math

import jax
import jax.numpy as jnp
from jax import lax
from jax.experimental import pallas as pl
from jax.experimental.pallas import tpu as pltpu
from jax.sharding import Mesh
from jax.sharding import PartitionSpec as P

CUBIC = 0.044715
ROOT = math.sqrt(2.0 / math.pi)
BF = jnp.bfloat16
F32 = jnp.float32
SIDE = 32
CELLS = SIDE * SIDE
C = 256
STEPS = 2
CHUNK = 256
VMEM_LIMIT = 60 * 1024 * 1024


def mm(a, b):
    return lax.dot_general(a, b, (((1,), (0,)), ((), ())), preferred_element_type=F32)


def mm_nt(a, b):
    return lax.dot_general(a, b, (((1,), (1,)), ((), ())), preferred_element_type=F32)


def mm_tn(a, b):
    return lax.dot_general(a, b, (((0,), (0,)), ((), ())), preferred_element_type=F32)


def one_hot(cond):
    return jnp.where(cond, 1.0, 0.0).astype(BF)


def iota(shape, dim):
    return lax.broadcasted_iota(jnp.int32, shape, dim)


def column_pick(first_col):
    rows = iota((SIDE, CELLS), 0)
    cells = iota((SIDE, CELLS), 1)
    return one_hot(cells == rows * SIDE + first_col)


def edges_kernel(fields_ref, to_next_ref, to_prev_ref):
    left = column_pick(0)
    right = column_pick(SIDE - 1)
    for step in range(STEPS):
        flat = fields_ref[step].reshape(CELLS, C)
        to_next_ref[step, 0] = mm(right, flat).astype(BF)
        to_prev_ref[step, 0] = mm(left, flat).astype(BF)
        for ref in (to_next_ref, to_prev_ref):
            ref[step, 1] = fields_ref[step, 0]
            ref[step, 2] = fields_ref[step, SIDE - 1]


def seam_rows(info_ref, own_top, own_bottom, from_prev, from_next):
    stacked = jnp.concatenate(
        [own_top, own_bottom, from_prev[1], from_prev[2], from_next[1], from_next[2]], axis=0
    )
    rows = iota((2 * SIDE, 6 * SIDE), 0)
    cols = iota((2 * SIDE, 6 * SIDE), 1)
    top_base, top_sign, bottom_base, bottom_sign = (info_ref[i] for i in range(4))
    wanted = jnp.where(
        rows < SIDE, top_base + top_sign * rows, bottom_base + bottom_sign * (rows - SIDE)
    )
    return mm(one_hot(cols == wanted), stacked)


def store_shifts(ref, step, low, high, middle, left, right):
    col = iota((SIDE, SIDE, C), 1)
    before = jnp.where(col == 0, left[:, None, :], pltpu.roll(middle, 1, axis=1))
    after = jnp.where(col == SIDE - 1, right[:, None, :], pltpu.roll(middle, SIDE - 1, axis=1))
    body = pl.ds(SIDE, CELLS)
    ref[step, body, 0:C] = before.reshape(CELLS, C).astype(BF)
    ref[step, body, C : 2 * C] = middle.reshape(CELLS, C).astype(BF)
    ref[step, body, 2 * C : 3 * C] = after.reshape(CELLS, C).astype(BF)
    col = iota((SIDE, C), 0)
    for at, line in ((0, low), (SIDE + CELLS, high)):
        row = pl.ds(at, SIDE)
        ref[step, row, 0:C] = jnp.where(col == 0, 0.0, pltpu.roll(line, 1, axis=0)).astype(BF)
        ref[step, row, C : 2 * C] = line.astype(BF)
        ref[step, row, 2 * C : 3 * C] = jnp.where(
            col == SIDE - 1, 0.0, pltpu.roll(line, SIDE - 1, axis=0)
        ).astype(BF)


def main_kernel(
    info_ref,
    fields_ref,
    prev_ref,
    next_ref,
    state_ref,
    adjoint_ref,
    grad_out_ref,
    conv_ref,
    update_ref,
    reset_ref,
    candidate_ref,
    head_ref,
    grad_state_ref,
    part_conv_ref,
    to_next_ref,
    to_prev_ref,
    keep_ref,
    send_ref,
    windows,
    joined,
    gated_all,
    parts,
    last_state,
):
    for step in range(STEPS):
        seams = seam_rows(
            info_ref, fields_ref[step, 0], fields_ref[step, SIDE - 1], prev_ref[step], next_ref[step]
        )
        store_shifts(
            windows,
            step,
            seams[:SIDE],
            seams[SIDE:],
            fields_ref[step].astype(F32),
            prev_ref[step, 0].astype(F32),
            next_ref[step, 0].astype(F32),
        )

    def chunk(index, _):
        start = pl.multiple_of(index * CHUNK, CHUNK)
        rows = pl.ds(start, CHUNK)
        hidden = state_ref[rows, :]
        saved = []
        for step in range(STEPS):
            raw = jnp.zeros((CHUNK, C), F32)
            for p in range(3):
                window = windows[step, pl.ds(start + p * SIDE, CHUNK), :]
                raw = raw + mm(window, conv_ref[pl.ds(3 * C * p, 3 * C), :])
            bend = jnp.tanh(raw * (ROOT + (ROOT * CUBIC) * (raw * raw)))
            feature = (0.5 * raw * (1.0 + bend)).astype(BF)
            joined[step, rows, 0:C] = feature
            joined[step, rows, C : 2 * C] = hidden.astype(BF)
            both = joined[step, rows, :]
            update = 0.5 * jnp.tanh(0.5 * mm(both, update_ref[...])) + 0.5
            reset = 0.5 * jnp.tanh(0.5 * mm(both, reset_ref[...])) + 0.5
            gated = (reset * hidden).astype(BF)
            gated_all[step, rows, :] = gated
            candidate = jnp.tanh(
                mm(feature, candidate_ref[0:C, :]) + mm(gated, candidate_ref[C : 2 * C, :])
            )
            following = hidden + update * (candidate - hidden)
            saved.append((raw, bend, update, reset, candidate, hidden))
            hidden = following
        last_state[rows, :] = hidden.astype(BF)
        carried = adjoint_ref[rows, :]
        for step in reversed(range(STEPS)):
            raw, bend, update, reset, candidate, hidden = saved[step]
            total = carried + mm_tn(grad_out_ref[step, :, rows], head_ref[...])
            keep = 1.0 - update
            scaled = total * update
            part_cand = (scaled * (1.0 - candidate * candidate)).astype(BF)
            part_update = (scaled * (candidate - hidden) * keep).astype(BF)
            grad_gated = mm_nt(part_cand, candidate_ref[C : 2 * C, :])
            part_reset = (grad_gated * hidden * reset * (1.0 - reset)).astype(BF)
            parts[step, rows, 0:C] = part_cand
            parts[step, rows, C : 2 * C] = part_update
            parts[step, rows, 2 * C : 3 * C] = part_reset
            carried = (
                total * keep
                + grad_gated * reset
                + mm_nt(part_update, update_ref[C : 2 * C, :])
                + mm_nt(part_reset, reset_ref[C : 2 * C, :])
            )
            grad_feature = (
                mm_nt(part_cand, candidate_ref[0:C, :])
                + mm_nt(part_update, update_ref[0:C, :])
                + mm_nt(part_reset, reset_ref[0:C, :])
            )
            slope = 0.5 * (1.0 + bend) + (0.5 * ROOT) * raw * (1.0 - bend * bend) * (
                1.0 + (3.0 * CUBIC) * (raw * raw)
            )
            part_conv_ref[step, rows, :] = (grad_feature * slope).astype(BF)
        grad_state_ref[rows, :] = carried
        return 0

    lax.fori_loop(0, CELLS // CHUNK, chunk, 0)

    core = info_ref[4]

    def share(block, value):
        value = value.reshape(16, 16, C)
        rows = pl.ds((block % 8) * 16, 16)

        @pl.when(core == block // 8)
        def _():
            keep_ref[:, rows, :] = value

        @pl.when(core != block // 8)
        def _():
            send_ref[:, rows, :] = value.astype(BF)

    def over_steps(one):
        return one(0) + one(1)

    for gate in range(2):
        lanes = slice(C * (gate + 1), C * (gate + 2))
        grad = over_steps(lambda s: mm_tn(parts[s, :, lanes], joined[s]))
        share(9 + 2 * gate, grad[:, :C])
        share(10 + 2 * gate, grad[:, C:])
    share(13, over_steps(lambda s: mm_tn(parts[s, :, 0:C], joined[s, :, 0:C])))
    share(14, over_steps(lambda s: mm_tn(parts[s, :, 0:C], gated_all[s])))
    grad_head = mm(grad_out_ref[0], joined[1, :, C : 2 * C]) + mm(grad_out_ref[1], last_state[...])
    grad_head = jnp.concatenate([grad_head, jnp.zeros((C - 8, C), F32)], axis=0)
    share(15, grad_head.T)
    for p in range(3):
        grad = over_steps(
            lambda s: mm_tn(part_conv_ref[s], windows[s, pl.ds(p * SIDE, CELLS), :])
        )
        for q in range(3):
            share(3 * p + q, grad[:, q * C : (q + 1) * C].T)

    picks = []
    row = iota((SIDE, CELLS), 0)
    cell = iota((SIDE, CELLS), 1)
    for col in (0, SIDE - 1):
        for p in range(3):
            at = row + 1 - p
            picks.append(one_hot((cell == at * SIDE + col) & (at >= 0) & (at < SIDE)))
    for line in (0, SIDE - 1):
        for q in range(3):
            at = row + 1 - q
            picks.append(one_hot((cell == line * SIDE + at) & (at >= 0) & (at < SIDE)))
    picks = jnp.concatenate(picks, axis=0)
    taps = [0, 3, 6, 2, 5, 8, 0, 1, 2, 6, 7, 8]
    for step in range(STEPS):
        picked = mm(picks, part_conv_ref[step]).astype(BF)
        outside = []
        for side in range(4):
            total = jnp.zeros((SIDE, C), F32)
            for k in range(3 * side, 3 * side + 3):
                total = total + mm_nt(
                    picked[k * SIDE : (k + 1) * SIDE], conv_ref[taps[k] * C : (taps[k] + 1) * C, :]
                )
            outside.append(total.astype(BF))
        to_next_ref[step, 0] = outside[1]
        to_prev_ref[step, 0] = outside[0]
        for ref in (to_next_ref, to_prev_ref):
            ref[step, 1] = outside[2]
            ref[step, 2] = outside[3]


def fields_kernel(
    info_ref,
    part_conv_ref,
    own_ref,
    prev_ref,
    next_ref,
    conv_ref,
    grad_fields_ref,
    shifted,
):
    zero = jnp.zeros((SIDE, C), F32)
    for step in range(STEPS):
        store_shifts(
            shifted,
            step,
            zero,
            zero,
            part_conv_ref[step].astype(F32).reshape(SIDE, SIDE, C),
            zero,
            zero,
        )
        seams = seam_rows(info_ref, own_ref[step, 1], own_ref[step, 2], prev_ref[step], next_ref[step])
        left = prev_ref[step, 0].astype(F32)
        right = next_ref[step, 0].astype(F32)
        for part in range(4):
            at = part * 8
            grad = jnp.zeros((CHUNK, C), F32)
            for p in range(3):
                for q in range(3):
                    lanes = slice((2 - q) * C, (3 - q) * C)
                    window = shifted[step, pl.ds((at + 2 - p) * SIDE, CHUNK), lanes]
                    tap = 3 * p + q
                    grad = grad + mm_nt(window, conv_ref[tap * C : (tap + 1) * C, :])
            grad = grad.reshape(8, SIDE, C)
            col = iota((8, SIDE, C), 1)
            row = iota((8, SIDE, C), 0)
            grad = grad + jnp.where(col == 0, left[at : at + 8][:, None, :], 0.0)
            grad = grad + jnp.where(col == SIDE - 1, right[at : at + 8][:, None, :], 0.0)
            if part == 0:
                grad = grad + jnp.where(row == 0, seams[:SIDE][None], 0.0)
            if part == 3:
                grad = grad + jnp.where(row == 7, seams[SIDE:][None], 0.0)
            grad_fields_ref[step, at : at + 8] = grad.astype(BF)


def in_vmem():
    return pl.BlockSpec(memory_space=pltpu.VMEM)


def in_smem():
    return pl.BlockSpec(memory_space=pltpu.SMEM)


def params():
    return pltpu.CompilerParams(vmem_limit_bytes=VMEM_LIMIT)


def shape(dims, kind=BF):
    return jax.ShapeDtypeStruct(dims, kind)


EDGE = (STEPS, 3, SIDE, C)


def edges_call(fields):
    return pl.pallas_call(
        edges_kernel,
        out_shape=(shape(EDGE), shape(EDGE)),
        in_specs=[in_vmem()],
        out_specs=(in_vmem(), in_vmem()),
        compiler_params=params(),
        name="edges",
    )(fields)


def main_call(info, fields, prev, following, state, adjoint, grad_out, conv, update, reset, cand, head):
    return pl.pallas_call(
        main_kernel,
        out_shape=(
            shape((CELLS, C), F32),
            shape((STEPS, CELLS, C)),
            shape(EDGE),
            shape(EDGE),
            shape((16, 128, C), F32),
            shape((16, 128, C)),
        ),
        in_specs=[in_smem()] + [in_vmem()] * 11,
        out_specs=tuple([in_vmem()] * 6),
        scratch_shapes=[
            pltpu.VMEM((STEPS, CELLS + 2 * SIDE, 3 * C), BF),
            pltpu.VMEM((STEPS, CELLS, 2 * C), BF),
            pltpu.VMEM((STEPS, CELLS, C), BF),
            pltpu.VMEM((STEPS, CELLS, 3 * C), BF),
            pltpu.VMEM((CELLS, C), BF),
        ],
        compiler_params=params(),
        name="steps",
    )(info, fields, prev, following, state, adjoint, grad_out, conv, update, reset, cand, head)


def fields_call(info, part_conv, own, prev, following, conv):
    return pl.pallas_call(
        fields_kernel,
        out_shape=shape((STEPS, SIDE, SIDE, C)),
        in_specs=[in_smem()] + [in_vmem()] * 5,
        out_specs=in_vmem(),
        scratch_shapes=[pltpu.VMEM((STEPS, CELLS + 2 * SIDE, 3 * C), BF)],
        compiler_params=params(),
        cost_estimate=pl.CostEstimate(
            flops=2 * STEPS * CELLS * C * C * 9, bytes_accessed=4 << 20, transcendentals=0
        ),
        name="fields",
    )(info, part_conv, own, prev, following, conv)


def seam_info(tile, core, neighbor_tile, seam_turns):
    partner = lax.dynamic_slice_in_dim(neighbor_tile, tile, 1, 0)[0]
    turns = lax.dynamic_slice_in_dim(seam_turns, tile, 1, 0)[0]
    words = []
    for side in (0, 2):
        other = (side + 2 - turns[side]) % 4
        place = jnp.where(
            partner[side] == tile, 0, jnp.where(partner[side] == (tile + 15) % 16, 1, 2)
        )
        flip = other == side
        base = (2 * place + other // 2) * SIDE
        words.append(jnp.where(flip, base + SIDE - 1, base))
        words.append(jnp.where(flip, -1, 1))
    return jnp.stack(words + [core, core, core, core]).astype(jnp.int32)


RING = [(i, (i + 1) % 16) for i in range(16)]
BACK = [((i + 1) % 16, i) for i in range(16)]


def reduce_weights(keep, send):
    y = lax.axis_index("y")
    got = lax.ppermute(send, "core", [(0, 1), (1, 0)])
    held = (keep + got.astype(F32)).reshape(16, 4, 2, 16, C)
    up = [(i, (i + 1) % 4) for i in range(4)]
    down = [((i + 1) % 4, i) for i in range(4)]

    def at(offset):
        return lax.dynamic_index_in_dim(held, (y + offset) % 4, 1, keepdims=False)

    far = at(2).astype(BF)
    from_low = lax.ppermute(far[:, 0], "y", up).astype(F32)
    from_high = lax.ppermute(far[:, 1], "y", down).astype(F32)
    above, below = at(1), at(3)
    above = jnp.stack([above[:, 0] + from_low, above[:, 1]], axis=1).astype(BF)
    below = jnp.stack([below[:, 0], below[:, 1] + from_high], axis=1).astype(BF)
    from_low = lax.ppermute(above, "y", up).astype(F32)
    from_high = lax.ppermute(below, "y", down).astype(F32)
    mine = (at(0) + from_low + from_high).astype(BF).reshape(16, 32, C)
    mine = lax.all_to_all(mine, ("x_lo", "z"), 0, 0, tiled=True)
    mine = jnp.sum(mine.astype(F32), axis=0)
    spread = jnp.broadcast_to(mine[None], (16, 32, C))
    whole = lax.all_to_all(spread, ("x_hi", "y", "core"), 0, 0, tiled=True)
    whole = whole.reshape(2, 4, 2, 32, C)
    whole = whole[0] + whole[1]
    return jnp.transpose(whole, (1, 0, 2, 3)).reshape(16, 16, C)


def body(
    fields_in,
    state_start,
    state_adjoint,
    output_grad,
    conv_weight,
    w_update,
    w_reset,
    w_candidate,
    head_weight,
    neighbor_tile,
    seam_turns,
):
    tile = lax.axis_index(("x_lo", "z"))
    core = lax.axis_index("core")
    info = seam_info(tile, core, neighbor_tile, seam_turns)
    fields = fields_in[0, 0]
    conv = conv_weight.reshape(9 * C, C)
    to_next, to_prev = edges_call(fields)
    prev = lax.ppermute(to_next, ("x_lo", "z"), RING)
    following = lax.ppermute(to_prev, ("x_lo", "z"), BACK)
    grad_state, part_conv, out_next, out_prev, keep, send = main_call(
        info,
        fields,
        prev,
        following,
        state_start.reshape(CELLS, C),
        state_adjoint.reshape(CELLS, C),
        output_grad[0, 0],
        conv,
        w_update,
        w_reset,
        w_candidate,
        head_weight,
    )
    prev = lax.ppermute(out_next, ("x_lo", "z"), RING)
    following = lax.ppermute(out_prev, ("x_lo", "z"), BACK)
    grad_fields = fields_call(info, part_conv, out_next, prev, following, conv)
    total = reduce_weights(keep, send)

    def gate(first):
        return jnp.concatenate([total[first], total[first + 1]], axis=1).T

    return (
        grad_fields[None, None],
        grad_state.reshape(1, 1, SIDE, SIDE, C),
        total[:9],
        gate(9),
        gate(11),
        gate(13),
        total[15, :, :8].T,
    )


def solution(mesh):
    cube = Mesh(mesh.devices.reshape(2, 4, 2, 2, 8), ("x_hi", "y", "core", "x_lo", "z"))
    dp = ("x_hi", "y", "core")
    tile = ("x_lo", "z")
    return jax.shard_map(
        body,
        mesh=cube,
        in_specs=(
            P(dp, tile, None, None, None, None),
            P(dp, tile, None, None, None),
            P(dp, tile, None, None, None),
            P(dp, tile, None, None, None),
            P(),
            P(),
            P(),
            P(),
            P(),
            P(),
            P(),
        ),
        out_specs=(
            P(dp, tile, None, None, None, None),
            P(dp, tile, None, None, None),
            P(None, tile, None),
            P(None, tile),
            P(None, tile),
            P(None, tile),
            P(None, tile),
        ),
        check_vma=False,
    )
```

time: 716 us -> 107 us (0.15)
  waiting for transfers between devices: 462 us -> 15.9 us
  local copies, waits for them, and re-layouts: 122 us -> 6.26 us
  matrix products: 87 us -> 0 us
  Pallas kernels: 0 us -> 36 us
  starting transfers between devices: 11.4 us -> 26.3 us
  blocking collectives: 0 us -> 13.6 us
  between operations: 15.8 us -> 4.81 us
  other arithmetic: 11.6 us -> 4.02 us
    psum x2 -> x0, waiting for transfers between devices: 282 us -> none  [body(): lax.psum((conv_part, update_part, reset_part, candidate_part, head_part),...]
    reduce_scatter x4 -> x0, waiting for transfers between devices: 178 us -> none  [the longest x1 73.6 us: body(): lax.psum_scatter(summed[0], 'tile', scatter_dimension=1, tiled=True)]
    scatter-add x20 -> x0, local copies, waits for them, and re-layouts: 88.1 us -> none  [the longest x18 86.5 us: local_backward(): grad_pad.at[:, row_at:row_at + side, col_at:col_at + side, :]]
    dot_general x78 -> x0, matrix products: 87 us -> none  [the longest x18 38.1 us: local_backward(): jnp.dot(part_conv, conv_weight[tap].T, preferred_element_type=jnp.float32)]
    pallas_call x0 -> x3, Pallas kernels: none -> 36 us  [the longest x1 28.2 us: main_call(): pl.pallas_call(main_kernel, out_shape=(shape((CELLS, C), F32), shape((STE...]
    unnamed x130 -> x12, local copies, waits for them, and re-layouts: 18 us -> 1.33 us
    all_to_all x0 -> x1, blocking collectives: none -> 13.6 us  [reduce_weights(): mine = lax.all_to_all(mine, ('x_lo', 'z'), 0, 0, tiled=True)]
    ppermute x4 -> x9, waiting for transfers between devices: 1.64 us -> 15.1 us  [the longest x1 4.23 us: reduce_weights(): from_high = lax.ppermute(below, 'y', down).astype(F32)]
  transfers between devices with their start and end apart: 11 -> 10, of which waited for: 6 -> 6; matrix products, arithmetic and copies ran while one was open for 24% -> 3% of each run, Pallas kernels for 0% -> 5%
where the time goes in v1:
time: 107 us
  Pallas kernels  36 us (34%)
  starting transfers between devices  26.3 us (25%)
  waiting for transfers between devices  15.9 us (15%)
  blocking collectives  13.6 us (13%)
  local copies, waits for them, and re-layouts  6.26 us (6%)
  between operations  4.81 us (4%)
  other arithmetic  4.02 us (4%)
    pallas_call x1, Pallas kernels, main_call(): pl.pallas_call(main_kernel, out_shape=(shape((CELLS, C), F32), shape((STE...  28.2 us
    all_to_all x1, blocking collectives, reduce_weights(): mine = lax.all_to_all(mine, ('x_lo', 'z'), 0, 0, tiled=True)  13.6 us
    all_to_all x1, starting transfers between devices, reduce_weights(): whole = lax.all_to_all(spread, ('x_hi', 'y', 'core'), 0, 0, tiled=True)  7.87 us
    pallas_call x1, Pallas kernels, fields_call(): pl.pallas_call(fields_kernel, out_shape=shape((STEPS, SIDE, SIDE, C)), in...  5.39 us
    ppermute x1, starting transfers between devices, body(): following = lax.ppermute(to_prev, ('x_lo', 'z'), BACK)  4.87 us
    ppermute x1, waiting for transfers between devices, reduce_weights(): from_high = lax.ppermute(below, 'y', down).astype(F32)  4.23 us
    ppermute x1, starting transfers between devices, reduce_weights(): from_high = lax.ppermute(below, 'y', down).astype(F32)  3.49 us
    ppermute x1, waiting for transfers between devices, reduce_weights(): from_low = lax.ppermute(above, 'y', up).astype(F32)  3.28 us
  transfers between devices with their start and end apart: 10, of which 6 were waited for; matrix products, arithmetic and copies ran while one was open for 3% of the time, Pallas kernels for 5%

profile of v1, /device:TPU:1, one launch (start us, length us, event | category | flops | bytes accessed | tf_op | source)
XLA Modules:
  0.0 106.8 jit_solution(7714043617773867207)
XLA Ops:
  0.6 2.4 %edges.1 = (bf16[2,3,32,256]{3,2,1,0:T(8,128)(2,1)}, bf16[2,3,32,256]{3,2,1,0:T(8,128)(2,1)}) custom-call(bf16[2,32,32,256]{3,2,1,0:T(8,128)(2,1)} %bitcast.84), custom_call_target="tpu_custom_call" | custom-call | tf_op jit(solution)/shard_map/edges/pallas_call | solution.py:319
  3.0 2.5 %collective-permute-start = (bf16[2,3,32,256]{3,2,1,0:T(8,128)(2,1)}, bf16[2,3,32,256]{3,2,1,0:T(8,128)(2,1)S(1)}, u32[]{:S(2)}, u32[]{:S(2)}) collective-permute-start(bf16[2,3,32,256]{3,2,1,0:T(8,128)(2,1)} %get-tuple-element.15), channel_id=1, source_target_pairs={{0,1},{1,2},{2,3},{3,4},{4,5},{5,6},{6,7},{7,8},{8,9},{9,10},{10,1... | collective-permute-start | bytes 294920 | tf_op jit(solution)/shard_map/ppermute | solution.py:436
  5.5 4.9 %collective-permute-start.1 = (bf16[2,3,32,256]{3,2,1,0:T(8,128)(2,1)}, bf16[2,3,32,256]{3,2,1,0:T(8,128)(2,1)S(1)}, u32[]{:S(2)}, u32[]{:S(2)}) collective-permute-start(bf16[2,3,32,256]{3,2,1,0:T(8,128)(2,1)} %get-tuple-element.16), channel_id=1, source_target_pairs={{1,0},{2,1},{3,2},{4,3},{5,4},{6,5},{7,6},{8,7},{9,8},{10,9},{11,1... | collective-permute-start | bytes 294920 | tf_op jit(solution)/shard_map/ppermute | solution.py:437
  10.3 0.8 constant_dynamic-slice_fusion.3
  17.5 28.2 %steps.1 = (f32[1024,256]{1,0:T(8,128)}, bf16[2,1024,256]{2,1,0:T(8,128)(2,1)}, bf16[2,3,32,256]{3,2,1,0:T(8,128)(2,1)}, bf16[2,3,32,256]{3,2,1,0:T(8,128)(2,1)}...) custom-call(s32[8]{0:T(128)} %stack.42.info_ref, bf16[2,32,32,256]{3,2,1,0:T(8,128)(2,1)} %bitcast.85, ...), custom_call_target="tpu_custom_call" | custom-call | tf_op jit(solution)/shard_map/steps/pallas_call | solution.py:330
  45.7 0.9 collective-permute-start.4
  46.6 2.5 %collective-permute-done.4 = bf16[16,128,256]{2,1,0:T(8,128)(2,1)S(1)} collective-permute-done((bf16[16,128,256]{2,1,0:T(8,128)(2,1)}, bf16[16,128,256]{2,1,0:T(8,128)(2,1)S(1)}, u32[]{:S(2)}, u32[]{:S(2)}) %collective-permute-start.4) | collective-permute-done | bytes 1048608 | tf_op jit(solution)/shard_map/ppermute | solution.py:391
  49.1 1.8 %convert_add_fusion = f32[16,128,256]{2,1,0:T(8,128)S(1)} fusion(f32[16,128,256]{2,1,0:T(8,128)} %get-tuple-element.21, bf16[16,128,256]{2,1,0:T(8,128)(2,1)S(1)} %collective-permute-done.4), kind=kLoop, calls=%fused_computation | loop fusion | flops 1048576 | bytes 5242880 | tf_op jit(solution)/shard_map/add | solution.py:392
  51.0 2.8 %collective-permute-start.7 = (bf16[16,16,256]{2,1,0:T(8,128)(2,1)S(1)}, bf16[16,16,256]{2,1,0:T(8,128)(2,1)S(1)}, u32[]{:S(2)}, u32[]{:S(2)}) collective-permute-start(bf16[16,16,256]{2,1,0:T(8,128)(2,1)S(1)} %get-tuple-element.40), channel_id=1, source_target_pairs={{32,0},{64,32},{96,64},{0,96},{33,1},{65,33},{97,65},{1,97},{34,2}... | collective-permute-start | bytes 393224 | tf_op jit(solution)/shard_map/ppermute | solution.py:401
  54.2 2.2 %collective-permute-done.7 = bf16[16,16,256]{2,1,0:T(8,128)(2,1)S(1)} collective-permute-done((bf16[16,16,256]{2,1,0:T(8,128)(2,1)S(1)}, bf16[16,16,256]{2,1,0:T(8,128)(2,1)S(1)}, u32[]{:S(2)}, u32[]{:S(2)}) %collective-permute-start.7) | collective-permute-done | bytes 131104 | tf_op jit(solution)/shard_map/ppermute | solution.py:401
  56.4 3.5 %collective-permute-start.8 = (bf16[16,2,16,256]{3,2,0,1:T(8,128)(2,1)S(1)}, bf16[16,2,16,256]{3,2,0,1:T(8,128)(2,1)S(1)}, u32[]{:S(2)}, u32[]{:S(2)}) collective-permute-start(bf16[16,2,16,256]{3,2,0,1:T(8,128)(2,1)S(1)} %pad_maximum_fusion.1), channel_id=1, source_target_pairs={{32,0},{64,32},{96,64},{0,96},{33,1},{65,33},{97,65},{1,97},{34,2}... | collective-permute-start | bytes 786440 | tf_op jit(solution)/shard_map/ppermute | solution.py:406
  60.1 4.2 %collective-permute-done.8 = bf16[16,2,16,256]{3,2,0,1:T(8,128)(2,1)S(1)} collective-permute-done((bf16[16,2,16,256]{3,2,0,1:T(8,128)(2,1)S(1)}, bf16[16,2,16,256]{3,2,0,1:T(8,128)(2,1)S(1)}, u32[]{:S(2)}, u32[]{:S(2)}) %collective-permute-start.8) | collective-permute-done | bytes 262176 | tf_op jit(solution)/shard_map/ppermute | solution.py:406
  64.3 3.3 %collective-permute-done.6 = bf16[16,2,16,256]{3,2,0,1:T(8,128)(2,1)S(1)} collective-permute-done((bf16[16,2,16,256]{3,2,0,1:T(8,128)(2,1)S(1)}, bf16[16,2,16,256]{3,2,0,1:T(8,128)(2,1)S(1)}, u32[]{:S(2)}, u32[]{:S(2)}) %collective-permute-start.6) | collective-permute-done | bytes 262176 | tf_op jit(solution)/shard_map/ppermute | solution.py:405
  67.8 13.6 %all_to_all.10 = bf16[16,32,256]{2,1,0:T(8,128)(2,1)S(1)} all-to-all(bf16[16,32,256]{2,1,0:T(8,128)(2,1)S(1)} %bitcast.93), channel_id=1, replica_groups=mesh['x_hi'=2,'y'=4,'core'=2,'x_lo'=2,'z'=8] {'x_lo','z'}, dimensions={0} | all-to-all | bytes 524288 | tf_op jit(solution)/shard_map/all_to_all | solution.py:408
  81.4 0.9 broadcast_in_dim.10
  82.2 7.9 %all-to-all-start.1 = ((f32[16,32,256]{2,1,0:T(8,128)}), f32[16,32,256]{2,1,0:T(8,128)S(1)}, u32[]{:S(2)}, u32[]{:S(2)}) async-start(f32[16,32,256]{2,1,0:T(8,128)} %broadcast_in_dim.10), calls=%async_computation.1 | async-start | bytes 1048576 | tf_op jit(solution)/shard_map/all_to_all | solution.py:411
  90.1 1.5 %collective-permute-start.2 = (bf16[2,3,32,256]{3,2,1,0:T(8,128)(2,1)S(1)}, bf16[2,3,32,256]{3,2,1,0:T(8,128)(2,1)S(1)}, u32[]{:S(2)}, u32[]{:S(2)}) collective-permute-start(bf16[2,3,32,256]{3,2,1,0:T(8,128)(2,1)S(1)} %copy-done.2), channel_id=1, source_target_pairs={{0,1},{1,2},{2,3},{3,4},{4,5},{5,6},{6,7},{7,8},{8,9},{9,10},{10,1... | collective-permute-start | bytes 294920 | tf_op jit(solution)/shard_map/ppermute | solution.py:452
  91.7 2.1 %collective-permute-start.3 = (bf16[2,3,32,256]{3,2,1,0:T(8,128)(2,1)S(1)}, bf16[2,3,32,256]{3,2,1,0:T(8,128)(2,1)S(1)}, u32[]{:S(2)}, u32[]{:S(2)}) collective-permute-start(bf16[2,3,32,256]{3,2,1,0:T(8,128)(2,1)S(1)} %copy-done.3), channel_id=1, source_target_pairs={{1,0},{2,1},{3,2},{4,3},{5,4},{6,5},{7,6},{8,7},{9,8},{10,9},{11,1... | collective-permute-start | bytes 294920 | tf_op jit(solution)/shard_map/ppermute | solution.py:453
  93.8 2.9 %collective-permute-done.2.prev_ref = bf16[2,3,32,256]{3,2,1,0:T(8,128)(2,1)S(1)} collective-permute-done((bf16[2,3,32,256]{3,2,1,0:T(8,128)(2,1)S(1)}, bf16[2,3,32,256]{3,2,1,0:T(8,128)(2,1)S(1)}, u32[]{:S(2)}, u32[]{:S(2)}) %collective-permute-start.2) | collective-permute-done | bytes 98336 | tf_op jit(solution)/shard_map/ppermute | solution.py:452
  96.7 0.6 copy-done.4
  97.3 5.4 %fields.1 = bf16[2,32,32,256]{3,2,1,0:T(8,128)(2,1)} custom-call(s32[8]{0:T(128)} %stack.42.info_ref, bf16[2,1024,256]{2,1,0:T(8,128)(2,1)} %get-tuple-element.17.part_conv_ref, bf16[2,3,32,256]{3,2,1,0:T(8,128)(2,1)} %get-tuple-element.18.own_ref, bf16[2,3,32,256]{3,2,1,0:T(8,128)(2,1)} %copy-done.4, bf16[2,3,32,256]{3,2,1,0:T(8,128)(2,1)} %copy-done.5, ...), custom_call_target="tpu_custom_call" | custom-call | flops 2415919104 | bytes 4194304 | tf_op jit(solution)/shard_map/fields/pallas_call | solution.py:355
  102.7 0.8 all-to-all-done.1
  103.6 0.7 slice.98
  104.3 0.7 copy.39
  (39 shorter events, 5.0 us)
Async XLA Ops:
  3.0 13.8 %collective-permute-start = (bf16[2,3,32,256]{3,2,1,0:T(8,128)(2,1)}, bf16[2,3,32,256]{3,2,1,0:T(8,128)(2,1)S(1)}, u32[]{:S(2)}, u32[]{:S(2)}) collective-permute-start(bf16[2,3,32,256]{3,2,1,0:T(8,128)(2,1)} %get-tuple-element.15), channel_id=1, source_target_pairs={{0,1},{1,2},{2,3},{3,4},{4,5},{5,6},{6,7},{7,8},{8,9},{9,10},{10,1... | collective-permute-start | bytes 294920 | tf_op jit(solution)/shard_map/ppermute | solution.py:436
  5.5 11.3 %collective-permute-start.1 = (bf16[2,3,32,256]{3,2,1,0:T(8,128)(2,1)}, bf16[2,3,32,256]{3,2,1,0:T(8,128)(2,1)S(1)}, u32[]{:S(2)}, u32[]{:S(2)}) collective-permute-start(bf16[2,3,32,256]{3,2,1,0:T(8,128)(2,1)} %get-tuple-element.16), channel_id=1, source_target_pairs={{1,0},{2,1},{3,2},{4,3},{5,4},{6,5},{7,6},{8,7},{9,8},{10,9},{11,1... | collective-permute-start | bytes 294920 | tf_op jit(solution)/shard_map/ppermute | solution.py:437
  16.8 0.6 copy-start
  16.8 0.7 copy-start.1
  45.7 3.4 %collective-permute-start.4 = (bf16[16,128,256]{2,1,0:T(8,128)(2,1)}, bf16[16,128,256]{2,1,0:T(8,128)(2,1)S(1)}, u32[]{:S(2)}, u32[]{:S(2)}) collective-permute-start(bf16[16,128,256]{2,1,0:T(8,128)(2,1)} %get-tuple-element.22), channel_id=1, source_target_pairs={{0,16},{16,0},{1,17},{17,1},{2,18},{18,2},{3,19},{19,3},{4,20},{20... | collective-permute-start | bytes 3145736 | tf_op jit(solution)/shard_map/ppermute | solution.py:391
  51.0 5.3 %collective-permute-start.7 = (bf16[16,16,256]{2,1,0:T(8,128)(2,1)S(1)}, bf16[16,16,256]{2,1,0:T(8,128)(2,1)S(1)}, u32[]{:S(2)}, u32[]{:S(2)}) collective-permute-start(bf16[16,16,256]{2,1,0:T(8,128)(2,1)S(1)} %get-tuple-element.40), channel_id=1, source_target_pairs={{32,0},{64,32},{96,64},{0,96},{33,1},{65,33},{97,65},{1,97},{34,2}... | collective-permute-start | bytes 393224 | tf_op jit(solution)/shard_map/ppermute | solution.py:401
  54.1 5.8 %collective-permute-start.5 = (bf16[16,16,256]{2,1,0:T(8,128)(2,1)S(1)}, bf16[16,16,256]{2,1,0:T(8,128)(2,1)S(1)}, u32[]{:S(2)}, u32[]{:S(2)}) collective-permute-start(bf16[16,16,256]{2,1,0:T(8,128)(2,1)S(1)} %get-tuple-element.39), channel_id=1, source_target_pairs={{0,32},{32,64},{64,96},{96,0},{1,33},{33,65},{65,97},{97,1},{2,34}... | collective-permute-start | bytes 393224 | tf_op jit(solution)/shard_map/ppermute | solution.py:400
  56.4 7.9 %collective-permute-start.8 = (bf16[16,2,16,256]{3,2,0,1:T(8,128)(2,1)S(1)}, bf16[16,2,16,256]{3,2,0,1:T(8,128)(2,1)S(1)}, u32[]{:S(2)}, u32[]{:S(2)}) collective-permute-start(bf16[16,2,16,256]{3,2,0,1:T(8,128)(2,1)S(1)} %pad_maximum_fusion.1), channel_id=1, source_target_pairs={{32,0},{64,32},{96,64},{0,96},{33,1},{65,33},{97,65},{1,97},{34,2}... | collective-permute-start | bytes 786440 | tf_op jit(solution)/shard_map/ppermute | solution.py:406
  60.0 7.6 %collective-permute-start.6 = (bf16[16,2,16,256]{3,2,0,1:T(8,128)(2,1)S(1)}, bf16[16,2,16,256]{3,2,0,1:T(8,128)(2,1)S(1)}, u32[]{:S(2)}, u32[]{:S(2)}) collective-permute-start(bf16[16,2,16,256]{3,2,0,1:T(8,128)(2,1)S(1)} %pad_maximum_fusion), channel_id=1, source_target_pairs={{0,32},{32,64},{64,96},{96,0},{1,33},{33,65},{65,97},{97,1},{2,34}... | collective-permute-start | bytes 786440 | tf_op jit(solution)/shard_map/ppermute | solution.py:405
  67.6 22.5 %copy-start.2 = (bf16[2,3,32,256]{3,2,1,0:T(8,128)(2,1)S(1)}, bf16[2,3,32,256]{3,2,1,0:T(8,128)(2,1)}, u32[]{:S(2)}) copy-start(bf16[2,3,32,256]{3,2,1,0:T(8,128)(2,1)} %get-tuple-element.18.own_ref) | copy-start | bytes 294916
  67.6 24.0 %copy-start.3 = (bf16[2,3,32,256]{3,2,1,0:T(8,128)(2,1)S(1)}, bf16[2,3,32,256]{3,2,1,0:T(8,128)(2,1)}, u32[]{:S(2)}) copy-start(bf16[2,3,32,256]{3,2,1,0:T(8,128)(2,1)} %get-tuple-element.19) | copy-start | bytes 294916
  82.2 21.3 %all-to-all-start.1 = ((f32[16,32,256]{2,1,0:T(8,128)}), f32[16,32,256]{2,1,0:T(8,128)S(1)}, u32[]{:S(2)}, u32[]{:S(2)}) async-start(f32[16,32,256]{2,1,0:T(8,128)} %broadcast_in_dim.10), calls=%async_computation.1 | async-start | bytes 1048576 | tf_op jit(solution)/shard_map/all_to_all | solution.py:411
  90.1 6.5 %collective-permute-start.2 = (bf16[2,3,32,256]{3,2,1,0:T(8,128)(2,1)S(1)}, bf16[2,3,32,256]{3,2,1,0:T(8,128)(2,1)S(1)}, u32[]{:S(2)}, u32[]{:S(2)}) collective-permute-start(bf16[2,3,32,256]{3,2,1,0:T(8,128)(2,1)S(1)} %copy-done.2), channel_id=1, source_target_pairs={{0,1},{1,2},{2,3},{3,4},{4,5},{5,6},{6,7},{7,8},{8,9},{9,10},{10,1... | collective-permute-start | bytes 294920 | tf_op jit(solution)/shard_map/ppermute | solution.py:452
  91.7 5.0 %collective-permute-start.3 = (bf16[2,3,32,256]{3,2,1,0:T(8,128)(2,1)S(1)}, bf16[2,3,32,256]{3,2,1,0:T(8,128)(2,1)S(1)}, u32[]{:S(2)}, u32[]{:S(2)}) collective-permute-start(bf16[2,3,32,256]{3,2,1,0:T(8,128)(2,1)S(1)} %copy-done.3), channel_id=1, source_target_pairs={{1,0},{2,1},{3,2},{4,3},{5,4},{6,5},{7,6},{8,7},{9,8},{10,9},{11,1... | collective-permute-start | bytes 294920 | tf_op jit(solution)/shard_map/ppermute | solution.py:453
  96.7 0.6 copy-start.4
  96.7 0.7 copy-start.5

commit v2 on v1

v2 whole, which is shorter than its diff:
```python
import math

import jax
import jax.numpy as jnp
from jax import lax
from jax.experimental import pallas as pl
from jax.experimental.pallas import tpu as pltpu
from jax.sharding import Mesh
from jax.sharding import PartitionSpec as P

CUBIC = 0.044715
ROOT = math.sqrt(2.0 / math.pi)
BF = jnp.bfloat16
F32 = jnp.float32
SIDE = 32
CELLS = SIDE * SIDE
C = 256
STEPS = 2
CHUNK = 512
VMEM_LIMIT = 60 * 1024 * 1024


def mm(a, b):
    return lax.dot_general(a, b, (((1,), (0,)), ((), ())), preferred_element_type=F32)


def mm_nt(a, b):
    return lax.dot_general(a, b, (((1,), (1,)), ((), ())), preferred_element_type=F32)


def mm_tn(a, b):
    return lax.dot_general(a, b, (((0,), (0,)), ((), ())), preferred_element_type=F32)


def one_hot(cond):
    return jnp.where(cond, 1.0, 0.0).astype(BF)


def iota(shape, dim):
    return lax.broadcasted_iota(jnp.int32, shape, dim)


def edges_kernel(fields_ref, to_next_ref, to_prev_ref):
    for step in range(STEPS):
        to_next_ref[step, 0] = fields_ref[step, :, SIDE - 1, :]
        to_prev_ref[step, 0] = fields_ref[step, :, 0, :]
        for ref in (to_next_ref, to_prev_ref):
            ref[step, 1] = fields_ref[step, 0]
            ref[step, 2] = fields_ref[step, SIDE - 1]


def seam_of(info_ref, belt_ref, turns_ref, side):
    tile = info_ref[0]
    partner = belt_ref[side, tile]
    other = lax.rem(side + 2 - turns_ref[side, tile], 4)
    before = lax.rem(tile + 15, 16)
    place = jnp.where(partner == tile, 0, jnp.where(partner == before, 1, 2))
    base = (2 * place + jnp.where(other == 2, 1, 0)) * SIDE
    flip = other == side
    return jnp.where(flip, base + SIDE - 1, base), jnp.where(flip, -1, 1)


def seam_rows(info_ref, belt_ref, turns_ref, own_top, own_bottom, from_prev, from_next):
    stacked = jnp.concatenate(
        [own_top, own_bottom, from_prev[1], from_prev[2], from_next[1], from_next[2]], axis=0
    )
    rows = iota((2 * SIDE, 6 * SIDE), 0)
    cols = iota((2 * SIDE, 6 * SIDE), 1)
    top_base, top_sign = seam_of(info_ref, belt_ref, turns_ref, 0)
    bottom_base, bottom_sign = seam_of(info_ref, belt_ref, turns_ref, 2)
    wanted = jnp.where(
        rows < SIDE, top_base + top_sign * rows, bottom_base + bottom_sign * (rows - SIDE)
    )
    return mm(one_hot(cols == wanted), stacked)


def store_shifts(ref, step, low, high, middle, left, right):
    col = iota((SIDE, SIDE, C), 1)
    before = jnp.where(col == 0, left[:, None, :], pltpu.roll(middle, 1, axis=1))
    after = jnp.where(col == SIDE - 1, right[:, None, :], pltpu.roll(middle, SIDE - 1, axis=1))
    body = pl.ds(SIDE, CELLS)
    ref[step, body, 0:C] = before.reshape(CELLS, C).astype(BF)
    ref[step, body, C : 2 * C] = middle.reshape(CELLS, C).astype(BF)
    ref[step, body, 2 * C : 3 * C] = after.reshape(CELLS, C).astype(BF)
    col = iota((SIDE, C), 0)
    for at, line in ((0, low), (SIDE + CELLS, high)):
        row = pl.ds(at, SIDE)
        ref[step, row, 0:C] = jnp.where(col == 0, 0.0, pltpu.roll(line, 1, axis=0)).astype(BF)
        ref[step, row, C : 2 * C] = line.astype(BF)
        ref[step, row, 2 * C : 3 * C] = jnp.where(
            col == SIDE - 1, 0.0, pltpu.roll(line, SIDE - 1, axis=0)
        ).astype(BF)


def main_kernel(
    info_ref,
    belt_ref,
    turns_ref,
    *refs,
):
    sources, refs = refs[:11], refs[11:]
    grad_state_out, part_conv_out, to_next_ref, to_prev_ref, keep_out, send_out = refs[:6]
    held, refs = refs[6:17], refs[17:]
    (
        windows,
        joined,
        gated_all,
        parts_t,
        part_conv,
        part_conv_t,
        last_state,
        grad_state,
        shares,
        in_sems,
        out_sems,
    ) = refs
    loads = [
        pltpu.make_async_copy(source, target, in_sems.at[k])
        for k, (source, target) in enumerate(zip(sources, held))
    ]
    for load in loads:
        load.start()
    (
        fields_ref,
        prev_ref,
        next_ref,
        conv_ref,
        state_ref,
        update_ref,
        reset_ref,
        candidate_ref,
        adjoint_ref,
        grad_out_ref,
        head_ref,
    ) = held
    for load in loads[:3]:
        load.wait()
    for step in range(STEPS):
        seams = seam_rows(
            info_ref,
            belt_ref,
            turns_ref,
            fields_ref[step, 0],
            fields_ref[step, SIDE - 1],
            prev_ref[step],
            next_ref[step],
        )
        store_shifts(
            windows,
            step,
            seams[:SIDE],
            seams[SIDE:],
            fields_ref[step].astype(F32),
            prev_ref[step, 0].astype(F32),
            next_ref[step, 0].astype(F32),
        )
    for load in loads[3:]:
        load.wait()

    def chunk(start):
        rows = pl.ds(start, CHUNK)
        hidden = state_ref[rows, :]
        saved = []
        for step in range(STEPS):
            raw = jnp.zeros((CHUNK, C), F32)
            for p in range(3):
                window = windows[step, pl.ds(start + p * SIDE, CHUNK), :]
                raw = raw + mm(window, conv_ref[pl.ds(3 * C * p, 3 * C), :])
            bend = jnp.tanh(raw * (ROOT + (ROOT * CUBIC) * (raw * raw)))
            feature = (0.5 * raw * (1.0 + bend)).astype(BF)
            joined[step, rows, 0:C] = feature
            joined[step, rows, C : 2 * C] = hidden.astype(BF)
            both = joined[step, rows, :]
            update = 0.5 * jnp.tanh(0.5 * mm(both, update_ref[...])) + 0.5
            reset = 0.5 * jnp.tanh(0.5 * mm(both, reset_ref[...])) + 0.5
            gated = (reset * hidden).astype(BF)
            gated_all[step, rows, :] = gated
            candidate = jnp.tanh(
                mm(feature, candidate_ref[0:C, :]) + mm(gated, candidate_ref[C : 2 * C, :])
            )
            following = hidden + update * (candidate - hidden)
            saved.append((raw, bend, update, reset, candidate, hidden))
            hidden = following
        last_state[rows, :] = hidden.astype(BF)
        carried = adjoint_ref[rows, :]
        for step in reversed(range(STEPS)):
            raw, bend, update, reset, candidate, hidden = saved[step]
            total = carried + mm_tn(grad_out_ref[step, :, rows], head_ref[...])
            keep = 1.0 - update
            scaled = total * update
            part_cand = (scaled * (1.0 - candidate * candidate)).astype(BF)
            part_update = (scaled * (candidate - hidden) * keep).astype(BF)
            grad_gated = mm_nt(part_cand, candidate_ref[C : 2 * C, :])
            part_reset = (grad_gated * hidden * reset * (1.0 - reset)).astype(BF)
            parts_t[step, 0:C, rows] = part_cand.T
            parts_t[step, C : 2 * C, rows] = part_update.T
            parts_t[step, 2 * C : 3 * C, rows] = part_reset.T
            carried = (
                total * keep
                + grad_gated * reset
                + mm_nt(part_update, update_ref[C : 2 * C, :])
                + mm_nt(part_reset, reset_ref[C : 2 * C, :])
            )
            grad_feature = (
                mm_nt(part_cand, candidate_ref[0:C, :])
                + mm_nt(part_update, update_ref[0:C, :])
                + mm_nt(part_reset, reset_ref[0:C, :])
            )
            slope = 0.5 * (1.0 + bend) + (0.5 * ROOT) * raw * (1.0 - bend * bend) * (
                1.0 + (3.0 * CUBIC) * (raw * raw)
            )
            grad_raw = (grad_feature * slope).astype(BF)
            part_conv[step, rows, :] = grad_raw
            part_conv_t[step, :, rows] = grad_raw.T
        grad_state[rows, :] = carried

    for index in range(CELLS // CHUNK):
        chunk(index * CHUNK)
    stores = [
        pltpu.make_async_copy(grad_state, grad_state_out, out_sems.at[16]),
        pltpu.make_async_copy(part_conv, part_conv_out, out_sems.at[17]),
    ]
    for store in stores:
        store.start()

    picks = []
    row = iota((SIDE, CELLS), 0)
    cell = iota((SIDE, CELLS), 1)
    for col in (0, SIDE - 1):
        for p in range(3):
            at = row + 1 - p
            picks.append(one_hot((cell == at * SIDE + col) & (at >= 0) & (at < SIDE)))
    for line in (0, SIDE - 1):
        for q in range(3):
            at = row + 1 - q
            picks.append(one_hot((cell == line * SIDE + at) & (at >= 0) & (at < SIDE)))
    picks = jnp.concatenate(picks, axis=0)
    taps = [0, 3, 6, 2, 5, 8, 0, 1, 2, 6, 7, 8]
    for step in range(STEPS):
        picked = mm(picks, part_conv[step]).astype(BF)
        outside = []
        for side in range(4):
            total = jnp.zeros((SIDE, C), F32)
            for k in range(3 * side, 3 * side + 3):
                total = total + mm_nt(
                    picked[k * SIDE : (k + 1) * SIDE], conv_ref[taps[k] * C : (taps[k] + 1) * C, :]
                )
            outside.append(total.astype(BF))
        to_next_ref[step, 0] = outside[1]
        to_prev_ref[step, 0] = outside[0]
        for ref in (to_next_ref, to_prev_ref):
            ref[step, 1] = outside[2]
            ref[step, 2] = outside[3]

    core = info_ref[1]

    def share(block, value):
        shares[block] = value.reshape(16, 16, C)
        kept = pltpu.make_async_copy(shares.at[block], keep_out.at[block % 8], out_sems.at[block])
        sent = pltpu.make_async_copy(shares.at[block], send_out.at[block % 8], out_sems.at[block])
        pl.when(core == block // 8)(kept.start)
        pl.when(core != block // 8)(sent.start)
        stores.append(kept)

    def over_steps(one):
        return one(0) + one(1)

    for gate in range(2):
        lanes = slice(C * (gate + 1), C * (gate + 2))
        grad = over_steps(lambda s: mm(parts_t[s, lanes, :], joined[s])).astype(BF)
        share(9 + 2 * gate, grad[:, :C])
        share(10 + 2 * gate, grad[:, C:])
    share(13, over_steps(lambda s: mm(parts_t[s, 0:C, :], joined[s, :, 0:C])).astype(BF))
    share(14, over_steps(lambda s: mm(parts_t[s, 0:C, :], gated_all[s])).astype(BF))
    grad_head = mm(grad_out_ref[0], joined[1, :, C : 2 * C]) + mm(grad_out_ref[1], last_state[...])
    grad_head = jnp.concatenate([grad_head, jnp.zeros((C - 8, C), F32)], axis=0)
    share(15, grad_head.T.astype(BF))
    for p in range(3):
        grad = over_steps(
            lambda s: mm(part_conv_t[s], windows[s, pl.ds(p * SIDE, CELLS), :])
        ).astype(BF)
        for q in range(3):
            share(3 * p + q, grad[:, q * C : (q + 1) * C].T)
    for store in stores:
        store.wait()


def fields_kernel(
    info_ref,
    belt_ref,
    turns_ref,
    part_conv_ref,
    own_ref,
    prev_ref,
    next_ref,
    conv_ref,
    grad_fields_ref,
    shifted,
):
    zero = jnp.zeros((SIDE, C), F32)
    for step in range(STEPS):
        store_shifts(
            shifted,
            step,
            zero,
            zero,
            part_conv_ref[step].astype(F32).reshape(SIDE, SIDE, C),
            zero,
            zero,
        )
        seams = seam_rows(
            info_ref,
            belt_ref,
            turns_ref,
            own_ref[step, 1],
            own_ref[step, 2],
            prev_ref[step],
            next_ref[step],
        )
        left = prev_ref[step, 0].astype(F32)
        right = next_ref[step, 0].astype(F32)
        for part in range(4):
            at = part * 8
            grad = jnp.zeros((8 * SIDE, C), F32)
            for p in range(3):
                for q in range(3):
                    lanes = slice((2 - q) * C, (3 - q) * C)
                    window = shifted[step, pl.ds((at + 2 - p) * SIDE, 8 * SIDE), lanes]
                    tap = 3 * p + q
                    grad = grad + mm_nt(window, conv_ref[tap * C : (tap + 1) * C, :])
            grad = grad.reshape(8, SIDE, C)
            col = iota((8, SIDE, C), 1)
            row = iota((8, SIDE, C), 0)
            grad = grad + jnp.where(col == 0, left[at : at + 8][:, None, :], 0.0)
            grad = grad + jnp.where(col == SIDE - 1, right[at : at + 8][:, None, :], 0.0)
            if part == 0:
                grad = grad + jnp.where(row == 0, seams[:SIDE][None], 0.0)
            if part == 3:
                grad = grad + jnp.where(row == 7, seams[SIDE:][None], 0.0)
            grad_fields_ref[step, at : at + 8] = grad.astype(BF)


def in_vmem():
    return pl.BlockSpec(memory_space=pltpu.VMEM)


def in_smem():
    return pl.BlockSpec(memory_space=pltpu.SMEM)


def params():
    return pltpu.CompilerParams(vmem_limit_bytes=VMEM_LIMIT)


def shape(dims, kind=BF):
    return jax.ShapeDtypeStruct(dims, kind)


EDGE = (STEPS, 3, SIDE, C)


def edges_call(fields):
    return pl.pallas_call(
        edges_kernel,
        out_shape=(shape(EDGE), shape(EDGE)),
        in_specs=[in_vmem()],
        out_specs=(in_vmem(), in_vmem()),
        compiler_params=params(),
        name="edges",
    )(fields)


def main_call(*args):
    anywhere = pl.BlockSpec(memory_space=pl.ANY)
    return pl.pallas_call(
        main_kernel,
        out_shape=(
            shape((CELLS, C), F32),
            shape((STEPS, CELLS, C)),
            shape(EDGE),
            shape(EDGE),
            shape((8, 16, 16, C)),
            shape((8, 16, 16, C)),
        ),
        in_specs=[in_smem()] * 3 + [anywhere] * 11,
        out_specs=(anywhere, anywhere, in_vmem(), in_vmem(), anywhere, anywhere),
        scratch_shapes=[pltpu.VMEM(arg.shape, arg.dtype) for arg in args[3:]]
        + [
            pltpu.VMEM((STEPS, CELLS + 2 * SIDE, 3 * C), BF),
            pltpu.VMEM((STEPS, CELLS, 2 * C), BF),
            pltpu.VMEM((STEPS, CELLS, C), BF),
            pltpu.VMEM((STEPS, 3 * C, CELLS), BF),
            pltpu.VMEM((STEPS, CELLS, C), BF),
            pltpu.VMEM((STEPS, C, CELLS), BF),
            pltpu.VMEM((CELLS, C), BF),
            pltpu.VMEM((CELLS, C), F32),
            pltpu.VMEM((16, 16, 16, C), BF),
            pltpu.SemaphoreType.DMA((11,)),
            pltpu.SemaphoreType.DMA((18,)),
        ],
        compiler_params=params(),
        name="steps",
    )(*args)


def fields_call(*args):
    return pl.pallas_call(
        fields_kernel,
        out_shape=shape((STEPS, SIDE, SIDE, C)),
        in_specs=[in_smem()] * 3 + [in_vmem()] * 5,
        out_specs=in_vmem(),
        scratch_shapes=[pltpu.VMEM((STEPS, CELLS + 2 * SIDE, 3 * C), BF)],
        compiler_params=params(),
        cost_estimate=pl.CostEstimate(
            flops=2 * STEPS * CELLS * C * C * 9, bytes_accessed=4 << 20, transcendentals=0
        ),
        name="fields",
    )(*args)


RING = [(i, (i + 1) % 16) for i in range(16)]
BACK = [((i + 1) % 16, i) for i in range(16)]


def finish_kernel(whole_ref, conv_ref, update_ref, reset_ref, candidate_ref, head_ref):
    def block(k):
        return whole_ref[((k // 4) % 2) * 8 + (k % 4) * 2 + k // 8].astype(F32)

    for tap in range(9):
        conv_ref[tap] = block(tap)
    for ref, first in ((update_ref, 9), (reset_ref, 11), (candidate_ref, 13)):
        ref[:, 0:C] = block(first)
        ref[:, C : 2 * C] = block(first + 1)
    head_ref[...] = block(15).T[:8]


def finish_call(whole):
    gate = shape((16, 2 * C), F32)
    return pl.pallas_call(
        finish_kernel,
        out_shape=(shape((9, 16, C), F32), gate, gate, gate, shape((8, 16), F32)),
        in_specs=[in_vmem()],
        out_specs=tuple([in_vmem()] * 5),
        compiler_params=params(),
        name="finish",
    )(whole)


def added(pieces):
    total = pieces[0].astype(F32)
    for k in range(1, pieces.shape[0]):
        total = total + pieces[k].astype(F32)
    return total


def body(
    fields_in,
    state_start,
    state_adjoint,
    output_grad,
    conv_weight,
    w_update,
    w_reset,
    w_candidate,
    head_weight,
    neighbor_tile,
    seam_turns,
):
    dp = ("x_hi", "y", "core")
    belt = ("x_lo", "z")
    info = jnp.stack([lax.axis_index(belt), lax.axis_index("core")]).astype(jnp.int32)
    seams = (info, neighbor_tile.T, seam_turns.T)
    fields = fields_in[0, 0]
    conv = conv_weight.reshape(9 * C, C)
    to_next, to_prev = edges_call(fields)
    prev = lax.ppermute(to_next, belt, RING)
    following = lax.ppermute(to_prev, belt, BACK)
    grad_state, part_conv, out_next, out_prev, keep, send = main_call(
        *seams,
        fields,
        prev,
        following,
        conv,
        state_start.reshape(CELLS, C),
        w_update,
        w_reset,
        w_candidate,
        state_adjoint.reshape(CELLS, C),
        output_grad[0, 0],
        head_weight,
    )
    got = lax.ppermute(send, "core", [(0, 1), (1, 0)])
    held = (keep.astype(F32) + got.astype(F32)).astype(BF)
    held = lax.all_to_all(held, ("x_hi", "y"), 0, 0, tiled=True)
    held = added(held).astype(BF)
    prev = lax.ppermute(out_next, belt, RING)
    following = lax.ppermute(out_prev, belt, BACK)
    held, prev, following = lax.optimization_barrier((held, prev, following))
    grad_fields = fields_call(*seams, part_conv, out_next, prev, following, conv)
    held = lax.all_to_all(held, belt, 0, 0, tiled=True)
    held = added(held).astype(BF)
    held, grad_fields = lax.optimization_barrier((held, grad_fields))
    whole = jnp.broadcast_to(held[None], (16, 16, C))
    whole = lax.all_to_all(whole, dp, 0, 0, tiled=True)
    grad_conv, grad_update, grad_reset, grad_candidate, grad_head = finish_call(whole)
    return (
        grad_fields[None, None],
        grad_state.reshape(1, 1, SIDE, SIDE, C),
        grad_conv,
        grad_update.T,
        grad_reset.T,
        grad_candidate.T,
        grad_head,
    )


def solution(mesh):
    cube = Mesh(mesh.devices.reshape(2, 4, 2, 2, 8), ("x_hi", "y", "core", "x_lo", "z"))
    dp = ("x_hi", "y", "core")
    tile = ("x_lo", "z")
    return jax.shard_map(
        body,
        mesh=cube,
        in_specs=(
            P(dp, tile, None, None, None, None),
            P(dp, tile, None, None, None),
            P(dp, tile, None, None, None),
            P(dp, tile, None, None, None),
            P(),
            P(),
            P(),
            P(),
            P(),
            P(),
            P(),
        ),
        out_specs=(
            P(dp, tile, None, None, None, None),
            P(dp, tile, None, None, None),
            P(None, tile, None),
            P(None, tile),
            P(None, tile),
            P(None, tile),
            P(None, tile),
        ),
        check_vma=False,
    )
```

time: 107 us -> 95 us (0.89)
  local copies, waits for them, and re-layouts: 6.26 us -> 0.69 us
  Pallas kernels: 36 us -> 30.9 us
  between operations: 4.81 us -> 0.72 us
  waiting for transfers between devices: 15.9 us -> 19.7 us
  starting transfers between devices: 26.3 us -> 23.3 us
  blocking collectives: 13.6 us -> 15.2 us
    all_to_all x1 -> x2, waiting for transfers between devices: 0.78 us -> 15.1 us  [the longest x1 13 us: body(): held = lax.all_to_all(held, ('x_hi', 'y'), 0, 0, tiled=True)]
    ppermute x9 -> x5, waiting for transfers between devices: 15.1 us -> 4.65 us  [the longest x1 2.5 us: body(): got = lax.ppermute(send, 'core', [(0, 1), (1, 0)])]
    pallas_call x1, Pallas kernels: 28.2 us -> 22 us  [main_call(): pl.pallas_call(main_kernel, out_shape=(shape((CELLS, C), F32), shape((STE...]
    ppermute x9 -> x5, starting transfers between devices: 18.4 us -> 12.3 us  [the longest x1 4.87 us: body(): following = lax.ppermute(to_prev, belt, BACK)]
    convert_element_type x1 -> x3, other arithmetic: 0.13 us -> 3.33 us  [the longest x1 2.51 us: body(): held = (keep.astype(F32) + got.astype(F32)).astype(BF)]
    all_to_all x1 -> x2, starting transfers between devices: 7.87 us -> 11 us  [the longest x1 6.49 us: body(): held = lax.all_to_all(held, ('x_hi', 'y'), 0, 0, tiled=True)]
    slice x6 -> x0, local copies, waits for them, and re-layouts: 2.39 us -> none  [the longest x1 0.67 us: body(): total[:9]]
    add x2 -> x0, other arithmetic: 1.88 us -> none  [the longest x1 1.84 us: reduce_weights(): held = (keep + got.astype(F32)).reshape(16, 4, 2, 16, C)]
  transfers between devices with their start and end apart: 10 -> 7, of which waited for: 6 -> 4; matrix products, arithmetic and copies ran while one was open for 3% -> 1% of each run, Pallas kernels for 5% -> 6%
where the time goes in v2:
time: 95 us; the launch traced here: 94.5 us
  Pallas kernels  30.9 us (33%)
  starting transfers between devices  23.3 us (25%)
  waiting for transfers between devices  19.7 us (21%)
  blocking collectives  15.2 us (16%)
  other arithmetic  3.91 us (4%)
    pallas_call x1, Pallas kernels, main_call(): pl.pallas_call(main_kernel, out_shape=(shape((CELLS, C), F32), shape((STE...  22 us
    all_to_all x1, blocking collectives, body(): whole = lax.all_to_all(whole, dp, 0, 0, tiled=True)  15.2 us
    all_to_all x1, waiting for transfers between devices, body(): held = lax.all_to_all(held, ('x_hi', 'y'), 0, 0, tiled=True)  13 us
    all_to_all x1, starting transfers between devices, body(): held = lax.all_to_all(held, ('x_hi', 'y'), 0, 0, tiled=True)  6.49 us
    pallas_call x1, Pallas kernels, fields_call(): pl.pallas_call(fields_kernel, out_shape=shape((STEPS, SIDE, SIDE, C)), in...  5.41 us
    ppermute x1, starting transfers between devices, body(): following = lax.ppermute(to_prev, belt, BACK)  4.87 us
    all_to_all x1, starting transfers between devices, body(): held = lax.all_to_all(held, belt, 0, 0, tiled=True)  4.56 us
    ppermute x1, starting transfers between devices, body(): following = lax.ppermute(out_prev, belt, BACK)  3.55 us
  transfers between devices with their start and end apart: 7, of which 4 were waited for; matrix products, arithmetic and copies ran while one was open for 1% of the time, Pallas kernels for 6%

profile of v2, /device:TPU:1, one launch (start us, length us, event | category | flops | bytes accessed | tf_op | source)
XLA Modules:
  0.0 94.5 jit_solution(13695760504415574620)
XLA Ops:
  0.6 2.0 %edges.1 = (bf16[2,3,32,256]{3,2,1,0:T(8,128)(2,1)}, bf16[2,3,32,256]{3,2,1,0:T(8,128)(2,1)}) custom-call(bf16[2,32,32,256]{3,2,1,0:T(8,128)(2,1)} %bitcast.23), custom_call_target="tpu_custom_call" | custom-call | tf_op jit(solution)/shard_map/edges/pallas_call | solution.py:363
  2.6 2.5 %collective-permute-start = (bf16[2,3,32,256]{3,2,1,0:T(8,128)(2,1)}, bf16[2,3,32,256]{3,2,1,0:T(8,128)(2,1)S(1)}, u32[]{:S(2)}, u32[]{:S(2)}) collective-permute-start(bf16[2,3,32,256]{3,2,1,0:T(8,128)(2,1)} %get-tuple-element.25), channel_id=1, source_target_pairs={{0,1},{1,2},{2,3},{3,4},{4,5},{5,6},{6,7},{7,8},{8,9},{9,10},{10,1... | collective-permute-start | bytes 294920 | tf_op jit(solution)/shard_map/ppermute | solution.py:476
  5.1 4.9 %collective-permute-start.1 = (bf16[2,3,32,256]{3,2,1,0:T(8,128)(2,1)}, bf16[2,3,32,256]{3,2,1,0:T(8,128)(2,1)S(1)}, u32[]{:S(2)}, u32[]{:S(2)}) collective-permute-start(bf16[2,3,32,256]{3,2,1,0:T(8,128)(2,1)} %get-tuple-element.26), channel_id=1, source_target_pairs={{1,0},{2,1},{3,2},{4,3},{5,4},{6,5},{7,6},{8,7},{9,8},{10,9},{11,1... | collective-permute-start | bytes 294920 | tf_op jit(solution)/shard_map/ppermute | solution.py:477
  9.9 0.6 pad_add_fusion.info_ref
  10.5 2.1 %collective-permute-done.refs_1_ = bf16[2,3,32,256]{3,2,1,0:T(8,128)(2,1)S(1)} collective-permute-done((bf16[2,3,32,256]{3,2,1,0:T(8,128)(2,1)}, bf16[2,3,32,256]{3,2,1,0:T(8,128)(2,1)S(1)}, u32[]{:S(2)}, u32[]{:S(2)}) %collective-permute-start) | collective-permute-done | bytes 98336 | tf_op jit(solution)/shard_map/ppermute | solution.py:476
  12.7 0.0 collective-permute-done.1.refs_2_
  12.7 0.6 copy-done
  13.3 0.0 copy-done.1
  13.3 22.0 %steps.1 = (f32[1024,256]{1,0:T(8,128)}, bf16[2,1024,256]{2,1,0:T(8,128)(2,1)}, bf16[2,3,32,256]{3,2,1,0:T(8,128)(2,1)}, bf16[2,3,32,256]{3,2,1,0:T(8,128)(2,1)}...) custom-call(s32[2]{0:T(128)} %pad_add_fusion.info_ref, s32[4,16]{1,0:T(4,128)} %bitcast.30, ...), custom_call_target="tpu_custom_call" | custom-call | tf_op jit(solution)/shard_map/steps/pallas_call | solution.py:375
  35.3 1.3 %collective-permute-start.2 = (bf16[8,16,16,256]{3,2,1,0:T(8,128)(2,1)}, bf16[8,16,16,256]{3,2,1,0:T(8,128)(2,1)S(1)}, u32[]{:S(2)}, u32[]{:S(2)}) collective-permute-start(bf16[8,16,16,256]{3,2,1,0:T(8,128)(2,1)} %get-tuple-element.28), channel_id=1, source_target_pairs={{0,16},{16,0},{1,17},{17,1},{2,18},{18,2},{3,19},{19,3},{4,20},{20... | collective-permute-start | bytes 3145736 | tf_op jit(solution)/shard_map/ppermute | solution.py:492
  36.6 2.5 %collective-permute-done.2 = bf16[8,16,16,256]{3,2,1,0:T(8,128)(2,1)S(1)} collective-permute-done((bf16[8,16,16,256]{3,2,1,0:T(8,128)(2,1)}, bf16[8,16,16,256]{3,2,1,0:T(8,128)(2,1)S(1)}, u32[]{:S(2)}, u32[]{:S(2)}) %collective-permute-start.2) | collective-permute-done | bytes 1048608 | tf_op jit(solution)/shard_map/ppermute | solution.py:492
  39.1 2.5 %add_convert_fusion = bf16[8,16,16,256]{3,2,1,0:T(8,128)(2,1)} fusion(bf16[8,16,16,256]{3,2,1,0:T(8,128)(2,1)S(1)} %collective-permute-done.2, bf16[8,16,16,256]{3,2,1,0:T(8,128)(2,1)} %get-tuple-element.27), kind=kLoop, calls=%fused_computation | loop fusion | flops 2097152 | bytes 3145728 | tf_op jit(solution)/shard_map/convert_element_type | solution.py:493
  41.6 6.5 %all-to-all-start = ((bf16[8,16,16,256]{3,2,1,0:T(8,128)(2,1)}), bf16[8,16,16,256]{3,2,1,0:T(8,128)(2,1)S(1)}, u32[]{:S(2)}, u32[]{:S(2)}) async-start(bf16[8,16,16,256]{3,2,1,0:T(8,128)(2,1)} %add_convert_fusion), calls=%async_computation | async-start | bytes 2097152 | tf_op jit(solution)/shard_map/all_to_all | solution.py:494
  48.1 0.1 collective-permute-start.3
  48.2 3.6 %collective-permute-start.4 = (bf16[2,3,32,256]{3,2,1,0:T(8,128)(2,1)S(1)}, bf16[2,3,32,256]{3,2,1,0:T(8,128)(2,1)S(1)}, u32[]{:S(2)}, u32[]{:S(2)}) collective-permute-start(bf16[2,3,32,256]{3,2,1,0:T(8,128)(2,1)S(1)} %copy-done.3), channel_id=1, source_target_pairs={{1,0},{2,1},{3,2},{4,3},{5,4},{6,5},{7,6},{8,7},{9,8},{10,9},{11,1... | collective-permute-start | bytes 294920 | tf_op jit(solution)/shard_map/ppermute | solution.py:497
  51.8 13.0 %all-to-all-done = bf16[8,16,16,256]{3,2,1,0:T(8,128)(2,1)S(1)} async-done(((bf16[8,16,16,256]{3,2,1,0:T(8,128)(2,1)}), bf16[8,16,16,256]{3,2,1,0:T(8,128)(2,1)S(1)}, u32[]{:S(2)}, u32[]{:S(2)}) %all-to-all-start) | async-done | bytes 1048608 | tf_op jit(solution)/shard_map/all_to_all | solution.py:494
  64.7 0.8 fusion
  65.5 0.0 collective-permute-done.3.prev_ref
  65.5 0.0 collective-permute-done.4.next_ref
  65.6 4.6 %all-to-all-start.1 = ((bf16[16,16,256]{2,1,0:T(8,128)(2,1)}), bf16[16,16,256]{2,1,0:T(8,128)(2,1)S(1)}, u32[]{:S(2)}, u32[]{:S(2)}) async-start(bf16[16,16,256]{2,1,0:T(8,128)(2,1)} %fusion), calls=%async_computation.1 | async-start | bytes 262144 | tf_op jit(solution)/shard_map/all_to_all | solution.py:500
  70.2 5.4 %fields.1 = bf16[2,32,32,256]{3,2,1,0:T(8,128)(2,1)} custom-call(s32[2]{0:T(128)} %pad_add_fusion.info_ref, s32[4,16]{1,0:T(4,128)} %bitcast.31, s32[4,16]{1,0:T(4,128)} %bitcast.33, bf16[2,1024,256]{2,1,0:T(8,128)(2,1)} %get-tuple-element.32.part_conv_ref, bf16[2,3,32,256]{3,2,1,0:T(8,128)(2,1)} %get-tuple-element.29.own_ref, ...), custom_call_target="tpu_custom_call" | custom-call | flops 2415919104 | bytes 4194304 | tf_op jit(solution)/shard_map/fields/pallas_call | solution.py:407
  75.6 2.1 %all-to-all-done.1 = bf16[16,16,256]{2,1,0:T(8,128)(2,1)S(1)} async-done(((bf16[16,16,256]{2,1,0:T(8,128)(2,1)}), bf16[16,16,256]{2,1,0:T(8,128)(2,1)S(1)}, u32[]{:S(2)}, u32[]{:S(2)}) %all-to-all-start.1) | async-done | bytes 131104 | tf_op jit(solution)/shard_map/all_to_all | solution.py:500
  77.7 15.2 %all_to_all.15.whole_ref = bf16[16,16,256]{2,1,0:T(8,128)(2,1)} all-to-all(bf16[16,16,256]{2,1,0:T(8,128)(2,1)S(1)} %broadcast_in_dim.10), channel_id=1, replica_groups=mesh['x_hi'=2,'y'=4,'core'=2,'x_lo'=2,'z'=8] {'x_hi','y','core'}, dimensions={0} | all-to-all | bytes 262144 | tf_op jit(solution)/shard_map/all_to_all | solution.py:504
  92.9 1.6 %finish.1 = (f32[9,16,256]{2,1,0:T(8,128)}, f32[16,512]{1,0:T(8,128)}, f32[16,512]{1,0:T(8,128)}, f32[16,512]{1,0:T(8,128)}, f32[8,16]{1,0:T(8,128)}) custom-call(bf16[16,16,256]{2,1,0:T(8,128)(2,1)} %all_to_all.15.whole_ref), custom_call_target="tpu_custom_call" | custom-call | tf_op jit(solution)/shard_map/finish/pallas_call | solution.py:439
  (12 shorter events, 0.1 us)
Async XLA Ops:
  2.6 10.1 %collective-permute-start = (bf16[2,3,32,256]{3,2,1,0:T(8,128)(2,1)}, bf16[2,3,32,256]{3,2,1,0:T(8,128)(2,1)S(1)}, u32[]{:S(2)}, u32[]{:S(2)}) collective-permute-start(bf16[2,3,32,256]{3,2,1,0:T(8,128)(2,1)} %get-tuple-element.25), channel_id=1, source_target_pairs={{0,1},{1,2},{2,3},{3,4},{4,5},{5,6},{6,7},{7,8},{8,9},{9,10},{10,1... | collective-permute-start | bytes 294920 | tf_op jit(solution)/shard_map/ppermute | solution.py:476
  5.1 7.6 %collective-permute-start.1 = (bf16[2,3,32,256]{3,2,1,0:T(8,128)(2,1)}, bf16[2,3,32,256]{3,2,1,0:T(8,128)(2,1)S(1)}, u32[]{:S(2)}, u32[]{:S(2)}) collective-permute-start(bf16[2,3,32,256]{3,2,1,0:T(8,128)(2,1)} %get-tuple-element.26), channel_id=1, source_target_pairs={{1,0},{2,1},{3,2},{4,3},{5,4},{6,5},{7,6},{8,7},{9,8},{10,9},{11,1... | collective-permute-start | bytes 294920 | tf_op jit(solution)/shard_map/ppermute | solution.py:477
  12.7 0.6 copy-start
  12.7 0.7 copy-start.1
  35.3 3.8 %collective-permute-start.2 = (bf16[8,16,16,256]{3,2,1,0:T(8,128)(2,1)}, bf16[8,16,16,256]{3,2,1,0:T(8,128)(2,1)S(1)}, u32[]{:S(2)}, u32[]{:S(2)}) collective-permute-start(bf16[8,16,16,256]{3,2,1,0:T(8,128)(2,1)} %get-tuple-element.28), channel_id=1, source_target_pairs={{0,16},{16,0},{1,17},{17,1},{2,18},{18,2},{3,19},{19,3},{4,20},{20... | collective-permute-start | bytes 3145736 | tf_op jit(solution)/shard_map/ppermute | solution.py:492
  41.6 6.5 %copy-start.2 = (bf16[2,3,32,256]{3,2,1,0:T(8,128)(2,1)S(1)}, bf16[2,3,32,256]{3,2,1,0:T(8,128)(2,1)}, u32[]{:S(2)}) copy-start(bf16[2,3,32,256]{3,2,1,0:T(8,128)(2,1)} %get-tuple-element.29.own_ref) | copy-start | bytes 294916
  41.6 6.6 %copy-start.3 = (bf16[2,3,32,256]{3,2,1,0:T(8,128)(2,1)S(1)}, bf16[2,3,32,256]{3,2,1,0:T(8,128)(2,1)}, u32[]{:S(2)}) copy-start(bf16[2,3,32,256]{3,2,1,0:T(8,128)(2,1)} %get-tuple-element.30) | copy-start | bytes 294916
  41.6 23.1 %all-to-all-start = ((bf16[8,16,16,256]{3,2,1,0:T(8,128)(2,1)}), bf16[8,16,16,256]{3,2,1,0:T(8,128)(2,1)S(1)}, u32[]{:S(2)}, u32[]{:S(2)}) async-start(bf16[8,16,16,256]{3,2,1,0:T(8,128)(2,1)} %add_convert_fusion), calls=%async_computation | async-start | bytes 2097152 | tf_op jit(solution)/shard_map/all_to_all | solution.py:494
  48.1 17.4 %collective-permute-start.3 = (bf16[2,3,32,256]{3,2,1,0:T(8,128)(2,1)S(1)}, bf16[2,3,32,256]{3,2,1,0:T(8,128)(2,1)S(1)}, u32[]{:S(2)}, u32[]{:S(2)}) collective-permute-start(bf16[2,3,32,256]{3,2,1,0:T(8,128)(2,1)S(1)} %copy-done.2), channel_id=1, source_target_pairs={{0,1},{1,2},{2,3},{3,4},{4,5},{5,6},{6,7},{7,8},{8,9},{9,10},{10,1... | collective-permute-start | bytes 294920 | tf_op jit(solution)/shard_map/ppermute | solution.py:496
  48.2 17.3 %collective-permute-start.4 = (bf16[2,3,32,256]{3,2,1,0:T(8,128)(2,1)S(1)}, bf16[2,3,32,256]{3,2,1,0:T(8,128)(2,1)S(1)}, u32[]{:S(2)}, u32[]{:S(2)}) collective-permute-start(bf16[2,3,32,256]{3,2,1,0:T(8,128)(2,1)S(1)} %copy-done.3), channel_id=1, source_target_pairs={{1,0},{2,1},{3,2},{4,3},{5,4},{6,5},{7,6},{8,7},{9,8},{10,9},{11,1... | collective-permute-start | bytes 294920 | tf_op jit(solution)/shard_map/ppermute | solution.py:497
  65.5 4.6 %copy-start.4 = (bf16[2,3,32,256]{3,2,1,0:T(8,128)(2,1)}, bf16[2,3,32,256]{3,2,1,0:T(8,128)(2,1)S(1)}, u32[]{:S(2)}) copy-start(bf16[2,3,32,256]{3,2,1,0:T(8,128)(2,1)S(1)} %collective-permute-done.3.prev_ref) | copy-start | bytes 294916
  65.6 4.6 %copy-start.5 = (bf16[2,3,32,256]{3,2,1,0:T(8,128)(2,1)}, bf16[2,3,32,256]{3,2,1,0:T(8,128)(2,1)S(1)}, u32[]{:S(2)}) copy-start(bf16[2,3,32,256]{3,2,1,0:T(8,128)(2,1)S(1)} %collective-permute-done.4.next_ref) | copy-start | bytes 294916
  65.6 12.1 %all-to-all-start.1 = ((bf16[16,16,256]{2,1,0:T(8,128)(2,1)}), bf16[16,16,256]{2,1,0:T(8,128)(2,1)S(1)}, u32[]{:S(2)}, u32[]{:S(2)}) async-start(bf16[16,16,256]{2,1,0:T(8,128)(2,1)} %fusion), calls=%async_computation.1 | async-start | bytes 262144 | tf_op jit(solution)/shard_map/all_to_all | solution.py:500

commit v3 on v2

--- a/solution.py
+++ b/solution.py
@@ -17,7 +17,6 @@
 C = 256
 STEPS = 2
 CHUNK = 512
-VMEM_LIMIT = 60 * 1024 * 1024
 
 
 def mm(a, b):
@@ -74,6 +73,13 @@
     return mm(one_hot(cols == wanted), stacked)
 
 
+def line_shifts(line):
+    at = iota((SIDE, C), 0)
+    before = jnp.where(at == 0, 0.0, pltpu.roll(line, 1, axis=0))
+    after = jnp.where(at == SIDE - 1, 0.0, pltpu.roll(line, SIDE - 1, axis=0))
+    return jnp.concatenate([before, line, after], axis=1).astype(BF)
+
+
 def store_shifts(ref, step, low, high, middle, left, right):
     col = iota((SIDE, SIDE, C), 1)
     before = jnp.where(col == 0, left[:, None, :], pltpu.roll(middle, 1, axis=1))
@@ -82,14 +88,34 @@
     ref[step, body, 0:C] = before.reshape(CELLS, C).astype(BF)
     ref[step, body, C : 2 * C] = middle.reshape(CELLS, C).astype(BF)
     ref[step, body, 2 * C : 3 * C] = after.reshape(CELLS, C).astype(BF)
-    col = iota((SIDE, C), 0)
-    for at, line in ((0, low), (SIDE + CELLS, high)):
-        row = pl.ds(at, SIDE)
-        ref[step, row, 0:C] = jnp.where(col == 0, 0.0, pltpu.roll(line, 1, axis=0)).astype(BF)
-        ref[step, row, C : 2 * C] = line.astype(BF)
-        ref[step, row, 2 * C : 3 * C] = jnp.where(
-            col == SIDE - 1, 0.0, pltpu.roll(line, SIDE - 1, axis=0)
-        ).astype(BF)
+    ref[step, pl.ds(0, SIDE), :] = line_shifts(low)
+    ref[step, pl.ds(SIDE + CELLS, SIDE), :] = line_shifts(high)
+
+
+def early_kernel(fields_in, conv_in, raw_out, fields_ref, conv_ref, windows, raw_ref, sems):
+    loads = [
+        pltpu.make_async_copy(fields_in, fields_ref, sems.at[0]),
+        pltpu.make_async_copy(conv_in, conv_ref, sems.at[1]),
+    ]
+    for load in loads:
+        load.start()
+    loads[0].wait()
+    zero = jnp.zeros((SIDE, C), F32)
+    stores = []
+    for step in range(STEPS):
+        store_shifts(windows, step, zero, zero, fields_ref[step].astype(F32), zero, zero)
+        if step == 0:
+            loads[1].wait()
+        for start in range(0, CELLS, CHUNK):
+            raw = jnp.zeros((CHUNK, C), F32)
+            for p in range(3):
+                window = windows[step, pl.ds(start + p * SIDE, CHUNK), :]
+                raw = raw + mm(window, conv_ref[pl.ds(3 * C * p, 3 * C), :])
+            raw_ref[step, pl.ds(start, CHUNK), :] = raw
+        stores.append(pltpu.make_async_copy(raw_ref.at[step], raw_out.at[step], sems.at[2 + step]))
+        stores[step].start()
+    for store in stores:
+        store.wait()
 
 
 def main_kernel(
@@ -98,9 +124,9 @@
     turns_ref,
     *refs,
 ):
-    sources, refs = refs[:11], refs[11:]
+    sources, refs = refs[:12], refs[12:]
     grad_state_out, part_conv_out, to_next_ref, to_prev_ref, keep_out, send_out = refs[:6]
-    held, refs = refs[6:17], refs[17:]
+    held, refs = refs[6:18], refs[18:]
     (
         windows,
         joined,
@@ -125,6 +151,7 @@
         prev_ref,
         next_ref,
         conv_ref,
+        raw_ref,
         state_ref,
         update_ref,
         reset_ref,
@@ -135,6 +162,7 @@
     ) = held
     for load in loads[:3]:
         load.wait()
+    tops, bottoms, lefts, rights = [], [], [], []
     for step in range(STEPS):
         seams = seam_rows(
             info_ref,
@@ -145,16 +173,43 @@
             prev_ref[step],
             next_ref[step],
         )
+        left = prev_ref[step, 0].astype(F32)
+        right = next_ref[step, 0].astype(F32)
         store_shifts(
             windows,
             step,
             seams[:SIDE],
             seams[SIDE:],
             fields_ref[step].astype(F32),
-            prev_ref[step, 0].astype(F32),
-            next_ref[step, 0].astype(F32),
+            left,
+            right,
         )
-    for load in loads[3:]:
+        tops.append(line_shifts(seams[:SIDE]))
+        bottoms.append(line_shifts(seams[SIDE:]))
+        lefts.append(line_shifts(left))
+        rights.append(line_shifts(right))
+    for load in loads[3:5]:
+        load.wait()
+
+    def taps_of(lines, taps):
+        lines = jnp.concatenate(lines, axis=0)
+        total = jnp.zeros((STEPS * SIDE, C), F32)
+        for k, tap in enumerate(taps):
+            total = total + mm(lines[:, k * C : (k + 1) * C], conv_ref[pl.ds(tap * C, C), :])
+        return total
+
+    top = taps_of(tops, (0, 1, 2))
+    bottom = taps_of(bottoms, (6, 7, 8))
+    left = taps_of(lefts, (0, 3, 6))
+    right = taps_of(rights, (2, 5, 8))
+    place = iota((SIDE, 8, C), 1)
+    for step in range(STEPS):
+        lines = slice(step * SIDE, (step + 1) * SIDE)
+        raw_ref[step, 0, :, :] += top[lines]
+        raw_ref[step, SIDE - 1, :, :] += bottom[lines]
+        raw_ref[step, :, 0:8, :] += jnp.where(place == 0, left[lines][:, None, :], 0.0)
+        raw_ref[step, :, SIDE - 8 : SIDE, :] += jnp.where(place == 7, right[lines][:, None, :], 0.0)
+    for load in loads[5:]:
         load.wait()
 
     def chunk(start):
@@ -162,10 +217,7 @@
         hidden = state_ref[rows, :]
         saved = []
         for step in range(STEPS):
-            raw = jnp.zeros((CHUNK, C), F32)
-            for p in range(3):
-                window = windows[step, pl.ds(start + p * SIDE, CHUNK), :]
-                raw = raw + mm(window, conv_ref[pl.ds(3 * C * p, 3 * C), :])
+            raw = raw_ref[step, pl.ds(start // SIDE, CHUNK // SIDE), :, :].reshape(CHUNK, C)
             bend = jnp.tanh(raw * (ROOT + (ROOT * CUBIC) * (raw * raw)))
             feature = (0.5 * raw * (1.0 + bend)).astype(BF)
             joined[step, rows, 0:C] = feature
@@ -348,8 +400,8 @@
     return pl.BlockSpec(memory_space=pltpu.SMEM)
 
 
-def params():
-    return pltpu.CompilerParams(vmem_limit_bytes=VMEM_LIMIT)
+def params(mebibytes=60):
+    return pltpu.CompilerParams(vmem_limit_bytes=mebibytes << 20)
 
 
 def shape(dims, kind=BF):
@@ -365,9 +417,32 @@
         out_shape=(shape(EDGE), shape(EDGE)),
         in_specs=[in_vmem()],
         out_specs=(in_vmem(), in_vmem()),
-        compiler_params=params(),
+        compiler_params=params(8),
         name="edges",
     )(fields)
+
+
+def early_call(fields, conv):
+    anywhere = pl.BlockSpec(memory_space=pl.ANY)
+    raw = (STEPS, CELLS, C)
+    return pl.pallas_call(
+        early_kernel,
+        out_shape=shape(raw, F32),
+        in_specs=[anywhere] * 2,
+        out_specs=anywhere,
+        scratch_shapes=[
+            pltpu.VMEM(fields.shape, BF),
+            pltpu.VMEM(conv.shape, BF),
+            pltpu.VMEM((STEPS, CELLS + 2 * SIDE, 3 * C), BF),
+            pltpu.VMEM(raw, F32),
+            pltpu.SemaphoreType.DMA((4,)),
+        ],
+        compiler_params=params(),
+        cost_estimate=pl.CostEstimate(
+            flops=2 * STEPS * CELLS * C * C * 9, bytes_accessed=5 << 20, transcendentals=0
+        ),
+        name="early",
+    )(fields, conv)
 
 
 def main_call(*args):
@@ -382,7 +457,7 @@
             shape((8, 16, 16, C)),
             shape((8, 16, 16, C)),
         ),
-        in_specs=[in_smem()] * 3 + [anywhere] * 11,
+        in_specs=[in_smem()] * 3 + [anywhere] * 12,
         out_specs=(anywhere, anywhere, in_vmem(), in_vmem(), anywhere, anywhere),
         scratch_shapes=[pltpu.VMEM(arg.shape, arg.dtype) for arg in args[3:]]
         + [
@@ -395,7 +470,7 @@
             pltpu.VMEM((CELLS, C), BF),
             pltpu.VMEM((CELLS, C), F32),
             pltpu.VMEM((16, 16, 16, C), BF),
-            pltpu.SemaphoreType.DMA((11,)),
+            pltpu.SemaphoreType.DMA((12,)),
             pltpu.SemaphoreType.DMA((18,)),
         ],
         compiler_params=params(),
@@ -410,7 +485,7 @@
         in_specs=[in_smem()] * 3 + [in_vmem()] * 5,
         out_specs=in_vmem(),
         scratch_shapes=[pltpu.VMEM((STEPS, CELLS + 2 * SIDE, 3 * C), BF)],
-        compiler_params=params(),
+        compiler_params=params(20),
         cost_estimate=pl.CostEstimate(
             flops=2 * STEPS * CELLS * C * C * 9, bytes_accessed=4 << 20, transcendentals=0
         ),
@@ -441,7 +516,7 @@
         out_shape=(shape((9, 16, C), F32), gate, gate, gate, shape((8, 16), F32)),
         in_specs=[in_vmem()],
         out_specs=tuple([in_vmem()] * 5),
-        compiler_params=params(),
+        compiler_params=params(8),
         name="finish",
     )(whole)
 
@@ -475,12 +550,14 @@
     to_next, to_prev = edges_call(fields)
     prev = lax.ppermute(to_next, belt, RING)
     following = lax.ppermute(to_prev, belt, BACK)
+    raw = early_call(fields, conv).reshape(STEPS, SIDE, SIDE, C)
     grad_state, part_conv, out_next, out_prev, keep, send = main_call(
         *seams,
         fields,
         prev,
         following,
         conv,
+        raw,
         state_start.reshape(CELLS, C),
         w_update,
         w_reset,

time: 95 us -> 92.3 us (0.972)
  Pallas kernels: 30.9 us -> 27.6 us
  starting transfers between devices: 23.3 us -> 20.1 us
  other arithmetic: 3.91 us -> 5.25 us
  local copies, waits for them, and re-layouts: 0.69 us -> 1.91 us
  waiting for transfers between devices: 19.7 us -> 20.8 us
    pallas_call x0 -> x1, Pallas kernels: none -> 5.22 us  [early_call(): pl.pallas_call(early_kernel, out_shape=shape(raw, F32), in_specs=[anywher...]
    pallas_call x1, Pallas kernels: 22 us -> 17.4 us  [main_call(): pl.pallas_call(main_kernel, out_shape=(shape((CELLS, C), F32), shape((STE...]
    ppermute x1, starting transfers between devices: 3.55 us -> 1.13 us  [body(): following = lax.ppermute(out_prev, belt, BACK)]
    all_to_all x1, waiting for transfers between devices: 13 us -> 15.2 us  [body(): held = lax.all_to_all(held, ('x_hi', 'y'), 0, 0, tiled=True)]
    ppermute x1, waiting for transfers between devices: 2.14 us -> 0.01 us  [body(): prev = lax.ppermute(to_next, belt, RING)]
    pallas_call x1, Pallas kernels: 1.97 us -> 0.1 us  [edges_call(): pl.pallas_call(edges_kernel, out_shape=(shape(EDGE), shape(EDGE)), in_spe...]
    convert_element_type x2, other arithmetic: 0.82 us -> 2.1 us  [body(): held = added(held).astype(BF)]
    unnamed x12 -> x20, local copies, waits for them, and re-layouts: 0.68 us -> 1.9 us
  transfers between devices with their start and end apart: 7 -> 7, of which waited for: 4 -> 3; matrix products, arithmetic and copies ran while one was open for 1% -> 3% of each run, Pallas kernels for 6% -> 10%
where the time goes in v3:
time: 92.3 us; the launch traced here: 91.9 us
  Pallas kernels  27.6 us (30%)
  waiting for transfers between devices  20.8 us (23%)
  starting transfers between devices  20.1 us (22%)
  blocking collectives  15.4 us (17%)
  other arithmetic  5.25 us (6%)
  local copies, waits for them, and re-layouts  1.91 us (2%)
    pallas_call x1, Pallas kernels, main_call(): pl.pallas_call(main_kernel, out_shape=(shape((CELLS, C), F32), shape((STE...  17.4 us
    all_to_all x1, blocking collectives, body(): whole = lax.all_to_all(whole, dp, 0, 0, tiled=True)  15.4 us
    all_to_all x1, waiting for transfers between devices, body(): held = lax.all_to_all(held, ('x_hi', 'y'), 0, 0, tiled=True)  15.2 us
    all_to_all x1, starting transfers between devices, body(): held = lax.all_to_all(held, ('x_hi', 'y'), 0, 0, tiled=True)  6.5 us
    pallas_call x1, Pallas kernels, early_call(): pl.pallas_call(early_kernel, out_shape=shape(raw, F32), in_specs=[anywher...  5.22 us
    ppermute x1, starting transfers between devices, body(): following = lax.ppermute(to_prev, belt, BACK)  4.96 us
    pallas_call x1, Pallas kernels, fields_call(): pl.pallas_call(fields_kernel, out_shape=shape((STEPS, SIDE, SIDE, C)), in...  4.29 us
    all_to_all x1, starting transfers between devices, body(): held = lax.all_to_all(held, belt, 0, 0, tiled=True)  3.52 us
  transfers between devices with their start and end apart: 7, of which 3 were waited for; matrix products, arithmetic and copies ran while one was open for 3% of the time, Pallas kernels for 10%

profile of v3, /device:TPU:1, one launch (start us, length us, event | category | flops | bytes accessed | tf_op | source)
XLA Modules:
  0.0 91.9 jit_solution(18436432766962640745)
XLA Ops:
  0.6 0.0 copy-start
  0.6 1.2 %copy-done = bf16[1,1,2,32,32,256]{5,4,3,2,1,0:T(8,128)(2,1)S(1)} copy-done((bf16[1,1,2,32,32,256]{5,4,3,2,1,0:T(8,128)(2,1)S(1)}, bf16[1,1,2,32,32,256]{5,4,3,2,1,0:T(8,128)(2,1)}, u32[]{:S(2)}) %copy-start) | copy-done | bytes 1048600
  1.9 0.1 edges.1
  2.0 2.5 %collective-permute-start = (bf16[2,3,32,256]{3,2,1,0:T(8,128)(2,1)S(1)}, bf16[2,3,32,256]{3,2,1,0:T(8,128)(2,1)S(1)}, u32[]{:S(2)}, u32[]{:S(2)}) collective-permute-start(bf16[2,3,32,256]{3,2,1,0:T(8,128)(2,1)S(1)} %get-tuple-element.25), channel_id=1, source_target_pairs={{0,1},{1,2},{2,3},{3,4},{4,5},{5,6},{6,7},{7,8},{8,9},{9,10},{10,1... | collective-permute-start | bytes 294920 | tf_op jit(solution)/shard_map/ppermute | solution.py:551
  4.5 5.0 %collective-permute-start.1 = (bf16[2,3,32,256]{3,2,1,0:T(8,128)(2,1)S(1)}, bf16[2,3,32,256]{3,2,1,0:T(8,128)(2,1)S(1)}, u32[]{:S(2)}, u32[]{:S(2)}) collective-permute-start(bf16[2,3,32,256]{3,2,1,0:T(8,128)(2,1)S(1)} %get-tuple-element.26), channel_id=1, source_target_pairs={{1,0},{2,1},{3,2},{4,3},{5,4},{6,5},{7,6},{8,7},{9,8},{10,9},{11,1... | collective-permute-start | bytes 294920 | tf_op jit(solution)/shard_map/ppermute | solution.py:552
  9.5 5.2 %early.1 = f32[2,1024,256]{2,1,0:T(8,128)} custom-call(bf16[2,32,32,256]{3,2,1,0:T(8,128)(2,1)} %bitcast.24, bf16[2304,256]{1,0:T(8,128)(2,1)} %bitcast.27), custom_call_target="tpu_custom_call" | custom-call | flops 2415919104 | bytes 5242880 | tf_op jit(solution)/shard_map/early/pallas_call | solution.py:428
  14.7 0.6 pad_add_fusion.info_ref
  15.3 0.6 copy-done.7
  15.9 0.0 copy-done.8
  16.0 17.4 %steps.1 = (f32[1024,256]{1,0:T(8,128)}, bf16[2,1024,256]{2,1,0:T(8,128)(2,1)}, bf16[2,3,32,256]{3,2,1,0:T(8,128)(2,1)}, bf16[2,3,32,256]{3,2,1,0:T(8,128)(2,1)}...) custom-call(s32[2]{0:T(128)} %pad_add_fusion.info_ref, s32[4,16]{1,0:T(4,128)} %bitcast.30, ...), custom_call_target="tpu_custom_call" | custom-call | tf_op jit(solution)/shard_map/steps/pallas_call | solution.py:450
  33.3 1.0 %collective-permute-start.2 = (bf16[8,16,16,256]{3,2,1,0:T(8,128)(2,1)}, bf16[8,16,16,256]{3,2,1,0:T(8,128)(2,1)S(1)}, u32[]{:S(2)}, u32[]{:S(2)}) collective-permute-start(bf16[8,16,16,256]{3,2,1,0:T(8,128)(2,1)} %get-tuple-element.28), channel_id=1, source_target_pairs={{0,16},{16,0},{1,17},{17,1},{2,18},{18,2},{3,19},{19,3},{4,20},{20... | collective-permute-start | bytes 3145736 | tf_op jit(solution)/shard_map/ppermute | solution.py:569
  34.3 2.5 %collective-permute-done.2 = bf16[8,16,16,256]{3,2,1,0:T(8,128)(2,1)S(1)} collective-permute-done((bf16[8,16,16,256]{3,2,1,0:T(8,128)(2,1)}, bf16[8,16,16,256]{3,2,1,0:T(8,128)(2,1)S(1)}, u32[]{:S(2)}, u32[]{:S(2)}) %collective-permute-start.2) | collective-permute-done | bytes 1048608 | tf_op jit(solution)/shard_map/ppermute | solution.py:569
  36.8 2.6 %add_convert_fusion = bf16[8,16,16,256]{3,2,1,0:T(8,128)(2,1)} fusion(bf16[8,16,16,256]{3,2,1,0:T(8,128)(2,1)S(1)} %collective-permute-done.2, bf16[8,16,16,256]{3,2,1,0:T(8,128)(2,1)} %get-tuple-element.27), kind=kLoop, calls=%fused_computation | loop fusion | flops 2097152 | bytes 3145728 | tf_op jit(solution)/shard_map/convert_element_type | solution.py:570
  39.4 0.0 copy-start.5
  39.4 6.5 %all-to-all-start = ((bf16[8,16,16,256]{3,2,1,0:T(8,128)(2,1)}), bf16[8,16,16,256]{3,2,1,0:T(8,128)(2,1)}, u32[]{:S(2)}, u32[]{:S(2)}) async-start(bf16[8,16,16,256]{3,2,1,0:T(8,128)(2,1)} %add_convert_fusion), calls=%async_computation | async-start | bytes 2097152 | tf_op jit(solution)/shard_map/all_to_all | solution.py:571
  45.9 1.1 %collective-permute-start.4 = (bf16[2,3,32,256]{3,2,1,0:T(8,128)(2,1)S(1)}, bf16[2,3,32,256]{3,2,1,0:T(8,128)(2,1)S(1)}, u32[]{:S(2)}, u32[]{:S(2)}) collective-permute-start(bf16[2,3,32,256]{3,2,1,0:T(8,128)(2,1)S(1)} %copy-done.9), channel_id=1, source_target_pairs={{1,0},{2,1},{3,2},{4,3},{5,4},{6,5},{7,6},{8,7},{9,8},{10,9},{11,1... | collective-permute-start | bytes 294920 | tf_op jit(solution)/shard_map/ppermute | solution.py:574
  47.1 0.4 collective-permute-start.3
  47.5 15.2 %all-to-all-done = bf16[8,16,16,256]{3,2,1,0:T(8,128)(2,1)} async-done(((bf16[8,16,16,256]{3,2,1,0:T(8,128)(2,1)}), bf16[8,16,16,256]{3,2,1,0:T(8,128)(2,1)}, u32[]{:S(2)}, u32[]{:S(2)}) %all-to-all-start) | async-done | bytes 1048608 | tf_op jit(solution)/shard_map/all_to_all | solution.py:571
  62.7 2.1 %fusion = bf16[16,16,256]{2,1,0:T(8,128)(2,1)} fusion(bf16[8,16,16,256]{3,2,1,0:T(8,128)(2,1)} %all-to-all-done), kind=kLoop, calls=%fused_computation.2 | loop fusion | flops 1048576 | bytes 1179648 | tf_op jit(solution)/shard_map/convert_element_type | solution.py:572
  64.7 3.5 %all-to-all-start.1 = ((bf16[16,16,256]{2,1,0:T(8,128)(2,1)}), bf16[16,16,256]{2,1,0:T(8,128)(2,1)S(1)}, u32[]{:S(2)}, u32[]{:S(2)}) async-start(bf16[16,16,256]{2,1,0:T(8,128)(2,1)} %fusion), calls=%async_computation.1 | async-start | bytes 262144 | tf_op jit(solution)/shard_map/all_to_all | solution.py:577
  68.3 4.3 %fields.1 = bf16[2,32,32,256]{3,2,1,0:T(8,128)(2,1)} custom-call(s32[2]{0:T(128)S(1)} %copy-done.4, s32[4,16]{1,0:T(4,128)S(1)} %bitcast.31, s32[4,16]{1,0:T(4,128)S(1)} %bitcast.33, bf16[2,1024,256]{2,1,0:T(8,128)(2,1)S(1)} %copy-done.5, bf16[2,3,32,256]{3,2,1,0:T(8,128)(2,1)S(1)} %copy-done.6, bf16[2,3,32,256]{3,2,1,0:T(8,128)(2,1)S(1)} %collective-permute-done.3.prev_ref, ...), custom_call_target="tpu_custom_call" | custom-call | flops 2415919104 | bytes 4194304 | tf_op jit(solution)/shard_map/fields/pallas_call | solution.py:482
  72.6 3.1 %all-to-all-done.1 = bf16[16,16,256]{2,1,0:T(8,128)(2,1)S(1)} async-done(((bf16[16,16,256]{2,1,0:T(8,128)(2,1)}), bf16[16,16,256]{2,1,0:T(8,128)(2,1)S(1)}, u32[]{:S(2)}, u32[]{:S(2)}) %all-to-all-start.1) | async-done | bytes 131104 | tf_op jit(solution)/shard_map/all_to_all | solution.py:577
  75.8 15.4 %all_to_all.15.whole_ref = bf16[16,16,256]{2,1,0:T(8,128)(2,1)S(1)} all-to-all(bf16[16,16,256]{2,1,0:T(8,128)(2,1)S(1)} %broadcast_in_dim.10), channel_id=1, replica_groups=mesh['x_hi'=2,'y'=4,'core'=2,'x_lo'=2,'z'=8] {'x_hi','y','core'}, dimensions={0} | all-to-all | bytes 262144 | tf_op jit(solution)/shard_map/all_to_all | solution.py:581
  91.2 0.7 finish.1
  (21 shorter events, 0.1 us)
Async XLA Ops:
  0.6 1.2 %copy-start = (bf16[1,1,2,32,32,256]{5,4,3,2,1,0:T(8,128)(2,1)S(1)}, bf16[1,1,2,32,32,256]{5,4,3,2,1,0:T(8,128)(2,1)}, u32[]{:S(2)}) copy-start(bf16[1,1,2,32,32,256]{5,4,3,2,1,0:T(8,128)(2,1)} %param.11) | copy-start | bytes 3145732
  2.0 13.3 %collective-permute-start = (bf16[2,3,32,256]{3,2,1,0:T(8,128)(2,1)S(1)}, bf16[2,3,32,256]{3,2,1,0:T(8,128)(2,1)S(1)}, u32[]{:S(2)}, u32[]{:S(2)}) collective-permute-start(bf16[2,3,32,256]{3,2,1,0:T(8,128)(2,1)S(1)} %get-tuple-element.25), channel_id=1, source_target_pairs={{0,1},{1,2},{2,3},{3,4},{4,5},{5,6},{6,7},{7,8},{8,9},{9,10},{10,1... | collective-permute-start | bytes 294920 | tf_op jit(solution)/shard_map/ppermute | solution.py:551
  4.5 10.8 %collective-permute-start.1 = (bf16[2,3,32,256]{3,2,1,0:T(8,128)(2,1)S(1)}, bf16[2,3,32,256]{3,2,1,0:T(8,128)(2,1)S(1)}, u32[]{:S(2)}, u32[]{:S(2)}) collective-permute-start(bf16[2,3,32,256]{3,2,1,0:T(8,128)(2,1)S(1)} %get-tuple-element.26), channel_id=1, source_target_pairs={{1,0},{2,1},{3,2},{4,3},{5,4},{6,5},{7,6},{8,7},{9,8},{10,9},{11,1... | collective-permute-start | bytes 294920 | tf_op jit(solution)/shard_map/ppermute | solution.py:552
  15.3 0.6 copy-start.7
  15.3 0.7 copy-start.8
  33.3 3.5 %collective-permute-start.2 = (bf16[8,16,16,256]{3,2,1,0:T(8,128)(2,1)}, bf16[8,16,16,256]{3,2,1,0:T(8,128)(2,1)S(1)}, u32[]{:S(2)}, u32[]{:S(2)}) collective-permute-start(bf16[8,16,16,256]{3,2,1,0:T(8,128)(2,1)} %get-tuple-element.28), channel_id=1, source_target_pairs={{0,16},{16,0},{1,17},{17,1},{2,18},{18,2},{3,19},{19,3},{4,20},{20... | collective-permute-start | bytes 3145736 | tf_op jit(solution)/shard_map/ppermute | solution.py:569
  36.8 9.1 %copy-start.9 = (bf16[2,3,32,256]{3,2,1,0:T(8,128)(2,1)S(1)}, bf16[2,3,32,256]{3,2,1,0:T(8,128)(2,1)}, u32[]{:S(2)}) copy-start(bf16[2,3,32,256]{3,2,1,0:T(8,128)(2,1)} %get-tuple-element.30) | copy-start | bytes 294916
  36.8 10.2 %copy-start.6 = (bf16[2,3,32,256]{3,2,1,0:T(8,128)(2,1)S(1)}, bf16[2,3,32,256]{3,2,1,0:T(8,128)(2,1)}, u32[]{:S(2)}) copy-start(bf16[2,3,32,256]{3,2,1,0:T(8,128)(2,1)} %get-tuple-element.29.own_ref) | copy-start | bytes 294916
  39.4 28.9 %copy-start.1 = (bf16[9,256,256]{2,1,0:T(8,128)(2,1)S(1)}, bf16[9,256,256]{2,1,0:T(8,128)(2,1)}, u32[]{:S(2)}) copy-start(bf16[9,256,256]{2,1,0:T(8,128)(2,1)} %param.15) | copy-start | bytes 3538948
  39.4 28.9 %copy-start.2 = (s32[16,4]{0,1:T(4,128)S(1)}, s32[16,4]{0,1:T(4,128)}, u32[]{:S(2)}) copy-start(s32[16,4]{0,1:T(4,128)} %param.20) | copy-start | bytes 772
  39.4 28.9 %copy-start.3 = (s32[16,4]{0,1:T(4,128)S(1)}, s32[16,4]{0,1:T(4,128)}, u32[]{:S(2)}) copy-start(s32[16,4]{0,1:T(4,128)} %param.21) | copy-start | bytes 772
  39.4 28.9 %copy-start.4 = (s32[2]{0:T(128)S(1)}, s32[2]{0:T(128)}, u32[]{:S(2)}) copy-start(s32[2]{0:T(128)} %pad_add_fusion.info_ref) | copy-start | bytes 28
  39.4 28.9 %copy-start.5 = (bf16[2,1024,256]{2,1,0:T(8,128)(2,1)S(1)}, bf16[2,1024,256]{2,1,0:T(8,128)(2,1)}, u32[]{:S(2)}) copy-start(bf16[2,1024,256]{2,1,0:T(8,128)(2,1)} %get-tuple-element.32.part_conv_ref) | copy-start | bytes 3145732
  39.4 23.2 %all-to-all-start = ((bf16[8,16,16,256]{3,2,1,0:T(8,128)(2,1)}), bf16[8,16,16,256]{3,2,1,0:T(8,128)(2,1)}, u32[]{:S(2)}, u32[]{:S(2)}) async-start(bf16[8,16,16,256]{3,2,1,0:T(8,128)(2,1)} %add_convert_fusion), calls=%async_computation | async-start | bytes 2097152 | tf_op jit(solution)/shard_map/all_to_all | solution.py:571
  45.9 18.8 %collective-permute-start.4 = (bf16[2,3,32,256]{3,2,1,0:T(8,128)(2,1)S(1)}, bf16[2,3,32,256]{3,2,1,0:T(8,128)(2,1)S(1)}, u32[]{:S(2)}, u32[]{:S(2)}) collective-permute-start(bf16[2,3,32,256]{3,2,1,0:T(8,128)(2,1)S(1)} %copy-done.9), channel_id=1, source_target_pairs={{1,0},{2,1},{3,2},{4,3},{5,4},{6,5},{7,6},{8,7},{9,8},{10,9},{11,1... | collective-permute-start | bytes 294920 | tf_op jit(solution)/shard_map/ppermute | solution.py:574
  47.1 17.7 %collective-permute-start.3 = (bf16[2,3,32,256]{3,2,1,0:T(8,128)(2,1)S(1)}, bf16[2,3,32,256]{3,2,1,0:T(8,128)(2,1)S(1)}, u32[]{:S(2)}, u32[]{:S(2)}) collective-permute-start(bf16[2,3,32,256]{3,2,1,0:T(8,128)(2,1)S(1)} %copy-done.6), channel_id=1, source_target_pairs={{0,1},{1,2},{2,3},{3,4},{4,5},{5,6},{6,7},{7,8},{8,9},{9,10},{10,1... | collective-permute-start | bytes 294920 | tf_op jit(solution)/shard_map/ppermute | solution.py:573
  64.7 11.0 %all-to-all-start.1 = ((bf16[16,16,256]{2,1,0:T(8,128)(2,1)}), bf16[16,16,256]{2,1,0:T(8,128)(2,1)S(1)}, u32[]{:S(2)}, u32[]{:S(2)}) async-start(bf16[16,16,256]{2,1,0:T(8,128)(2,1)} %fusion), calls=%async_computation.1 | async-start | bytes 262144 | tf_op jit(solution)/shard_map/all_to_all | solution.py:577

commit v4 on v3

--- a/solution.py
+++ b/solution.py
@@ -48,8 +48,8 @@
             ref[step, 2] = fields_ref[step, SIDE - 1]
 
 
-def seam_of(info_ref, belt_ref, turns_ref, side):
-    tile = info_ref[0]
+def seam_of(belt_ref, turns_ref, side):
+    tile = lax.axis_index(("x_lo", "z"))
     partner = belt_ref[side, tile]
     other = lax.rem(side + 2 - turns_ref[side, tile], 4)
     before = lax.rem(tile + 15, 16)
@@ -59,14 +59,14 @@
     return jnp.where(flip, base + SIDE - 1, base), jnp.where(flip, -1, 1)
 
 
-def seam_rows(info_ref, belt_ref, turns_ref, own_top, own_bottom, from_prev, from_next):
+def seam_rows(belt_ref, turns_ref, own_top, own_bottom, from_prev, from_next):
     stacked = jnp.concatenate(
         [own_top, own_bottom, from_prev[1], from_prev[2], from_next[1], from_next[2]], axis=0
     )
     rows = iota((2 * SIDE, 6 * SIDE), 0)
     cols = iota((2 * SIDE, 6 * SIDE), 1)
-    top_base, top_sign = seam_of(info_ref, belt_ref, turns_ref, 0)
-    bottom_base, bottom_sign = seam_of(info_ref, belt_ref, turns_ref, 2)
+    top_base, top_sign = seam_of(belt_ref, turns_ref, 0)
+    bottom_base, bottom_sign = seam_of(belt_ref, turns_ref, 2)
     wanted = jnp.where(
         rows < SIDE, top_base + top_sign * rows, bottom_base + bottom_sign * (rows - SIDE)
     )
@@ -119,14 +119,13 @@
 
 
 def main_kernel(
-    info_ref,
     belt_ref,
     turns_ref,
     *refs,
 ):
     sources, refs = refs[:12], refs[12:]
-    grad_state_out, part_conv_out, to_next_ref, to_prev_ref, keep_out, send_out = refs[:6]
-    held, refs = refs[6:18], refs[18:]
+    grad_state_out, part_conv_out, keep_out, send_out = refs[:4]
+    held, refs = refs[4:16], refs[16:]
     (
         windows,
         joined,
@@ -165,7 +164,6 @@
     tops, bottoms, lefts, rights = [], [], [], []
     for step in range(STEPS):
         seams = seam_rows(
-            info_ref,
             belt_ref,
             turns_ref,
             fields_ref[step, 0],
@@ -275,36 +273,7 @@
     for store in stores:
         store.start()
 
-    picks = []
-    row = iota((SIDE, CELLS), 0)
-    cell = iota((SIDE, CELLS), 1)
-    for col in (0, SIDE - 1):
-        for p in range(3):
-            at = row + 1 - p
-            picks.append(one_hot((cell == at * SIDE + col) & (at >= 0) & (at < SIDE)))
-    for line in (0, SIDE - 1):
-        for q in range(3):
-            at = row + 1 - q
-            picks.append(one_hot((cell == line * SIDE + at) & (at >= 0) & (at < SIDE)))
-    picks = jnp.concatenate(picks, axis=0)
-    taps = [0, 3, 6, 2, 5, 8, 0, 1, 2, 6, 7, 8]
-    for step in range(STEPS):
-        picked = mm(picks, part_conv[step]).astype(BF)
-        outside = []
-        for side in range(4):
-            total = jnp.zeros((SIDE, C), F32)
-            for k in range(3 * side, 3 * side + 3):
-                total = total + mm_nt(
-                    picked[k * SIDE : (k + 1) * SIDE], conv_ref[taps[k] * C : (taps[k] + 1) * C, :]
-                )
-            outside.append(total.astype(BF))
-        to_next_ref[step, 0] = outside[1]
-        to_prev_ref[step, 0] = outside[0]
-        for ref in (to_next_ref, to_prev_ref):
-            ref[step, 1] = outside[2]
-            ref[step, 2] = outside[3]
-
-    core = info_ref[1]
+    core = lax.axis_index("core")
 
     def share(block, value):
         shares[block] = value.reshape(16, 16, C)
@@ -337,8 +306,38 @@
         store.wait()
 
 
+def outside_kernel(part_conv_ref, conv_ref, to_next_ref, to_prev_ref):
+    picks = []
+    row = iota((SIDE, CELLS), 0)
+    cell = iota((SIDE, CELLS), 1)
+    for col in (0, SIDE - 1):
+        for p in range(3):
+            at = row + 1 - p
+            picks.append(one_hot((cell == at * SIDE + col) & (at >= 0) & (at < SIDE)))
+    for line in (0, SIDE - 1):
+        for q in range(3):
+            at = row + 1 - q
+            picks.append(one_hot((cell == line * SIDE + at) & (at >= 0) & (at < SIDE)))
+    picks = jnp.concatenate(picks, axis=0)
+    taps = [0, 3, 6, 2, 5, 8, 0, 1, 2, 6, 7, 8]
+    for step in range(STEPS):
+        picked = mm(picks, part_conv_ref[step]).astype(BF)
+        outside = []
+        for side in range(4):
+            total = jnp.zeros((SIDE, C), F32)
+            for k in range(3 * side, 3 * side + 3):
+                total = total + mm_nt(
+                    picked[k * SIDE : (k + 1) * SIDE], conv_ref[taps[k] * C : (taps[k] + 1) * C, :]
+                )
+            outside.append(total.astype(BF))
+        to_next_ref[step, 0] = outside[1]
+        to_prev_ref[step, 0] = outside[0]
+        for ref in (to_next_ref, to_prev_ref):
+            ref[step, 1] = outside[2]
+            ref[step, 2] = outside[3]
+
+
 def fields_kernel(
-    info_ref,
     belt_ref,
     turns_ref,
     part_conv_ref,
@@ -361,7 +360,6 @@
             zero,
         )
         seams = seam_rows(
-            info_ref,
             belt_ref,
             turns_ref,
             own_ref[step, 1],
@@ -452,14 +450,12 @@
         out_shape=(
             shape((CELLS, C), F32),
             shape((STEPS, CELLS, C)),
-            shape(EDGE),
-            shape(EDGE),
             shape((8, 16, 16, C)),
             shape((8, 16, 16, C)),
         ),
-        in_specs=[in_smem()] * 3 + [anywhere] * 12,
-        out_specs=(anywhere, anywhere, in_vmem(), in_vmem(), anywhere, anywhere),
-        scratch_shapes=[pltpu.VMEM(arg.shape, arg.dtype) for arg in args[3:]]
+        in_specs=[in_smem()] * 2 + [anywhere] * 12,
+        out_specs=(anywhere,) * 4,
+        scratch_shapes=[pltpu.VMEM(arg.shape, arg.dtype) for arg in args[2:]]
         + [
             pltpu.VMEM((STEPS, CELLS + 2 * SIDE, 3 * C), BF),
             pltpu.VMEM((STEPS, CELLS, 2 * C), BF),
@@ -478,11 +474,59 @@
     )(*args)
 
 
+def outside_call(part_conv, conv):
+    return pl.pallas_call(
+        outside_kernel,
+        out_shape=(shape(EDGE), shape(EDGE)),
+        in_specs=[in_vmem()] * 2,
+        out_specs=(in_vmem(), in_vmem()),
+        compiler_params=params(16),
+        cost_estimate=pl.CostEstimate(flops=1 << 30, bytes_accessed=3 << 20, transcendentals=0),
+        name="outside",
+    )(part_conv, conv)
+
+
+def pair_kernel(left_ref, right_ref, out_ref):
+    out_ref[...] = (left_ref[...].astype(F32) + right_ref[...].astype(F32)).astype(BF)
+
+
+def pair_call(left, right):
+    block = pl.BlockSpec((2, 16, 16, C), lambda i: (i, 0, 0, 0))
+    return pl.pallas_call(
+        pair_kernel,
+        out_shape=shape(left.shape),
+        grid=(4,),
+        in_specs=[block, block],
+        out_specs=block,
+        compiler_params=params(8),
+        name="pair",
+    )(left, right)
+
+
+def added_kernel(pieces_ref, out_ref):
+    total = pieces_ref[0].astype(F32)
+    for k in range(1, 8):
+        total = total + pieces_ref[k].astype(F32)
+    out_ref[...] = total.astype(BF)
+
+
+def added_call(pieces):
+    return pl.pallas_call(
+        added_kernel,
+        out_shape=shape((16, 16, C)),
+        grid=(2,),
+        in_specs=[pl.BlockSpec((8, 8, 16, C), lambda i: (0, i, 0, 0))],
+        out_specs=pl.BlockSpec((8, 16, C), lambda i: (i, 0, 0)),
+        compiler_params=params(8),
+        name="added",
+    )(pieces)
+
+
 def fields_call(*args):
     return pl.pallas_call(
         fields_kernel,
         out_shape=shape((STEPS, SIDE, SIDE, C)),
-        in_specs=[in_smem()] * 3 + [in_vmem()] * 5,
+        in_specs=[in_smem()] * 2 + [in_vmem()] * 5,
         out_specs=in_vmem(),
         scratch_shapes=[pltpu.VMEM((STEPS, CELLS + 2 * SIDE, 3 * C), BF)],
         compiler_params=params(20),
@@ -543,15 +587,14 @@
 ):
     dp = ("x_hi", "y", "core")
     belt = ("x_lo", "z")
-    info = jnp.stack([lax.axis_index(belt), lax.axis_index("core")]).astype(jnp.int32)
-    seams = (info, neighbor_tile.T, seam_turns.T)
+    seams = (neighbor_tile.T, seam_turns.T)
     fields = fields_in[0, 0]
     conv = conv_weight.reshape(9 * C, C)
     to_next, to_prev = edges_call(fields)
     prev = lax.ppermute(to_next, belt, RING)
     following = lax.ppermute(to_prev, belt, BACK)
     raw = early_call(fields, conv).reshape(STEPS, SIDE, SIDE, C)
-    grad_state, part_conv, out_next, out_prev, keep, send = main_call(
+    grad_state, part_conv, keep, send = main_call(
         *seams,
         fields,
         prev,
@@ -567,12 +610,13 @@
         head_weight,
     )
     got = lax.ppermute(send, "core", [(0, 1), (1, 0)])
-    held = (keep.astype(F32) + got.astype(F32)).astype(BF)
+    held = pair_call(keep, got)
     held = lax.all_to_all(held, ("x_hi", "y"), 0, 0, tiled=True)
-    held = added(held).astype(BF)
+    out_next, out_prev = outside_call(part_conv, conv)
     prev = lax.ppermute(out_next, belt, RING)
     following = lax.ppermute(out_prev, belt, BACK)
     held, prev, following = lax.optimization_barrier((held, prev, following))
+    held = added_call(held)
     grad_fields = fields_call(*seams, part_conv, out_next, prev, following, conv)
     held = lax.all_to_all(held, belt, 0, 0, tiled=True)
     held = added(held).astype(BF)

time: 92.3 us -> 88 us (0.953)
  other arithmetic: 5.25 us -> 0.02 us
  waiting for transfers between devices: 20.8 us -> 17.5 us
  local copies, waits for them, and re-layouts: 1.91 us -> 4.66 us
  Pallas kernels: 27.6 us -> 29.4 us
    all_to_all x1, waiting for transfers between devices: 15.2 us -> 7.24 us  [body(): held = lax.all_to_all(held, ('x_hi', 'y'), 0, 0, tiled=True)]
    pallas_call x0 -> x3, Pallas kernels: none -> 4.26 us  [the longest x1 1.74 us: outside_call(): pl.pallas_call(outside_kernel, out_shape=(shape(EDGE), shape(EDGE)), in_s...]
    ppermute x1, waiting for transfers between devices: 0.01 us -> 3.16 us  [body(): prev = lax.ppermute(out_next, belt, RING)]
    unnamed x20, local copies, waits for them, and re-layouts: 1.9 us -> 4.65 us
    convert_element_type x1 -> x0, other arithmetic: 2.57 us -> none  [body(): held = (keep.astype(F32) + got.astype(F32)).astype(BF)]
    pallas_call x1, Pallas kernels: 17.4 us -> 14.9 us  [main_call(): pl.pallas_call(main_kernel, out_shape=(shape((CELLS, C), F32), shape((STE...]
    ppermute x1, waiting for transfers between devices: 0.01 us -> 2.3 us  [body(): following = lax.ppermute(out_prev, belt, BACK)]
    convert_element_type x2 -> x1, other arithmetic: 2.1 us -> 0.02 us  [body(): held = added(held).astype(BF)]
  transfers between devices with their start and end apart: 7 -> 7, of which waited for: 3 -> 5; matrix products, arithmetic and copies ran while one was open for 3% -> 0% of each run, Pallas kernels for 10% -> 13%
where the time goes in v4:
time: 88 us; the launch traced here: 87.6 us
  Pallas kernels  29.4 us (33%)
  starting transfers between devices  19.9 us (23%)
  waiting for transfers between devices  17.5 us (20%)
  blocking collectives  15.4 us (18%)
  local copies, waits for them, and re-layouts  4.66 us (5%)
    all_to_all x1, blocking collectives, body(): whole = lax.all_to_all(whole, dp, 0, 0, tiled=True)  15.4 us
    pallas_call x1, Pallas kernels, main_call(): pl.pallas_call(main_kernel, out_shape=(shape((CELLS, C), F32), shape((STE...  14.9 us
    all_to_all x1, waiting for transfers between devices, body(): held = lax.all_to_all(held, ('x_hi', 'y'), 0, 0, tiled=True)  7.24 us
    all_to_all x1, starting transfers between devices, body(): held = lax.all_to_all(held, ('x_hi', 'y'), 0, 0, tiled=True)  6.35 us
    pallas_call x1, Pallas kernels, early_call(): pl.pallas_call(early_kernel, out_shape=shape(raw, F32), in_specs=[anywher...  5.21 us
    ppermute x1, starting transfers between devices, body(): following = lax.ppermute(to_prev, belt, BACK)  4.96 us
    unnamed x20, local copies, waits for them, and re-layouts  4.65 us
    pallas_call x1, Pallas kernels, fields_call(): pl.pallas_call(fields_kernel, out_shape=shape((STEPS, SIDE, SIDE, C)), in...  4.29 us
  transfers between devices with their start and end apart: 7, of which 5 were waited for; matrix products, arithmetic and copies ran while one was open for 0% of the time, Pallas kernels for 13%

profile of v4, /device:TPU:1, one launch (start us, length us, event | category | flops | bytes accessed | tf_op | source)
XLA Modules:
  0.0 87.6 jit_solution(991509034094569029)
XLA Ops:
  0.6 1.2 %copy-done = bf16[1,1,2,32,32,256]{5,4,3,2,1,0:T(8,128)(2,1)S(1)} copy-done((bf16[1,1,2,32,32,256]{5,4,3,2,1,0:T(8,128)(2,1)S(1)}, bf16[1,1,2,32,32,256]{5,4,3,2,1,0:T(8,128)(2,1)}, u32[]{:S(2)}) %copy-start) | copy-done | bytes 1048600
  2.0 2.5 %collective-permute-start = (bf16[2,3,32,256]{3,2,1,0:T(8,128)(2,1)S(1)}, bf16[2,3,32,256]{3,2,1,0:T(8,128)(2,1)S(1)}, u32[]{:S(2)}, u32[]{:S(2)}) collective-permute-start(bf16[2,3,32,256]{3,2,1,0:T(8,128)(2,1)S(1)} %get-tuple-element.25), channel_id=1, source_target_pairs={{0,1},{1,2},{2,3},{3,4},{4,5},{5,6},{6,7},{7,8},{8,9},{9,10},{10,1... | collective-permute-start | bytes 294920 | tf_op jit(solution)/shard_map/ppermute | solution.py:594
  4.5 5.0 %collective-permute-start.1 = (bf16[2,3,32,256]{3,2,1,0:T(8,128)(2,1)S(1)}, bf16[2,3,32,256]{3,2,1,0:T(8,128)(2,1)S(1)}, u32[]{:S(2)}, u32[]{:S(2)}) collective-permute-start(bf16[2,3,32,256]{3,2,1,0:T(8,128)(2,1)S(1)} %get-tuple-element.26), channel_id=1, source_target_pairs={{1,0},{2,1},{3,2},{4,3},{5,4},{6,5},{7,6},{8,7},{9,8},{10,9},{11,1... | collective-permute-start | bytes 294920 | tf_op jit(solution)/shard_map/ppermute | solution.py:595
  9.5 5.2 %early.1 = f32[2,1024,256]{2,1,0:T(8,128)} custom-call(bf16[2,32,32,256]{3,2,1,0:T(8,128)(2,1)} %bitcast.20, bf16[2304,256]{1,0:T(8,128)(2,1)} %bitcast.23), custom_call_target="tpu_custom_call" | custom-call | flops 2415919104 | bytes 5242880 | tf_op jit(solution)/shard_map/early/pallas_call | solution.py:426
  14.7 0.6 copy-done.8
  15.4 14.9 %steps.1 = (f32[1024,256]{1,0:T(8,128)}, bf16[2,1024,256]{2,1,0:T(8,128)(2,1)}, bf16[8,16,16,256]{3,2,1,0:T(8,128)(2,1)}, bf16[8,16,16,256]{3,2,1,0:T(8,128)(2,1)}) custom-call(s32[4,16]{1,0:T(4,128)} %bitcast.27, s32[4,16]{1,0:T(4,128)} %bitcast.29, bf16[2,32,32,256]{3,2,1,0:T(8,128)(2,1)} %bitcast.21, bf16[2,3,32,256]{3,2,1,0:T(8,128)(2,1)} %copy-done.8, ...), custom_call_target="tpu_custom_call" | custom-call | tf_op jit(solution)/shard_map/steps/pallas_call | solution.py:448
  30.2 1.0 %collective-permute-start.2 = (bf16[8,16,16,256]{3,2,1,0:T(8,128)(2,1)}, bf16[8,16,16,256]{3,2,1,0:T(8,128)(2,1)S(1)}, u32[]{:S(2)}, u32[]{:S(2)}) collective-permute-start(bf16[8,16,16,256]{3,2,1,0:T(8,128)(2,1)} %get-tuple-element.28), channel_id=1, source_target_pairs={{0,16},{16,0},{1,17},{17,1},{2,18},{18,2},{3,19},{19,3},{4,20},{20... | collective-permute-start | bytes 3145736 | tf_op jit(solution)/shard_map/ppermute | solution.py:612
  31.3 2.5 %collective-permute-done.2.right_ref = bf16[8,16,16,256]{3,2,1,0:T(8,128)(2,1)S(1)} collective-permute-done((bf16[8,16,16,256]{3,2,1,0:T(8,128)(2,1)}, bf16[8,16,16,256]{3,2,1,0:T(8,128)(2,1)S(1)}, u32[]{:S(2)}, u32[]{:S(2)}) %collective-permute-start.2) | collective-permute-done | bytes 1048608 | tf_op jit(solution)/shard_map/ppermute | solution.py:612
  33.8 1.2 %copy-done.2 = bf16[8,16,16,256]{3,2,1,0:T(8,128)(2,1)S(1)} copy-done((bf16[8,16,16,256]{3,2,1,0:T(8,128)(2,1)S(1)}, bf16[8,16,16,256]{3,2,1,0:T(8,128)(2,1)}, u32[]{:S(2)}) %copy-start.2) | copy-done | bytes 1048600
  35.0 1.6 %pair.1 = bf16[8,16,16,256]{3,2,1,0:T(8,128)(2,1)} custom-call(bf16[8,16,16,256]{3,2,1,0:T(8,128)(2,1)S(1)} %copy-done.2, bf16[8,16,16,256]{3,2,1,0:T(8,128)(2,1)S(1)} %collective-permute-done.2.right_ref), custom_call_target="tpu_custom_call" | custom-call | tf_op jit(solution)/shard_map/pair/pallas_call | solution.py:495
  36.6 6.4 %all-to-all-start = ((bf16[8,16,16,256]{3,2,1,0:T(8,128)(2,1)}), bf16[8,16,16,256]{3,2,1,0:T(8,128)(2,1)S(1)}, u32[]{:S(2)}, u32[]{:S(2)}) async-start(bf16[8,16,16,256]{3,2,1,0:T(8,128)(2,1)} %pair.1), calls=%async_computation | async-start | bytes 2097152 | tf_op jit(solution)/shard_map/all_to_all | solution.py:614
  43.0 1.7 %outside.1 = (bf16[2,3,32,256]{3,2,1,0:T(8,128)(2,1)S(1)}, bf16[2,3,32,256]{3,2,1,0:T(8,128)(2,1)S(1)}) custom-call(bf16[2,1024,256]{2,1,0:T(8,128)(2,1)S(1)} %copy-done.5, bf16[2304,256]{1,0:T(8,128)(2,1)S(1)} %bitcast.25), custom_call_target="tpu_custom_call" | custom-call | flops 1073741824 | bytes 3145728 | tf_op jit(solution)/shard_map/outside/pallas_call | solution.py:478
  44.8 1.1 %collective-permute-start.4 = (bf16[2,3,32,256]{3,2,1,0:T(8,128)(2,1)S(1)}, bf16[2,3,32,256]{3,2,1,0:T(8,128)(2,1)S(1)}, u32[]{:S(2)}, u32[]{:S(2)}) collective-permute-start(bf16[2,3,32,256]{3,2,1,0:T(8,128)(2,1)S(1)} %get-tuple-element.31), channel_id=1, source_target_pairs={{1,0},{2,1},{3,2},{4,3},{5,4},{6,5},{7,6},{8,7},{9,8},{10,9},{11,1... | collective-permute-start | bytes 294920 | tf_op jit(solution)/shard_map/ppermute | solution.py:617
  46.3 2.3 %collective-permute-done.4.next_ref = bf16[2,3,32,256]{3,2,1,0:T(8,128)(2,1)S(1)} collective-permute-done((bf16[2,3,32,256]{3,2,1,0:T(8,128)(2,1)S(1)}, bf16[2,3,32,256]{3,2,1,0:T(8,128)(2,1)S(1)}, u32[]{:S(2)}, u32[]{:S(2)}) %collective-permute-start.4) | collective-permute-done | bytes 98336 | tf_op jit(solution)/shard_map/ppermute | solution.py:617
  48.6 3.2 %collective-permute-done.3.prev_ref = bf16[2,3,32,256]{3,2,1,0:T(8,128)(2,1)S(1)} collective-permute-done((bf16[2,3,32,256]{3,2,1,0:T(8,128)(2,1)S(1)}, bf16[2,3,32,256]{3,2,1,0:T(8,128)(2,1)S(1)}, u32[]{:S(2)}, u32[]{:S(2)}) %collective-permute-start.3) | collective-permute-done | bytes 98336 | tf_op jit(solution)/shard_map/ppermute | solution.py:616
  51.7 0.6 copy-done.6
  52.4 7.2 %all-to-all-done.pieces_ref = bf16[8,16,16,256]{3,2,1,0:T(8,128)(2,1)S(1)} async-done(((bf16[8,16,16,256]{3,2,1,0:T(8,128)(2,1)}), bf16[8,16,16,256]{3,2,1,0:T(8,128)(2,1)S(1)}, u32[]{:S(2)}, u32[]{:S(2)}) %all-to-all-start) | async-done | bytes 1048608 | tf_op jit(solution)/shard_map/all_to_all | solution.py:614
  59.6 0.9 added.1
  60.5 3.5 %all-to-all-start.1 = ((bf16[16,16,256]{2,1,0:T(8,128)(2,1)}), bf16[16,16,256]{2,1,0:T(8,128)(2,1)S(1)}, u32[]{:S(2)}, u32[]{:S(2)}) async-start(bf16[16,16,256]{2,1,0:T(8,128)(2,1)} %added.1), calls=%async_computation.1 | async-start | bytes 262144 | tf_op jit(solution)/shard_map/all_to_all | solution.py:621
  64.0 0.9 %copy-done.7 = bf16[2,3,32,256]{3,2,1,0:T(8,128)(2,1)S(1)} copy-done((bf16[2,3,32,256]{3,2,1,0:T(8,128)(2,1)S(1)}, bf16[2,3,32,256]{3,2,1,0:T(8,128)(2,1)}, u32[]{:S(2)}) %copy-start.7) | copy-done | bytes 98328
  64.9 4.3 %fields.1 = bf16[2,32,32,256]{3,2,1,0:T(8,128)(2,1)} custom-call(s32[4,16]{1,0:T(4,128)S(1)} %bitcast.28, s32[4,16]{1,0:T(4,128)S(1)} %bitcast.30, bf16[2,1024,256]{2,1,0:T(8,128)(2,1)S(1)} %copy-done.5, bf16[2,3,32,256]{3,2,1,0:T(8,128)(2,1)S(1)} %get-tuple-element.30.own_ref, bf16[2,3,32,256]{3,2,1,0:T(8,128)(2,1)S(1)} %copy-done.7, ...), custom_call_target="tpu_custom_call" | custom-call | flops 2415919104 | bytes 4194304 | tf_op jit(solution)/shard_map/fields/pallas_call | solution.py:526
  69.2 2.3 %all-to-all-done.1 = bf16[16,16,256]{2,1,0:T(8,128)(2,1)S(1)} async-done(((bf16[16,16,256]{2,1,0:T(8,128)(2,1)}), bf16[16,16,256]{2,1,0:T(8,128)(2,1)S(1)}, u32[]{:S(2)}, u32[]{:S(2)}) %all-to-all-start.1) | async-done | bytes 131104 | tf_op jit(solution)/shard_map/all_to_all | solution.py:621
  71.5 15.4 %all_to_all.15.whole_ref = bf16[16,16,256]{2,1,0:T(8,128)(2,1)S(1)} all-to-all(bf16[16,16,256]{2,1,0:T(8,128)(2,1)S(1)} %broadcast_in_dim.10), channel_id=1, replica_groups=mesh['x_hi'=2,'y'=4,'core'=2,'x_lo'=2,'z'=8] {'x_hi','y','core'}, dimensions={0} | all-to-all | bytes 262144 | tf_op jit(solution)/shard_map/all_to_all | solution.py:625
  86.9 0.7 finish.1
  (21 shorter events, 0.6 us)
Async XLA Ops:
  0.6 1.2 %copy-start = (bf16[1,1,2,32,32,256]{5,4,3,2,1,0:T(8,128)(2,1)S(1)}, bf16[1,1,2,32,32,256]{5,4,3,2,1,0:T(8,128)(2,1)}, u32[]{:S(2)}) copy-start(bf16[1,1,2,32,32,256]{5,4,3,2,1,0:T(8,128)(2,1)} %param.11) | copy-start | bytes 3145732
  2.0 12.7 %collective-permute-start = (bf16[2,3,32,256]{3,2,1,0:T(8,128)(2,1)S(1)}, bf16[2,3,32,256]{3,2,1,0:T(8,128)(2,1)S(1)}, u32[]{:S(2)}, u32[]{:S(2)}) collective-permute-start(bf16[2,3,32,256]{3,2,1,0:T(8,128)(2,1)S(1)} %get-tuple-element.25), channel_id=1, source_target_pairs={{0,1},{1,2},{2,3},{3,4},{4,5},{5,6},{6,7},{7,8},{8,9},{9,10},{10,1... | collective-permute-start | bytes 294920 | tf_op jit(solution)/shard_map/ppermute | solution.py:594
  4.5 10.2 %collective-permute-start.1 = (bf16[2,3,32,256]{3,2,1,0:T(8,128)(2,1)S(1)}, bf16[2,3,32,256]{3,2,1,0:T(8,128)(2,1)S(1)}, u32[]{:S(2)}, u32[]{:S(2)}) collective-permute-start(bf16[2,3,32,256]{3,2,1,0:T(8,128)(2,1)S(1)} %get-tuple-element.26), channel_id=1, source_target_pairs={{1,0},{2,1},{3,2},{4,3},{5,4},{6,5},{7,6},{8,7},{9,8},{10,9},{11,1... | collective-permute-start | bytes 294920 | tf_op jit(solution)/shard_map/ppermute | solution.py:595
  14.7 0.6 copy-start.8
  14.7 0.7 copy-start.9
  30.2 3.5 %collective-permute-start.2 = (bf16[8,16,16,256]{3,2,1,0:T(8,128)(2,1)}, bf16[8,16,16,256]{3,2,1,0:T(8,128)(2,1)S(1)}, u32[]{:S(2)}, u32[]{:S(2)}) collective-permute-start(bf16[8,16,16,256]{3,2,1,0:T(8,128)(2,1)} %get-tuple-element.28), channel_id=1, source_target_pairs={{0,16},{16,0},{1,17},{17,1},{2,18},{18,2},{3,19},{19,3},{4,20},{20... | collective-permute-start | bytes 3145736 | tf_op jit(solution)/shard_map/ppermute | solution.py:612
  33.8 1.2 %copy-start.2 = (bf16[8,16,16,256]{3,2,1,0:T(8,128)(2,1)S(1)}, bf16[8,16,16,256]{3,2,1,0:T(8,128)(2,1)}, u32[]{:S(2)}) copy-start(bf16[8,16,16,256]{3,2,1,0:T(8,128)(2,1)} %get-tuple-element.27.left_ref) | copy-start | bytes 3145732
  35.0 8.0 %copy-start.1 = (bf16[9,256,256]{2,1,0:T(8,128)(2,1)S(1)}, bf16[9,256,256]{2,1,0:T(8,128)(2,1)}, u32[]{:S(2)}) copy-start(bf16[9,256,256]{2,1,0:T(8,128)(2,1)} %param.15) | copy-start | bytes 3538948
  35.0 8.0 %copy-start.5 = (bf16[2,1024,256]{2,1,0:T(8,128)(2,1)S(1)}, bf16[2,1024,256]{2,1,0:T(8,128)(2,1)}, u32[]{:S(2)}) copy-start(bf16[2,1024,256]{2,1,0:T(8,128)(2,1)} %get-tuple-element.29.part_conv_ref) | copy-start | bytes 3145732
  36.6 23.0 %all-to-all-start = ((bf16[8,16,16,256]{3,2,1,0:T(8,128)(2,1)}), bf16[8,16,16,256]{3,2,1,0:T(8,128)(2,1)S(1)}, u32[]{:S(2)}, u32[]{:S(2)}) async-start(bf16[8,16,16,256]{3,2,1,0:T(8,128)(2,1)} %pair.1), calls=%async_computation | async-start | bytes 2097152 | tf_op jit(solution)/shard_map/all_to_all | solution.py:614
  43.0 21.0 %copy-start.3 = (s32[16,4]{0,1:T(4,128)S(1)}, s32[16,4]{0,1:T(4,128)}, u32[]{:S(2)}) copy-start(s32[16,4]{0,1:T(4,128)} %param.20) | copy-start | bytes 772
  43.0 21.0 %copy-start.4 = (s32[16,4]{0,1:T(4,128)S(1)}, s32[16,4]{0,1:T(4,128)}, u32[]{:S(2)}) copy-start(s32[16,4]{0,1:T(4,128)} %param.21) | copy-start | bytes 772
  44.8 3.8 %collective-permute-start.4 = (bf16[2,3,32,256]{3,2,1,0:T(8,128)(2,1)S(1)}, bf16[2,3,32,256]{3,2,1,0:T(8,128)(2,1)S(1)}, u32[]{:S(2)}, u32[]{:S(2)}) collective-permute-start(bf16[2,3,32,256]{3,2,1,0:T(8,128)(2,1)S(1)} %get-tuple-element.31), channel_id=1, source_target_pairs={{1,0},{2,1},{3,2},{4,3},{5,4},{6,5},{7,6},{8,7},{9,8},{10,9},{11,1... | collective-permute-start | bytes 294920 | tf_op jit(solution)/shard_map/ppermute | solution.py:617
  45.9 5.9 %collective-permute-start.3 = (bf16[2,3,32,256]{3,2,1,0:T(8,128)(2,1)S(1)}, bf16[2,3,32,256]{3,2,1,0:T(8,128)(2,1)S(1)}, u32[]{:S(2)}, u32[]{:S(2)}) collective-permute-start(bf16[2,3,32,256]{3,2,1,0:T(8,128)(2,1)S(1)} %get-tuple-element.30.own_ref), channel_id=1, source_target_pairs={{0,1},{1,2},{2,3},{3,4},{4,5},{5,6},{6,7},{7,8},{8,9},{9,10},{10,1... | collective-permute-start | bytes 294920 | tf_op jit(solution)/shard_map/ppermute | solution.py:616
  51.7 0.6 copy-start.6
  60.5 11.0 %all-to-all-start.1 = ((bf16[16,16,256]{2,1,0:T(8,128)(2,1)}), bf16[16,16,256]{2,1,0:T(8,128)(2,1)S(1)}, u32[]{:S(2)}, u32[]{:S(2)}) async-start(bf16[16,16,256]{2,1,0:T(8,128)(2,1)} %added.1), calls=%async_computation.1 | async-start | bytes 262144 | tf_op jit(solution)/shard_map/all_to_all | solution.py:621
  64.0 0.9 %copy-start.7 = (bf16[2,3,32,256]{3,2,1,0:T(8,128)(2,1)S(1)}, bf16[2,3,32,256]{3,2,1,0:T(8,128)(2,1)}, u32[]{:S(2)}) copy-start(bf16[2,3,32,256]{3,2,1,0:T(8,128)(2,1)} %copy-done.6) | copy-start | bytes 294916

commit v5 on v4

--- a/solution.py
+++ b/solution.py
@@ -2,6 +2,7 @@
 
 import jax
 import jax.numpy as jnp
+import numpy as np
 from jax import lax
 from jax.experimental import pallas as pl
 from jax.experimental.pallas import tpu as pltpu
@@ -94,26 +95,32 @@
 
 def early_kernel(fields_in, conv_in, raw_out, fields_ref, conv_ref, windows, raw_ref, sems):
     loads = [
-        pltpu.make_async_copy(fields_in, fields_ref, sems.at[0]),
-        pltpu.make_async_copy(conv_in, conv_ref, sems.at[1]),
+        pltpu.make_async_copy(fields_in.at[0], fields_ref.at[0], sems.at[0]),
+        pltpu.make_async_copy(fields_in.at[1], fields_ref.at[1], sems.at[1]),
+        pltpu.make_async_copy(conv_in, conv_ref, sems.at[2]),
     ]
     for load in loads:
         load.start()
-    loads[0].wait()
     zero = jnp.zeros((SIDE, C), F32)
     stores = []
+    loads[0].wait()
+    store_shifts(windows, 0, zero, zero, fields_ref[0].astype(F32), zero, zero)
+    loads[1].wait()
+    loads[2].wait()
     for step in range(STEPS):
-        store_shifts(windows, step, zero, zero, fields_ref[step].astype(F32), zero, zero)
         if step == 0:
-            loads[1].wait()
+            store_shifts(windows, 1, zero, zero, fields_ref[1].astype(F32), zero, zero)
         for start in range(0, CELLS, CHUNK):
             raw = jnp.zeros((CHUNK, C), F32)
             for p in range(3):
                 window = windows[step, pl.ds(start + p * SIDE, CHUNK), :]
                 raw = raw + mm(window, conv_ref[pl.ds(3 * C * p, 3 * C), :])
-            raw_ref[step, pl.ds(start, CHUNK), :] = raw
-        stores.append(pltpu.make_async_copy(raw_ref.at[step], raw_out.at[step], sems.at[2 + step]))
-        stores[step].start()
+            rows = pl.ds(start, CHUNK)
+            raw_ref[step, rows, :] = raw
+            at = (step, rows)
+            sem = sems.at[3 + step * (CELLS // CHUNK) + start // CHUNK]
+            stores.append(pltpu.make_async_copy(raw_ref.at[at], raw_out.at[at], sem))
+            stores[-1].start()
     for store in stores:
         store.wait()
 
@@ -143,7 +150,7 @@
         pltpu.make_async_copy(source, target, in_sems.at[k])
         for k, (source, target) in enumerate(zip(sources, held))
     ]
-    for load in loads:
+    for load in loads[:9]:
         load.start()
     (
         fields_ref,
@@ -207,8 +214,10 @@
         raw_ref[step, SIDE - 1, :, :] += bottom[lines]
         raw_ref[step, :, 0:8, :] += jnp.where(place == 0, left[lines][:, None, :], 0.0)
         raw_ref[step, :, SIDE - 8 : SIDE, :] += jnp.where(place == 7, right[lines][:, None, :], 0.0)
-    for load in loads[5:]:
+    for load in loads[5:9]:
         load.wait()
+    for load in loads[9:]:
+        load.start()
 
     def chunk(start):
         rows = pl.ds(start, CHUNK)
@@ -232,6 +241,9 @@
             saved.append((raw, bend, update, reset, candidate, hidden))
             hidden = following
         last_state[rows, :] = hidden.astype(BF)
+        if start == 0:
+            for load in loads[9:]:
+                load.wait()
         carried = adjoint_ref[rows, :]
         for step in reversed(range(STEPS)):
             raw, bend, update, reset, candidate, hidden = saved[step]
@@ -277,11 +289,20 @@
 
     def share(block, value):
         shares[block] = value.reshape(16, 16, C)
-        kept = pltpu.make_async_copy(shares.at[block], keep_out.at[block % 8], out_sems.at[block])
-        sent = pltpu.make_async_copy(shares.at[block], send_out.at[block % 8], out_sems.at[block])
-        pl.when(core == block // 8)(kept.start)
-        pl.when(core != block // 8)(sent.start)
-        stores.append(kept)
+        x_hi, y = block % 8 // 4, block % 4
+        if block < 8:
+            pieces = [(slice(0, 16), y, x_hi * 16)]
+        else:
+            pieces = [(slice(k * 8, k * 8 + 8), 2 * x_hi + k, y * 8) for k in range(2)]
+        for lines, place, first in pieces:
+            count = lines.stop - lines.start
+            where = (place, pl.ds(first, count))
+            sem = out_sems.at[block]
+            kept = pltpu.make_async_copy(shares.at[block, lines], keep_out.at[where], sem)
+            sent = pltpu.make_async_copy(shares.at[block, lines], send_out.at[where], sem)
+            pl.when(core == block // 8)(kept.start)
+            pl.when(core != block // 8)(sent.start)
+            stores.append(kept)
 
     def over_steps(one):
         return one(0) + one(1)
@@ -402,6 +423,10 @@
     return pltpu.CompilerParams(vmem_limit_bytes=mebibytes << 20)
 
 
+def busy():
+    return pl.CostEstimate(flops=1 << 33, bytes_accessed=1 << 16, transcendentals=0)
+
+
 def shape(dims, kind=BF):
     return jax.ShapeDtypeStruct(dims, kind)
 
@@ -433,7 +458,7 @@
             pltpu.VMEM(conv.shape, BF),
             pltpu.VMEM((STEPS, CELLS + 2 * SIDE, 3 * C), BF),
             pltpu.VMEM(raw, F32),
-            pltpu.SemaphoreType.DMA((4,)),
+            pltpu.SemaphoreType.DMA((7,)),
         ],
         compiler_params=params(),
         cost_estimate=pl.CostEstimate(
@@ -450,8 +475,8 @@
         out_shape=(
             shape((CELLS, C), F32),
             shape((STEPS, CELLS, C)),
-            shape((8, 16, 16, C)),
-            shape((8, 16, 16, C)),
+            shape((4, 32, 16, C)),
+            shape((4, 32, 16, C)),
         ),
         in_specs=[in_smem()] * 2 + [anywhere] * 12,
         out_specs=(anywhere,) * 4,
@@ -491,7 +516,7 @@
 
 
 def pair_call(left, right):
-    block = pl.BlockSpec((2, 16, 16, C), lambda i: (i, 0, 0, 0))
+    block = pl.BlockSpec((1, 32, 16, C), lambda i: (i, 0, 0, 0))
     return pl.pallas_call(
         pair_kernel,
         out_shape=shape(left.shape),
@@ -499,13 +524,14 @@
         in_specs=[block, block],
         out_specs=block,
         compiler_params=params(8),
+        cost_estimate=busy(),
         name="pair",
     )(left, right)
 
 
 def added_kernel(pieces_ref, out_ref):
     total = pieces_ref[0].astype(F32)
-    for k in range(1, 8):
+    for k in range(1, pieces_ref.shape[0]):
         total = total + pieces_ref[k].astype(F32)
     out_ref[...] = total.astype(BF)
 
@@ -513,11 +539,12 @@
 def added_call(pieces):
     return pl.pallas_call(
         added_kernel,
-        out_shape=shape((16, 16, C)),
+        out_shape=shape((32, 16, C)),
         grid=(2,),
-        in_specs=[pl.BlockSpec((8, 8, 16, C), lambda i: (0, i, 0, 0))],
-        out_specs=pl.BlockSpec((8, 16, C), lambda i: (i, 0, 0)),
+        in_specs=[pl.BlockSpec((4, 16, 16, C), lambda i: (0, i, 0, 0))],
+        out_specs=pl.BlockSpec((16, 16, C), lambda i: (i, 0, 0)),
         compiler_params=params(8),
+        cost_estimate=busy(),
         name="added",
     )(pieces)
 
@@ -570,6 +597,25 @@
     for k in range(1, pieces.shape[0]):
         total = total + pieces[k].astype(F32)
     return total
+
+
+EVERY = ("x_hi", "y", "core", "x_lo", "z")
+
+
+def groups_of(*axes_of_core):
+    devices = np.arange(256).reshape(2, 4, 2, 2, 8)
+    found = []
+    for core, axes in enumerate(axes_of_core):
+        inner = [("x_hi", "y", "x_lo", "z").index(axis) for axis in axes]
+        outer = [axis for axis in range(4) if axis not in inner]
+        here = devices[:, :, core].transpose(outer + inner)
+        size = math.prod(here.shape[len(outer) :])
+        found += here.reshape(-1, size).tolist()
+    return found
+
+
+FIRST = groups_of(("y",), ("x_hi", "x_lo"))
+SECOND = groups_of(("x_hi", "x_lo", "z"), ("y", "z"))
 
 
 def body(
@@ -610,15 +656,16 @@
         head_weight,
     )
     got = lax.ppermute(send, "core", [(0, 1), (1, 0)])
+    out_next, out_prev = outside_call(part_conv, conv)
+    got, out_next, out_prev = lax.optimization_barrier((got, out_next, out_prev))
     held = pair_call(keep, got)
-    held = lax.all_to_all(held, ("x_hi", "y"), 0, 0, tiled=True)
-    out_next, out_prev = outside_call(part_conv, conv)
+    held = lax.all_to_all(held, EVERY, 0, 0, axis_index_groups=FIRST, tiled=True)
     prev = lax.ppermute(out_next, belt, RING)
     following = lax.ppermute(out_prev, belt, BACK)
     held, prev, following = lax.optimization_barrier((held, prev, following))
     held = added_call(held)
     grad_fields = fields_call(*seams, part_conv, out_next, prev, following, conv)
-    held = lax.all_to_all(held, belt, 0, 0, tiled=True)
+    held = lax.all_to_all(held, EVERY, 0, 0, axis_index_groups=SECOND, tiled=True)
     held = added(held).astype(BF)
     held, grad_fields = lax.optimization_barrier((held, grad_fields))
     whole = jnp.broadcast_to(held[None], (16, 16, C))

time: 88 us -> 84.9 us (0.965)
  blocking collectives: 15.4 us -> 12.9 us
  waiting for transfers between devices: 17.5 us -> 15.5 us
    ppermute x1, waiting for transfers between devices: 2.5 us -> 0.01 us  [body(): got = lax.ppermute(send, 'core', [(0, 1), (1, 0)])]
    all_to_all x1, blocking collectives: 15.4 us -> 12.9 us  [body(): whole = lax.all_to_all(whole, dp, 0, 0, tiled=True)]
    ppermute x1, starting transfers between devices: 1.09 us -> 2.2 us  [body(): following = lax.ppermute(out_prev, belt, BACK)]
    unnamed x20 -> x24, local copies, waits for them, and re-layouts: 4.65 us -> 5.32 us
  transfers between devices with their start and end apart: 7 -> 7, of which waited for: 5 -> 4; matrix products, arithmetic and copies ran while one was open for 0% -> 0% of each run, Pallas kernels for 13% -> 13%
where the time goes in v5:
time: 84.9 us; the launch traced here: 84.5 us
  Pallas kernels  29.7 us (35%)
  starting transfers between devices  20.3 us (24%)
  waiting for transfers between devices  15.5 us (18%)
  blocking collectives  12.9 us (15%)
  local copies, waits for them, and re-layouts  5.33 us (6%)
    pallas_call x1, Pallas kernels, main_call(): pl.pallas_call(main_kernel, out_shape=(shape((CELLS, C), F32), shape((STE...  15.1 us
    all_to_all x1, blocking collectives, body(): whole = lax.all_to_all(whole, dp, 0, 0, tiled=True)  12.9 us
    all_to_all x1, waiting for transfers between devices, body(): lax.all_to_all(held, EVERY, 0, 0, axis_index_groups=SECOND, tiled=True)  6.53 us
    all_to_all x1, starting transfers between devices, body(): lax.all_to_all(held, EVERY, 0, 0, axis_index_groups=SECOND, tiled=True)  5.76 us
    unnamed x24, local copies, waits for them, and re-layouts  5.32 us
    pallas_call x1, Pallas kernels, early_call(): pl.pallas_call(early_kernel, out_shape=shape(raw, F32), in_specs=[anywher...  5.3 us
    ppermute x1, starting transfers between devices, body(): following = lax.ppermute(to_prev, belt, BACK)  4.96 us
    pallas_call x1, Pallas kernels, fields_call(): pl.pallas_call(fields_kernel, out_shape=shape((STEPS, SIDE, SIDE, C)), in...  4.26 us
  transfers between devices with their start and end apart: 7, of which 4 were waited for; matrix products, arithmetic and copies ran while one was open for 0% of the time, Pallas kernels for 13%

profile of v5, /device:TPU:1, one launch (start us, length us, event | category | flops | bytes accessed | tf_op | source)
XLA Modules:
  0.0 84.5 jit_solution(13349784770325424366)
XLA Ops:
  0.6 1.2 %copy-done = bf16[1,1,2,32,32,256]{5,4,3,2,1,0:T(8,128)(2,1)S(1)} copy-done((bf16[1,1,2,32,32,256]{5,4,3,2,1,0:T(8,128)(2,1)S(1)}, bf16[1,1,2,32,32,256]{5,4,3,2,1,0:T(8,128)(2,1)}, u32[]{:S(2)}) %copy-start) | copy-done | bytes 1048600
  2.0 2.5 %collective-permute-start = (bf16[2,3,32,256]{3,2,1,0:T(8,128)(2,1)S(1)}, bf16[2,3,32,256]{3,2,1,0:T(8,128)(2,1)S(1)}, u32[]{:S(2)}, u32[]{:S(2)}) collective-permute-start(bf16[2,3,32,256]{3,2,1,0:T(8,128)(2,1)S(1)} %get-tuple-element.28), channel_id=1, source_target_pairs={{0,1},{1,2},{2,3},{3,4},{4,5},{5,6},{6,7},{7,8},{8,9},{9,10},{10,1... | collective-permute-start | bytes 294920 | tf_op jit(solution)/shard_map/ppermute | solution.py:640
  4.5 5.0 %collective-permute-start.1 = (bf16[2,3,32,256]{3,2,1,0:T(8,128)(2,1)S(1)}, bf16[2,3,32,256]{3,2,1,0:T(8,128)(2,1)S(1)}, u32[]{:S(2)}, u32[]{:S(2)}) collective-permute-start(bf16[2,3,32,256]{3,2,1,0:T(8,128)(2,1)S(1)} %get-tuple-element.29), channel_id=1, source_target_pairs={{1,0},{2,1},{3,2},{4,3},{5,4},{6,5},{7,6},{8,7},{9,8},{10,9},{11,1... | collective-permute-start | bytes 294920 | tf_op jit(solution)/shard_map/ppermute | solution.py:641
  9.5 5.3 %early.1 = f32[2,1024,256]{2,1,0:T(8,128)} custom-call(bf16[2,32,32,256]{3,2,1,0:T(8,128)(2,1)} %bitcast.100, bf16[2304,256]{1,0:T(8,128)(2,1)} %bitcast.103), custom_call_target="tpu_custom_call" | custom-call | flops 2415919104 | bytes 5242880 | tf_op jit(solution)/shard_map/early/pallas_call | solution.py:451
  14.8 0.6 copy-done.10
  15.5 15.1 %steps.1 = (f32[1024,256]{1,0:T(8,128)}, bf16[2,1024,256]{2,1,0:T(8,128)(2,1)}, bf16[4,32,16,256]{3,2,1,0:T(8,128)(2,1)}, bf16[4,32,16,256]{3,2,1,0:T(8,128)(2,1)}) custom-call(s32[4,16]{1,0:T(4,128)} %bitcast.107, s32[4,16]{1,0:T(4,128)} %bitcast.109, bf16[2,32,32,256]{3,2,1,0:T(8,128)(2,1)} %bitcast.101, bf16[2,3,32,256]{3,2,1,0:T(8,128)(2,1)} %copy-done.10, ...), custom_call_target="tpu_custom_call" | custom-call | tf_op jit(solution)/shard_map/steps/pallas_call | solution.py:473
  30.5 1.1 %collective-permute-start.2 = (bf16[4,32,16,256]{3,2,1,0:T(8,128)(2,1)}, bf16[4,32,16,256]{3,2,1,0:T(8,128)(2,1)S(1)}, u32[]{:S(2)}, u32[]{:S(2)}) collective-permute-start(bf16[4,32,16,256]{3,2,1,0:T(8,128)(2,1)} %get-tuple-element.31), channel_id=1, source_target_pairs={{0,16},{16,0},{1,17},{17,1},{2,18},{18,2},{3,19},{19,3},{4,20},{20... | collective-permute-start | bytes 3145736 | tf_op jit(solution)/shard_map/ppermute | solution.py:658
  31.6 1.2 %copy-done.4 = bf16[2,1024,256]{2,1,0:T(8,128)(2,1)S(1)} copy-done((bf16[2,1024,256]{2,1,0:T(8,128)(2,1)S(1)}, bf16[2,1024,256]{2,1,0:T(8,128)(2,1)}, u32[]{:S(2)}) %copy-start.4) | copy-done | bytes 1048600
  32.8 1.7 %outside.1 = (bf16[2,3,32,256]{3,2,1,0:T(8,128)(2,1)S(1)}, bf16[2,3,32,256]{3,2,1,0:T(8,128)(2,1)S(1)}) custom-call(bf16[2,1024,256]{2,1,0:T(8,128)(2,1)S(1)} %copy-done.4, bf16[2304,256]{1,0:T(8,128)(2,1)S(1)} %bitcast.105), custom_call_target="tpu_custom_call" | custom-call | flops 1073741824 | bytes 3145728 | tf_op jit(solution)/shard_map/outside/pallas_call | solution.py:503
  34.6 0.7 copy-done.9
  35.3 1.6 %pair.1 = bf16[4,32,16,256]{3,2,1,0:T(8,128)(2,1)} custom-call(bf16[4,32,16,256]{3,2,1,0:T(8,128)(2,1)S(1)} %copy-done.6, bf16[4,32,16,256]{3,2,1,0:T(8,128)(2,1)S(1)} %collective-permute-done.2.right_ref), custom_call_target="tpu_custom_call" | custom-call | flops 8589934592 | bytes 65536 | tf_op jit(solution)/shard_map/pair/pallas_call | solution.py:520
  36.9 3.7 %all-to-all-start = ((bf16[4,32,16,256]{3,2,1,0:T(8,128)(2,1)}), bf16[4,32,16,256]{3,2,1,0:T(8,128)(2,1)S(1)}, u32[]{:S(2)}, u32[]{:S(2)}) async-start(bf16[4,32,16,256]{3,2,1,0:T(8,128)(2,1)} %pair.1), calls=%async_computation | async-start | bytes 2097152 | tf_op jit(solution)/shard_map/all_to_all | solution.py:662
  40.6 2.2 %collective-permute-start.4 = (bf16[2,3,32,256]{3,2,1,0:T(8,128)(2,1)}, bf16[2,3,32,256]{3,2,1,0:T(8,128)(2,1)S(1)}, u32[]{:S(2)}, u32[]{:S(2)}) collective-permute-start(bf16[2,3,32,256]{3,2,1,0:T(8,128)(2,1)} %copy-done.9), channel_id=1, source_target_pairs={{1,0},{2,1},{3,2},{4,3},{5,4},{6,5},{7,6},{8,7},{9,8},{10,9},{11,1... | collective-permute-start | bytes 294920 | tf_op jit(solution)/shard_map/ppermute | solution.py:664
  42.8 2.2 %collective-permute-done.4.next_ref = bf16[2,3,32,256]{3,2,1,0:T(8,128)(2,1)S(1)} collective-permute-done((bf16[2,3,32,256]{3,2,1,0:T(8,128)(2,1)}, bf16[2,3,32,256]{3,2,1,0:T(8,128)(2,1)S(1)}, u32[]{:S(2)}, u32[]{:S(2)}) %collective-permute-start.4) | collective-permute-done | bytes 98336 | tf_op jit(solution)/shard_map/ppermute | solution.py:664
  45.0 3.5 %collective-permute-done.3.prev_ref = bf16[2,3,32,256]{3,2,1,0:T(8,128)(2,1)S(1)} collective-permute-done((bf16[2,3,32,256]{3,2,1,0:T(8,128)(2,1)S(1)}, bf16[2,3,32,256]{3,2,1,0:T(8,128)(2,1)S(1)}, u32[]{:S(2)}, u32[]{:S(2)}) %collective-permute-start.3) | collective-permute-done | bytes 98336 | tf_op jit(solution)/shard_map/ppermute | solution.py:663
  48.5 0.6 copy-done.7
  49.2 3.3 %all-to-all-done.pieces_ref = bf16[4,32,16,256]{3,2,1,0:T(8,128)(2,1)S(1)} async-done(((bf16[4,32,16,256]{3,2,1,0:T(8,128)(2,1)}), bf16[4,32,16,256]{3,2,1,0:T(8,128)(2,1)S(1)}, u32[]{:S(2)}, u32[]{:S(2)}) %all-to-all-start) | async-done | bytes 1048608 | tf_op jit(solution)/shard_map/all_to_all | solution.py:662
  52.5 0.9 %added.1 = bf16[32,16,256]{2,1,0:T(8,128)(2,1)} custom-call(bf16[4,32,16,256]{3,2,1,0:T(8,128)(2,1)S(1)} %all-to-all-done.pieces_ref), custom_call_target="tpu_custom_call" | custom-call | flops 8589934592 | bytes 65536 | tf_op jit(solution)/shard_map/added/pallas_call | solution.py:540
  53.4 5.8 %all-to-all-start.1 = ((bf16[32,16,256]{2,1,0:T(8,128)(2,1)}), bf16[32,16,256]{2,1,0:T(8,128)(2,1)S(1)}, u32[]{:S(2)}, u32[]{:S(2)}) async-start(bf16[32,16,256]{2,1,0:T(8,128)(2,1)} %added.1), calls=%async_computation.1 | async-start | bytes 524288 | tf_op jit(solution)/shard_map/all_to_all | solution.py:668
  59.2 0.9 %copy-done.8 = bf16[2,3,32,256]{3,2,1,0:T(8,128)(2,1)S(1)} copy-done((bf16[2,3,32,256]{3,2,1,0:T(8,128)(2,1)S(1)}, bf16[2,3,32,256]{3,2,1,0:T(8,128)(2,1)}, u32[]{:S(2)}) %copy-start.8) | copy-done | bytes 98328
  60.1 4.3 %fields.1 = bf16[2,32,32,256]{3,2,1,0:T(8,128)(2,1)} custom-call(s32[4,16]{1,0:T(4,128)S(1)} %bitcast.108, s32[4,16]{1,0:T(4,128)S(1)} %bitcast.110, bf16[2,1024,256]{2,1,0:T(8,128)(2,1)S(1)} %copy-done.5, bf16[2,3,32,256]{3,2,1,0:T(8,128)(2,1)S(1)} %get-tuple-element.36.own_ref, bf16[2,3,32,256]{3,2,1,0:T(8,128)(2,1)S(1)} %copy-done.8, ...), custom_call_target="tpu_custom_call" | custom-call | flops 2415919104 | bytes 4194304 | tf_op jit(solution)/shard_map/fields/pallas_call | solution.py:553
  64.3 6.5 %all-to-all-done.1 = bf16[32,16,256]{2,1,0:T(8,128)(2,1)S(1)} async-done(((bf16[32,16,256]{2,1,0:T(8,128)(2,1)}), bf16[32,16,256]{2,1,0:T(8,128)(2,1)S(1)}, u32[]{:S(2)}, u32[]{:S(2)}) %all-to-all-start.1) | async-done | bytes 262176 | tf_op jit(solution)/shard_map/all_to_all | solution.py:668
  70.9 12.9 %all_to_all.15.whole_ref = bf16[16,16,256]{2,1,0:T(8,128)(2,1)S(1)} all-to-all(bf16[16,16,256]{2,1,0:T(8,128)(2,1)S(1)} %broadcast_in_dim.10), channel_id=1, replica_groups=mesh['x_hi'=2,'y'=4,'core'=2,'x_lo'=2,'z'=8] {'x_hi','y','core'}, dimensions={0} | all-to-all | bytes 262144 | tf_op jit(solution)/shard_map/all_to_all | solution.py:672
  83.8 0.7 finish.1
  (25 shorter events, 0.2 us)
Async XLA Ops:
  0.6 1.2 %copy-start = (bf16[1,1,2,32,32,256]{5,4,3,2,1,0:T(8,128)(2,1)S(1)}, bf16[1,1,2,32,32,256]{5,4,3,2,1,0:T(8,128)(2,1)}, u32[]{:S(2)}) copy-start(bf16[1,1,2,32,32,256]{5,4,3,2,1,0:T(8,128)(2,1)} %param.11) | copy-start | bytes 3145732
  2.0 12.8 %collective-permute-start = (bf16[2,3,32,256]{3,2,1,0:T(8,128)(2,1)S(1)}, bf16[2,3,32,256]{3,2,1,0:T(8,128)(2,1)S(1)}, u32[]{:S(2)}, u32[]{:S(2)}) collective-permute-start(bf16[2,3,32,256]{3,2,1,0:T(8,128)(2,1)S(1)} %get-tuple-element.28), channel_id=1, source_target_pairs={{0,1},{1,2},{2,3},{3,4},{4,5},{5,6},{6,7},{7,8},{8,9},{9,10},{10,1... | collective-permute-start | bytes 294920 | tf_op jit(solution)/shard_map/ppermute | solution.py:640
  4.5 10.3 %collective-permute-start.1 = (bf16[2,3,32,256]{3,2,1,0:T(8,128)(2,1)S(1)}, bf16[2,3,32,256]{3,2,1,0:T(8,128)(2,1)S(1)}, u32[]{:S(2)}, u32[]{:S(2)}) collective-permute-start(bf16[2,3,32,256]{3,2,1,0:T(8,128)(2,1)S(1)} %get-tuple-element.29), channel_id=1, source_target_pairs={{1,0},{2,1},{3,2},{4,3},{5,4},{6,5},{7,6},{8,7},{9,8},{10,9},{11,1... | collective-permute-start | bytes 294920 | tf_op jit(solution)/shard_map/ppermute | solution.py:641
  14.8 0.6 copy-start.10
  14.8 0.7 copy-start.11
  15.5 16.2 %copy-start.1 = (bf16[9,256,256]{2,1,0:T(8,128)(2,1)S(1)}, bf16[9,256,256]{2,1,0:T(8,128)(2,1)}, u32[]{:S(2)}) copy-start(bf16[9,256,256]{2,1,0:T(8,128)(2,1)} %param.15) | copy-start | bytes 3538948
  30.5 4.7 %collective-permute-start.2 = (bf16[4,32,16,256]{3,2,1,0:T(8,128)(2,1)}, bf16[4,32,16,256]{3,2,1,0:T(8,128)(2,1)S(1)}, u32[]{:S(2)}, u32[]{:S(2)}) collective-permute-start(bf16[4,32,16,256]{3,2,1,0:T(8,128)(2,1)} %get-tuple-element.31), channel_id=1, source_target_pairs={{0,16},{16,0},{1,17},{17,1},{2,18},{18,2},{3,19},{19,3},{4,20},{20... | collective-permute-start | bytes 3145736 | tf_op jit(solution)/shard_map/ppermute | solution.py:658
  31.6 1.2 %copy-start.4 = (bf16[2,1024,256]{2,1,0:T(8,128)(2,1)S(1)}, bf16[2,1024,256]{2,1,0:T(8,128)(2,1)}, u32[]{:S(2)}) copy-start(bf16[2,1024,256]{2,1,0:T(8,128)(2,1)} %get-tuple-element.32.part_conv_ref) | copy-start | bytes 3145732
  32.8 2.4 %copy-start.6 = (bf16[4,32,16,256]{3,2,1,0:T(8,128)(2,1)S(1)}, bf16[4,32,16,256]{3,2,1,0:T(8,128)(2,1)}, u32[]{:S(2)}) copy-start(bf16[4,32,16,256]{3,2,1,0:T(8,128)(2,1)} %get-tuple-element.30.left_ref) | copy-start | bytes 3145732
  34.6 0.7 copy-start.9
  36.9 15.6 %all-to-all-start = ((bf16[4,32,16,256]{3,2,1,0:T(8,128)(2,1)}), bf16[4,32,16,256]{3,2,1,0:T(8,128)(2,1)S(1)}, u32[]{:S(2)}, u32[]{:S(2)}) async-start(bf16[4,32,16,256]{3,2,1,0:T(8,128)(2,1)} %pair.1), calls=%async_computation | async-start | bytes 2097152 | tf_op jit(solution)/shard_map/all_to_all | solution.py:662
  40.6 18.5 %copy-start.2 = (s32[16,4]{0,1:T(4,128)S(1)}, s32[16,4]{0,1:T(4,128)}, u32[]{:S(2)}) copy-start(s32[16,4]{0,1:T(4,128)} %param.20) | copy-start | bytes 772
  40.6 18.5 %copy-start.3 = (s32[16,4]{0,1:T(4,128)S(1)}, s32[16,4]{0,1:T(4,128)}, u32[]{:S(2)}) copy-start(s32[16,4]{0,1:T(4,128)} %param.21) | copy-start | bytes 772
  40.6 18.5 %copy-start.5 = (bf16[2,1024,256]{2,1,0:T(8,128)(2,1)S(1)}, bf16[2,1024,256]{2,1,0:T(8,128)(2,1)}, u32[]{:S(2)}) copy-start(bf16[2,1024,256]{2,1,0:T(8,128)(2,1)} %get-tuple-element.32.part_conv_ref) | copy-start | bytes 3145732
  40.6 4.4 %collective-permute-start.4 = (bf16[2,3,32,256]{3,2,1,0:T(8,128)(2,1)}, bf16[2,3,32,256]{3,2,1,0:T(8,128)(2,1)S(1)}, u32[]{:S(2)}, u32[]{:S(2)}) collective-permute-start(bf16[2,3,32,256]{3,2,1,0:T(8,128)(2,1)} %copy-done.9), channel_id=1, source_target_pairs={{1,0},{2,1},{3,2},{4,3},{5,4},{6,5},{7,6},{8,7},{9,8},{10,9},{11,1... | collective-permute-start | bytes 294920 | tf_op jit(solution)/shard_map/ppermute | solution.py:664
  42.8 5.7 %collective-permute-start.3 = (bf16[2,3,32,256]{3,2,1,0:T(8,128)(2,1)S(1)}, bf16[2,3,32,256]{3,2,1,0:T(8,128)(2,1)S(1)}, u32[]{:S(2)}, u32[]{:S(2)}) collective-permute-start(bf16[2,3,32,256]{3,2,1,0:T(8,128)(2,1)S(1)} %get-tuple-element.36.own_ref), channel_id=1, source_target_pairs={{0,1},{1,2},{2,3},{3,4},{4,5},{5,6},{6,7},{7,8},{8,9},{9,10},{10,1... | collective-permute-start | bytes 294920 | tf_op jit(solution)/shard_map/ppermute | solution.py:663
  48.5 0.6 copy-start.7
  53.4 17.5 %all-to-all-start.1 = ((bf16[32,16,256]{2,1,0:T(8,128)(2,1)}), bf16[32,16,256]{2,1,0:T(8,128)(2,1)S(1)}, u32[]{:S(2)}, u32[]{:S(2)}) async-start(bf16[32,16,256]{2,1,0:T(8,128)(2,1)} %added.1), calls=%async_computation.1 | async-start | bytes 524288 | tf_op jit(solution)/shard_map/all_to_all | solution.py:668
  59.2 0.9 %copy-start.8 = (bf16[2,3,32,256]{3,2,1,0:T(8,128)(2,1)S(1)}, bf16[2,3,32,256]{3,2,1,0:T(8,128)(2,1)}, u32[]{:S(2)}) copy-start(bf16[2,3,32,256]{3,2,1,0:T(8,128)(2,1)} %copy-done.7) | copy-start | bytes 294916

commit v6 on v5

--- a/solution.py
+++ b/solution.py
@@ -328,34 +328,26 @@
 
 
 def outside_kernel(part_conv_ref, conv_ref, to_next_ref, to_prev_ref):
-    picks = []
-    row = iota((SIDE, CELLS), 0)
-    cell = iota((SIDE, CELLS), 1)
-    for col in (0, SIDE - 1):
-        for p in range(3):
-            at = row + 1 - p
-            picks.append(one_hot((cell == at * SIDE + col) & (at >= 0) & (at < SIDE)))
-    for line in (0, SIDE - 1):
-        for q in range(3):
-            at = row + 1 - q
-            picks.append(one_hot((cell == line * SIDE + at) & (at >= 0) & (at < SIDE)))
-    picks = jnp.concatenate(picks, axis=0)
-    taps = [0, 3, 6, 2, 5, 8, 0, 1, 2, 6, 7, 8]
+    lines = [[], [], [], []]
     for step in range(STEPS):
-        picked = mm(picks, part_conv_ref[step]).astype(BF)
-        outside = []
-        for side in range(4):
-            total = jnp.zeros((SIDE, C), F32)
-            for k in range(3 * side, 3 * side + 3):
-                total = total + mm_nt(
-                    picked[k * SIDE : (k + 1) * SIDE], conv_ref[taps[k] * C : (taps[k] + 1) * C, :]
-                )
-            outside.append(total.astype(BF))
-        to_next_ref[step, 0] = outside[1]
-        to_prev_ref[step, 0] = outside[0]
+        plane = part_conv_ref.at[step]
+        for side, line in enumerate((plane[0], plane[SIDE - 1], plane[:, 0], plane[:, SIDE - 1])):
+            lines[side].append(line_shifts(line.astype(F32)))
+    taps = ((2, 1, 0), (8, 7, 6), (6, 3, 0), (8, 5, 2))
+    outside = []
+    for side in range(4):
+        line = jnp.concatenate(lines[side], axis=0)
+        total = jnp.zeros((STEPS * SIDE, C), F32)
+        for k, tap in enumerate(taps[side]):
+            total = total + mm_nt(line[:, k * C : (k + 1) * C], conv_ref[pl.ds(tap * C, C), :])
+        outside.append(total.astype(BF))
+    for step in range(STEPS):
+        rows = slice(step * SIDE, (step + 1) * SIDE)
+        to_next_ref[step, 0] = outside[3][rows]
+        to_prev_ref[step, 0] = outside[2][rows]
         for ref in (to_next_ref, to_prev_ref):
-            ref[step, 1] = outside[2]
-            ref[step, 2] = outside[3]
+            ref[step, 1] = outside[0][rows]
+            ref[step, 2] = outside[1][rows]
 
 
 def fields_kernel(
@@ -423,10 +415,6 @@
     return pltpu.CompilerParams(vmem_limit_bytes=mebibytes << 20)
 
 
-def busy():
-    return pl.CostEstimate(flops=1 << 33, bytes_accessed=1 << 16, transcendentals=0)
-
-
 def shape(dims, kind=BF):
     return jax.ShapeDtypeStruct(dims, kind)
 
@@ -505,10 +493,10 @@
         out_shape=(shape(EDGE), shape(EDGE)),
         in_specs=[in_vmem()] * 2,
         out_specs=(in_vmem(), in_vmem()),
-        compiler_params=params(16),
+        compiler_params=params(),
         cost_estimate=pl.CostEstimate(flops=1 << 30, bytes_accessed=3 << 20, transcendentals=0),
         name="outside",
-    )(part_conv, conv)
+    )(part_conv.reshape(STEPS, SIDE, SIDE, C), conv)
 
 
 def pair_kernel(left_ref, right_ref, out_ref):
@@ -516,15 +504,12 @@
 
 
 def pair_call(left, right):
-    block = pl.BlockSpec((1, 32, 16, C), lambda i: (i, 0, 0, 0))
     return pl.pallas_call(
         pair_kernel,
         out_shape=shape(left.shape),
-        grid=(4,),
-        in_specs=[block, block],
-        out_specs=block,
+        in_specs=[in_vmem()] * 2,
+        out_specs=in_vmem(),
         compiler_params=params(8),
-        cost_estimate=busy(),
         name="pair",
     )(left, right)
 
@@ -540,11 +525,9 @@
     return pl.pallas_call(
         added_kernel,
         out_shape=shape((32, 16, C)),
-        grid=(2,),
-        in_specs=[pl.BlockSpec((4, 16, 16, C), lambda i: (0, i, 0, 0))],
-        out_specs=pl.BlockSpec((16, 16, C), lambda i: (i, 0, 0)),
+        in_specs=[in_vmem()],
+        out_specs=in_vmem(),
         compiler_params=params(8),
-        cost_estimate=busy(),
         name="added",
     )(pieces)
 

time: 84.9 us -> 83.7 us (0.986)
  local copies, waits for them, and re-layouts: 5.33 us -> 3.43 us
    unnamed x24 -> x22, local copies, waits for them, and re-layouts: 5.32 us -> 3.42 us
    pallas_call x1, Pallas kernels: 1.74 us -> 2.86 us  [outside_call(): pl.pallas_call(outside_kernel, out_shape=(shape(EDGE), shape(EDGE)), in_s...]
  transfers between devices with their start and end apart: 7 -> 7, of which waited for: 4 -> 4; matrix products, arithmetic and copies ran while one was open for 0% -> 0% of each run, Pallas kernels for 13% -> 15%
where the time goes in v6:
time: 83.7 us; the launch traced here: 83.3 us
  Pallas kernels  30.2 us (36%)
  starting transfers between devices  20.4 us (24%)
  waiting for transfers between devices  15.5 us (19%)
  blocking collectives  12.9 us (15%)
  local copies, waits for them, and re-layouts  3.43 us (4%)
    pallas_call x1, Pallas kernels, main_call(): pl.pallas_call(main_kernel, out_shape=(shape((CELLS, C), F32), shape((STE...  14.9 us
    all_to_all x1, blocking collectives, body(): whole = lax.all_to_all(whole, dp, 0, 0, tiled=True)  12.9 us
    all_to_all x1, waiting for transfers between devices, body(): lax.all_to_all(held, EVERY, 0, 0, axis_index_groups=SECOND, tiled=True)  6.49 us
    all_to_all x1, starting transfers between devices, body(): lax.all_to_all(held, EVERY, 0, 0, axis_index_groups=SECOND, tiled=True)  5.75 us
    pallas_call x1, Pallas kernels, early_call(): pl.pallas_call(early_kernel, out_shape=shape(raw, F32), in_specs=[anywher...  5.29 us
    ppermute x1, starting transfers between devices, body(): following = lax.ppermute(to_prev, belt, BACK)  4.96 us
    pallas_call x1, Pallas kernels, fields_call(): pl.pallas_call(fields_kernel, out_shape=shape((STEPS, SIDE, SIDE, C)), in...  4.26 us
    all_to_all x1, starting transfers between devices, body(): lax.all_to_all(held, EVERY, 0, 0, axis_index_groups=FIRST, tiled=True)  3.87 us
  transfers between devices with their start and end apart: 7, of which 4 were waited for; matrix products, arithmetic and copies ran while one was open for 0% of the time, Pallas kernels for 15%

profile of v6, /device:TPU:1, one launch (start us, length us, event | category | flops | bytes accessed | tf_op | source)
XLA Modules:
  0.0 83.3 jit_solution(3006779503887895596)
XLA Ops:
  0.6 1.2 %copy-done = bf16[1,1,2,32,32,256]{5,4,3,2,1,0:T(8,128)(2,1)S(1)} copy-done((bf16[1,1,2,32,32,256]{5,4,3,2,1,0:T(8,128)(2,1)S(1)}, bf16[1,1,2,32,32,256]{5,4,3,2,1,0:T(8,128)(2,1)}, u32[]{:S(2)}) %copy-start) | copy-done | bytes 1048600
  1.9 0.1 edges.1
  2.0 2.5 %collective-permute-start = (bf16[2,3,32,256]{3,2,1,0:T(8,128)(2,1)S(1)}, bf16[2,3,32,256]{3,2,1,0:T(8,128)(2,1)S(1)}, u32[]{:S(2)}, u32[]{:S(2)}) collective-permute-start(bf16[2,3,32,256]{3,2,1,0:T(8,128)(2,1)S(1)} %get-tuple-element.28), channel_id=1, source_target_pairs={{0,1},{1,2},{2,3},{3,4},{4,5},{5,6},{6,7},{7,8},{8,9},{9,10},{10,1... | collective-permute-start | bytes 294920 | tf_op jit(solution)/shard_map/ppermute | solution.py:623
  4.5 5.0 %collective-permute-start.1 = (bf16[2,3,32,256]{3,2,1,0:T(8,128)(2,1)S(1)}, bf16[2,3,32,256]{3,2,1,0:T(8,128)(2,1)S(1)}, u32[]{:S(2)}, u32[]{:S(2)}) collective-permute-start(bf16[2,3,32,256]{3,2,1,0:T(8,128)(2,1)S(1)} %get-tuple-element.29), channel_id=1, source_target_pairs={{1,0},{2,1},{3,2},{4,3},{5,4},{6,5},{7,6},{8,7},{9,8},{10,9},{11,1... | collective-permute-start | bytes 294920 | tf_op jit(solution)/shard_map/ppermute | solution.py:624
  9.5 5.3 %early.1 = f32[2,1024,256]{2,1,0:T(8,128)} custom-call(bf16[2,32,32,256]{3,2,1,0:T(8,128)(2,1)} %bitcast.101, bf16[2304,256]{1,0:T(8,128)(2,1)} %bitcast.104), custom_call_target="tpu_custom_call" | custom-call | flops 2415919104 | bytes 5242880 | tf_op jit(solution)/shard_map/early/pallas_call | solution.py:439
  14.8 0.6 copy-done.9
  15.4 14.9 %steps.1 = (f32[1024,256]{1,0:T(8,128)}, bf16[2,1024,256]{2,1,0:T(8,128)(2,1)}, bf16[4,32,16,256]{3,2,1,0:T(8,128)(2,1)}, bf16[4,32,16,256]{3,2,1,0:T(8,128)(2,1)}) custom-call(s32[4,16]{1,0:T(4,128)} %bitcast.108, s32[4,16]{1,0:T(4,128)} %bitcast.110, bf16[2,32,32,256]{3,2,1,0:T(8,128)(2,1)} %bitcast.102, bf16[2,3,32,256]{3,2,1,0:T(8,128)(2,1)} %copy-done.9, ...), custom_call_target="tpu_custom_call" | custom-call | tf_op jit(solution)/shard_map/steps/pallas_call | solution.py:461
  30.4 1.1 %collective-permute-start.2 = (bf16[4,32,16,256]{3,2,1,0:T(8,128)(2,1)}, bf16[4,32,16,256]{3,2,1,0:T(8,128)(2,1)S(1)}, u32[]{:S(2)}, u32[]{:S(2)}) collective-permute-start(bf16[4,32,16,256]{3,2,1,0:T(8,128)(2,1)} %get-tuple-element.31), channel_id=1, source_target_pairs={{0,16},{16,0},{1,17},{17,1},{2,18},{18,2},{3,19},{19,3},{4,20},{20... | collective-permute-start | bytes 3145736 | tf_op jit(solution)/shard_map/ppermute | solution.py:641
  31.5 2.9 %outside.1 = (bf16[2,3,32,256]{3,2,1,0:T(8,128)(2,1)}, bf16[2,3,32,256]{3,2,1,0:T(8,128)(2,1)}) custom-call(bf16[2,32,32,256]{3,2,1,0:T(8,128)(2,1)} %bitcast.112, bf16[2304,256]{1,0:T(8,128)(2,1)} %bitcast.106), custom_call_target="tpu_custom_call" | custom-call | flops 1073741824 | bytes 3145728 | tf_op jit(solution)/shard_map/outside/pallas_call | solution.py:491
  34.4 1.2 %pair.1 = bf16[4,32,16,256]{3,2,1,0:T(8,128)(2,1)} custom-call(bf16[4,32,16,256]{3,2,1,0:T(8,128)(2,1)S(1)} %copy-done.2, bf16[4,32,16,256]{3,2,1,0:T(8,128)(2,1)S(1)} %collective-permute-done.2.right_ref), custom_call_target="tpu_custom_call" | custom-call | tf_op jit(solution)/shard_map/pair/pallas_call | solution.py:507
  35.6 3.9 %all-to-all-start = ((bf16[4,32,16,256]{3,2,1,0:T(8,128)(2,1)}), bf16[4,32,16,256]{3,2,1,0:T(8,128)(2,1)S(1)}, u32[]{:S(2)}, u32[]{:S(2)}) async-start(bf16[4,32,16,256]{3,2,1,0:T(8,128)(2,1)} %pair.1), calls=%async_computation | async-start | bytes 2097152 | tf_op jit(solution)/shard_map/all_to_all | solution.py:645
  39.5 2.2 %collective-permute-start.4 = (bf16[2,3,32,256]{3,2,1,0:T(8,128)(2,1)}, bf16[2,3,32,256]{3,2,1,0:T(8,128)(2,1)S(1)}, u32[]{:S(2)}, u32[]{:S(2)}) collective-permute-start(bf16[2,3,32,256]{3,2,1,0:T(8,128)(2,1)} %get-tuple-element.37), channel_id=1, source_target_pairs={{1,0},{2,1},{3,2},{4,3},{5,4},{6,5},{7,6},{8,7},{9,8},{10,9},{11,1... | collective-permute-start | bytes 294920 | tf_op jit(solution)/shard_map/ppermute | solution.py:647
  41.7 2.2 %collective-permute-done.4.next_ref = bf16[2,3,32,256]{3,2,1,0:T(8,128)(2,1)S(1)} collective-permute-done((bf16[2,3,32,256]{3,2,1,0:T(8,128)(2,1)}, bf16[2,3,32,256]{3,2,1,0:T(8,128)(2,1)S(1)}, u32[]{:S(2)}, u32[]{:S(2)}) %collective-permute-start.4) | collective-permute-done | bytes 98336 | tf_op jit(solution)/shard_map/ppermute | solution.py:647
  43.9 3.7 %collective-permute-done.3.prev_ref = bf16[2,3,32,256]{3,2,1,0:T(8,128)(2,1)S(1)} collective-permute-done((bf16[2,3,32,256]{3,2,1,0:T(8,128)(2,1)S(1)}, bf16[2,3,32,256]{3,2,1,0:T(8,128)(2,1)S(1)}, u32[]{:S(2)}, u32[]{:S(2)}) %collective-permute-start.3) | collective-permute-done | bytes 98336 | tf_op jit(solution)/shard_map/ppermute | solution.py:646
  47.6 0.6 copy-done.7
  48.2 3.1 %all-to-all-done.pieces_ref = bf16[4,32,16,256]{3,2,1,0:T(8,128)(2,1)S(1)} async-done(((bf16[4,32,16,256]{3,2,1,0:T(8,128)(2,1)}), bf16[4,32,16,256]{3,2,1,0:T(8,128)(2,1)S(1)}, u32[]{:S(2)}, u32[]{:S(2)}) %all-to-all-start) | async-done | bytes 1048608 | tf_op jit(solution)/shard_map/all_to_all | solution.py:645
  51.3 0.8 added.1
  52.1 5.8 %all-to-all-start.1 = ((bf16[32,16,256]{2,1,0:T(8,128)(2,1)}), bf16[32,16,256]{2,1,0:T(8,128)(2,1)S(1)}, u32[]{:S(2)}, u32[]{:S(2)}) async-start(bf16[32,16,256]{2,1,0:T(8,128)(2,1)} %added.1), calls=%async_computation.1 | async-start | bytes 524288 | tf_op jit(solution)/shard_map/all_to_all | solution.py:651
  58.0 0.9 %copy-done.8 = bf16[2,3,32,256]{3,2,1,0:T(8,128)(2,1)S(1)} copy-done((bf16[2,3,32,256]{3,2,1,0:T(8,128)(2,1)S(1)}, bf16[2,3,32,256]{3,2,1,0:T(8,128)(2,1)}, u32[]{:S(2)}) %copy-start.8) | copy-done | bytes 98328
  58.8 4.3 %fields.1 = bf16[2,32,32,256]{3,2,1,0:T(8,128)(2,1)} custom-call(s32[4,16]{1,0:T(4,128)S(1)} %bitcast.109, s32[4,16]{1,0:T(4,128)S(1)} %bitcast.111, bf16[2,1024,256]{2,1,0:T(8,128)(2,1)S(1)} %copy-done.5, bf16[2,3,32,256]{3,2,1,0:T(8,128)(2,1)S(1)} %copy-done.6, bf16[2,3,32,256]{3,2,1,0:T(8,128)(2,1)S(1)} %copy-done.8, ...), custom_call_target="tpu_custom_call" | custom-call | flops 2415919104 | bytes 4194304 | tf_op jit(solution)/shard_map/fields/pallas_call | solution.py:536
  63.1 6.5 %all-to-all-done.1 = bf16[32,16,256]{2,1,0:T(8,128)(2,1)S(1)} async-done(((bf16[32,16,256]{2,1,0:T(8,128)(2,1)}), bf16[32,16,256]{2,1,0:T(8,128)(2,1)S(1)}, u32[]{:S(2)}, u32[]{:S(2)}) %all-to-all-start.1) | async-done | bytes 262176 | tf_op jit(solution)/shard_map/all_to_all | solution.py:651
  69.6 0.1 fusion
  69.7 12.9 %all_to_all.15.whole_ref = bf16[16,16,256]{2,1,0:T(8,128)(2,1)S(1)} all-to-all(bf16[16,16,256]{2,1,0:T(8,128)(2,1)S(1)} %broadcast_in_dim.10), channel_id=1, replica_groups=mesh['x_hi'=2,'y'=4,'core'=2,'x_lo'=2,'z'=8] {'x_hi','y','core'}, dimensions={0} | all-to-all | bytes 262144 | tf_op jit(solution)/shard_map/all_to_all | solution.py:655
  82.6 0.7 finish.1
  (23 shorter events, 0.1 us)
Async XLA Ops:
  0.6 1.2 %copy-start = (bf16[1,1,2,32,32,256]{5,4,3,2,1,0:T(8,128)(2,1)S(1)}, bf16[1,1,2,32,32,256]{5,4,3,2,1,0:T(8,128)(2,1)}, u32[]{:S(2)}) copy-start(bf16[1,1,2,32,32,256]{5,4,3,2,1,0:T(8,128)(2,1)} %param.11) | copy-start | bytes 3145732
  2.0 12.8 %collective-permute-start = (bf16[2,3,32,256]{3,2,1,0:T(8,128)(2,1)S(1)}, bf16[2,3,32,256]{3,2,1,0:T(8,128)(2,1)S(1)}, u32[]{:S(2)}, u32[]{:S(2)}) collective-permute-start(bf16[2,3,32,256]{3,2,1,0:T(8,128)(2,1)S(1)} %get-tuple-element.28), channel_id=1, source_target_pairs={{0,1},{1,2},{2,3},{3,4},{4,5},{5,6},{6,7},{7,8},{8,9},{9,10},{10,1... | collective-permute-start | bytes 294920 | tf_op jit(solution)/shard_map/ppermute | solution.py:623
  4.5 10.3 %collective-permute-start.1 = (bf16[2,3,32,256]{3,2,1,0:T(8,128)(2,1)S(1)}, bf16[2,3,32,256]{3,2,1,0:T(8,128)(2,1)S(1)}, u32[]{:S(2)}, u32[]{:S(2)}) collective-permute-start(bf16[2,3,32,256]{3,2,1,0:T(8,128)(2,1)S(1)} %get-tuple-element.29), channel_id=1, source_target_pairs={{1,0},{2,1},{3,2},{4,3},{5,4},{6,5},{7,6},{8,7},{9,8},{10,9},{11,1... | collective-permute-start | bytes 294920 | tf_op jit(solution)/shard_map/ppermute | solution.py:624
  14.8 0.6 copy-start.9
  14.8 0.6 copy-start.10
  30.4 3.9 %copy-start.2 = (bf16[4,32,16,256]{3,2,1,0:T(8,128)(2,1)S(1)}, bf16[4,32,16,256]{3,2,1,0:T(8,128)(2,1)}, u32[]{:S(2)}) copy-start(bf16[4,32,16,256]{3,2,1,0:T(8,128)(2,1)} %get-tuple-element.30.left_ref) | copy-start | bytes 3145732
  30.4 3.9 %collective-permute-start.2 = (bf16[4,32,16,256]{3,2,1,0:T(8,128)(2,1)}, bf16[4,32,16,256]{3,2,1,0:T(8,128)(2,1)S(1)}, u32[]{:S(2)}, u32[]{:S(2)}) collective-permute-start(bf16[4,32,16,256]{3,2,1,0:T(8,128)(2,1)} %get-tuple-element.31), channel_id=1, source_target_pairs={{0,16},{16,0},{1,17},{17,1},{2,18},{18,2},{3,19},{19,3},{4,20},{20... | collective-permute-start | bytes 3145736 | tf_op jit(solution)/shard_map/ppermute | solution.py:641
  34.3 7.3 %copy-start.6 = (bf16[2,3,32,256]{3,2,1,0:T(8,128)(2,1)S(1)}, bf16[2,3,32,256]{3,2,1,0:T(8,128)(2,1)}, u32[]{:S(2)}) copy-start(bf16[2,3,32,256]{3,2,1,0:T(8,128)(2,1)} %get-tuple-element.36.own_ref) | copy-start | bytes 294916
  35.6 22.3 %copy-start.1 = (bf16[9,256,256]{2,1,0:T(8,128)(2,1)S(1)}, bf16[9,256,256]{2,1,0:T(8,128)(2,1)}, u32[]{:S(2)}) copy-start(bf16[9,256,256]{2,1,0:T(8,128)(2,1)} %param.15) | copy-start | bytes 3538948
  35.6 22.3 %copy-start.3 = (s32[16,4]{0,1:T(4,128)S(1)}, s32[16,4]{0,1:T(4,128)}, u32[]{:S(2)}) copy-start(s32[16,4]{0,1:T(4,128)} %param.20) | copy-start | bytes 772
  35.6 22.3 %copy-start.4 = (s32[16,4]{0,1:T(4,128)S(1)}, s32[16,4]{0,1:T(4,128)}, u32[]{:S(2)}) copy-start(s32[16,4]{0,1:T(4,128)} %param.21) | copy-start | bytes 772
  35.6 22.3 %copy-start.5 = (bf16[2,1024,256]{2,1,0:T(8,128)(2,1)S(1)}, bf16[2,1024,256]{2,1,0:T(8,128)(2,1)}, u32[]{:S(2)}) copy-start(bf16[2,1024,256]{2,1,0:T(8,128)(2,1)} %get-tuple-element.32.part_conv_ref) | copy-start | bytes 3145732
  35.6 15.7 %all-to-all-start = ((bf16[4,32,16,256]{3,2,1,0:T(8,128)(2,1)}), bf16[4,32,16,256]{3,2,1,0:T(8,128)(2,1)S(1)}, u32[]{:S(2)}, u32[]{:S(2)}) async-start(bf16[4,32,16,256]{3,2,1,0:T(8,128)(2,1)} %pair.1), calls=%async_computation | async-start | bytes 2097152 | tf_op jit(solution)/shard_map/all_to_all | solution.py:645
  39.5 4.4 %collective-permute-start.4 = (bf16[2,3,32,256]{3,2,1,0:T(8,128)(2,1)}, bf16[2,3,32,256]{3,2,1,0:T(8,128)(2,1)S(1)}, u32[]{:S(2)}, u32[]{:S(2)}) collective-permute-start(bf16[2,3,32,256]{3,2,1,0:T(8,128)(2,1)} %get-tuple-element.37), channel_id=1, source_target_pairs={{1,0},{2,1},{3,2},{4,3},{5,4},{6,5},{7,6},{8,7},{9,8},{10,9},{11,1... | collective-permute-start | bytes 294920 | tf_op jit(solution)/shard_map/ppermute | solution.py:647
  41.7 5.9 %collective-permute-start.3 = (bf16[2,3,32,256]{3,2,1,0:T(8,128)(2,1)S(1)}, bf16[2,3,32,256]{3,2,1,0:T(8,128)(2,1)S(1)}, u32[]{:S(2)}, u32[]{:S(2)}) collective-permute-start(bf16[2,3,32,256]{3,2,1,0:T(8,128)(2,1)S(1)} %copy-done.6), channel_id=1, source_target_pairs={{0,1},{1,2},{2,3},{3,4},{4,5},{5,6},{6,7},{7,8},{8,9},{9,10},{10,1... | collective-permute-start | bytes 294920 | tf_op jit(solution)/shard_map/ppermute | solution.py:646
  47.6 0.6 copy-start.7
  52.1 17.5 %all-to-all-start.1 = ((bf16[32,16,256]{2,1,0:T(8,128)(2,1)}), bf16[32,16,256]{2,1,0:T(8,128)(2,1)S(1)}, u32[]{:S(2)}, u32[]{:S(2)}) async-start(bf16[32,16,256]{2,1,0:T(8,128)(2,1)} %added.1), calls=%async_computation.1 | async-start | bytes 524288 | tf_op jit(solution)/shard_map/all_to_all | solution.py:651
  58.0 0.9 %copy-start.8 = (bf16[2,3,32,256]{3,2,1,0:T(8,128)(2,1)S(1)}, bf16[2,3,32,256]{3,2,1,0:T(8,128)(2,1)}, u32[]{:S(2)}) copy-start(bf16[2,3,32,256]{3,2,1,0:T(8,128)(2,1)} %copy-done.7) | copy-start | bytes 294916

commit v7 on v6

--- a/solution.py
+++ b/solution.py
@@ -499,8 +499,14 @@
     )(part_conv.reshape(STEPS, SIDE, SIDE, C), conv)
 
 
-def pair_kernel(left_ref, right_ref, out_ref):
-    out_ref[...] = (left_ref[...].astype(F32) + right_ref[...].astype(F32)).astype(BF)
+def pair_kernel(left_ref, right_ref, out, out_ref, sems):
+    stores = []
+    for k in range(left_ref.shape[0]):
+        out_ref[k] = (left_ref[k].astype(F32) + right_ref[k].astype(F32)).astype(BF)
+        stores.append(pltpu.make_async_copy(out_ref.at[k], out.at[k], sems.at[k]))
+        stores[k].start()
+    for store in stores:
+        store.wait()
 
 
 def pair_call(left, right):
@@ -508,7 +514,11 @@
         pair_kernel,
         out_shape=shape(left.shape),
         in_specs=[in_vmem()] * 2,
-        out_specs=in_vmem(),
+        out_specs=pl.BlockSpec(memory_space=pl.ANY),
+        scratch_shapes=[
+            pltpu.VMEM(left.shape, BF),
+            pltpu.SemaphoreType.DMA((left.shape[0],)),
+        ],
         compiler_params=params(8),
         name="pair",
     )(left, right)
@@ -647,12 +657,13 @@
     following = lax.ppermute(out_prev, belt, BACK)
     held, prev, following = lax.optimization_barrier((held, prev, following))
     held = added_call(held)
+    held = lax.all_to_all(held, EVERY, 0, 0, axis_index_groups=SECOND, tiled=True)
+    held, prev, following = lax.optimization_barrier((held, prev, following))
+    held = added(held).astype(BF)
     grad_fields = fields_call(*seams, part_conv, out_next, prev, following, conv)
-    held = lax.all_to_all(held, EVERY, 0, 0, axis_index_groups=SECOND, tiled=True)
-    held = added(held).astype(BF)
-    held, grad_fields = lax.optimization_barrier((held, grad_fields))
     whole = jnp.broadcast_to(held[None], (16, 16, C))
     whole = lax.all_to_all(whole, dp, 0, 0, tiled=True)
+    whole, grad_fields = lax.optimization_barrier((whole, grad_fields))
     grad_conv, grad_update, grad_reset, grad_candidate, grad_head = finish_call(whole)
     return (
         grad_fields[None, None],

time: 83.7 us -> 83.6 us (level)
  blocking collectives: 12.9 us -> 17.3 us
  waiting for transfers between devices: 15.5 us -> 11.5 us
    all_to_all x1, blocking collectives: 12.9 us -> 17.3 us  [body(): lax.all_to_all(held, EVERY, 0, 0, axis_index_groups=SECOND, tiled=True)]
    all_to_all x1, waiting for transfers between devices: 6.49 us -> 2.46 us  [body(): whole = lax.all_to_all(whole, dp, 0, 0, tiled=True)]
where the time goes in v7:
time: 83.6 us; the launch traced here: 83.1 us
  Pallas kernels  29.4 us (35%)
  starting transfers between devices  20.1 us (24%)
  blocking collectives  17.3 us (21%)
  waiting for transfers between devices  11.5 us (14%)
  local copies, waits for them, and re-layouts  4.09 us (5%)
    all_to_all x1, blocking collectives, body(): lax.all_to_all(held, EVERY, 0, 0, axis_index_groups=SECOND, tiled=True)  17.3 us
    pallas_call x1, Pallas kernels, main_call(): pl.pallas_call(main_kernel, out_shape=(shape((CELLS, C), F32), shape((STE...  14.9 us
    all_to_all x1, starting transfers between devices, body(): whole = lax.all_to_all(whole, dp, 0, 0, tiled=True)  5.45 us
    pallas_call x1, Pallas kernels, early_call(): pl.pallas_call(early_kernel, out_shape=shape(raw, F32), in_specs=[anywher...  5.29 us
    ppermute x1, starting transfers between devices, body(): following = lax.ppermute(to_prev, belt, BACK)  4.96 us
    pallas_call x1, Pallas kernels, fields_call(): pl.pallas_call(fields_kernel, out_shape=shape((STEPS, SIDE, SIDE, C)), in...  4.26 us
    all_to_all x1, starting transfers between devices, body(): lax.all_to_all(held, EVERY, 0, 0, axis_index_groups=FIRST, tiled=True)  3.87 us
    ppermute x1, waiting for transfers between devices, body(): prev = lax.ppermute(out_next, belt, RING)  3.68 us
  transfers between devices with their start and end apart: 7, of which 4 were waited for; matrix products, arithmetic and copies ran while one was open for 0% of the time, Pallas kernels for 15%

profile of v7, /device:TPU:1, one launch (start us, length us, event | category | flops | bytes accessed | tf_op | source)
XLA Modules:
  0.0 83.1 jit_solution(12711347960498748521)
XLA Ops:
  0.6 1.2 %copy-done = bf16[1,1,2,32,32,256]{5,4,3,2,1,0:T(8,128)(2,1)S(1)} copy-done((bf16[1,1,2,32,32,256]{5,4,3,2,1,0:T(8,128)(2,1)S(1)}, bf16[1,1,2,32,32,256]{5,4,3,2,1,0:T(8,128)(2,1)}, u32[]{:S(2)}) %copy-start) | copy-done | bytes 1048600
  1.9 0.1 edges.1
  2.0 2.5 %collective-permute-start = (bf16[2,3,32,256]{3,2,1,0:T(8,128)(2,1)S(1)}, bf16[2,3,32,256]{3,2,1,0:T(8,128)(2,1)S(1)}, u32[]{:S(2)}, u32[]{:S(2)}) collective-permute-start(bf16[2,3,32,256]{3,2,1,0:T(8,128)(2,1)S(1)} %get-tuple-element.31), channel_id=1, source_target_pairs={{0,1},{1,2},{2,3},{3,4},{4,5},{5,6},{6,7},{7,8},{8,9},{9,10},{10,1... | collective-permute-start | bytes 294920 | tf_op jit(solution)/shard_map/ppermute | solution.py:633
  4.5 5.0 %collective-permute-start.1 = (bf16[2,3,32,256]{3,2,1,0:T(8,128)(2,1)S(1)}, bf16[2,3,32,256]{3,2,1,0:T(8,128)(2,1)S(1)}, u32[]{:S(2)}, u32[]{:S(2)}) collective-permute-start(bf16[2,3,32,256]{3,2,1,0:T(8,128)(2,1)S(1)} %get-tuple-element.32), channel_id=1, source_target_pairs={{1,0},{2,1},{3,2},{4,3},{5,4},{6,5},{7,6},{8,7},{9,8},{10,9},{11,1... | collective-permute-start | bytes 294920 | tf_op jit(solution)/shard_map/ppermute | solution.py:634
  9.5 5.3 %early.1 = f32[2,1024,256]{2,1,0:T(8,128)} custom-call(bf16[2,32,32,256]{3,2,1,0:T(8,128)(2,1)} %bitcast.16, bf16[2304,256]{1,0:T(8,128)(2,1)} %bitcast.19), custom_call_target="tpu_custom_call" | custom-call | flops 2415919104 | bytes 5242880 | tf_op jit(solution)/shard_map/early/pallas_call | solution.py:439
  14.8 0.6 copy-done.9
  15.4 14.9 %steps.1 = (f32[1024,256]{1,0:T(8,128)}, bf16[2,1024,256]{2,1,0:T(8,128)(2,1)}, bf16[4,32,16,256]{3,2,1,0:T(8,128)(2,1)}, bf16[4,32,16,256]{3,2,1,0:T(8,128)(2,1)}) custom-call(s32[4,16]{1,0:T(4,128)} %bitcast.23, s32[4,16]{1,0:T(4,128)} %bitcast.25, bf16[2,32,32,256]{3,2,1,0:T(8,128)(2,1)} %bitcast.17, bf16[2,3,32,256]{3,2,1,0:T(8,128)(2,1)} %copy-done.9, ...), custom_call_target="tpu_custom_call" | custom-call | tf_op jit(solution)/shard_map/steps/pallas_call | solution.py:461
  30.4 1.1 %collective-permute-start.2 = (bf16[4,32,16,256]{3,2,1,0:T(8,128)(2,1)}, bf16[4,32,16,256]{3,2,1,0:T(8,128)(2,1)S(1)}, u32[]{:S(2)}, u32[]{:S(2)}) collective-permute-start(bf16[4,32,16,256]{3,2,1,0:T(8,128)(2,1)} %get-tuple-element.34), channel_id=1, source_target_pairs={{0,16},{16,0},{1,17},{17,1},{2,18},{18,2},{3,19},{19,3},{4,20},{20... | collective-permute-start | bytes 3145736 | tf_op jit(solution)/shard_map/ppermute | solution.py:651
  31.5 2.9 %outside.1 = (bf16[2,3,32,256]{3,2,1,0:T(8,128)(2,1)}, bf16[2,3,32,256]{3,2,1,0:T(8,128)(2,1)}) custom-call(bf16[2,32,32,256]{3,2,1,0:T(8,128)(2,1)} %bitcast.27, bf16[2304,256]{1,0:T(8,128)(2,1)} %bitcast.21), custom_call_target="tpu_custom_call" | custom-call | flops 1073741824 | bytes 3145728 | tf_op jit(solution)/shard_map/outside/pallas_call | solution.py:491
  34.4 1.1 %pair.1 = bf16[4,32,16,256]{3,2,1,0:T(8,128)(2,1)} custom-call(bf16[4,32,16,256]{3,2,1,0:T(8,128)(2,1)S(1)} %copy-done.2, bf16[4,32,16,256]{3,2,1,0:T(8,128)(2,1)S(1)} %collective-permute-done.2.right_ref), custom_call_target="tpu_custom_call" | custom-call | tf_op jit(solution)/shard_map/pair/pallas_call | solution.py:513
  35.5 3.9 %all-to-all-start = ((bf16[4,32,16,256]{3,2,1,0:T(8,128)(2,1)}), bf16[4,32,16,256]{3,2,1,0:T(8,128)(2,1)S(1)}, u32[]{:S(2)}, u32[]{:S(2)}) async-start(bf16[4,32,16,256]{3,2,1,0:T(8,128)(2,1)} %pair.1), calls=%async_computation | async-start | bytes 2097152 | tf_op jit(solution)/shard_map/all_to_all | solution.py:655
  39.4 2.2 %collective-permute-start.4 = (bf16[2,3,32,256]{3,2,1,0:T(8,128)(2,1)}, bf16[2,3,32,256]{3,2,1,0:T(8,128)(2,1)S(1)}, u32[]{:S(2)}, u32[]{:S(2)}) collective-permute-start(bf16[2,3,32,256]{3,2,1,0:T(8,128)(2,1)} %get-tuple-element.40), channel_id=1, source_target_pairs={{1,0},{2,1},{3,2},{4,3},{5,4},{6,5},{7,6},{8,7},{9,8},{10,9},{11,1... | collective-permute-start | bytes 294920 | tf_op jit(solution)/shard_map/ppermute | solution.py:657
  41.6 2.2 %collective-permute-done.4.next_ref = bf16[2,3,32,256]{3,2,1,0:T(8,128)(2,1)S(1)} collective-permute-done((bf16[2,3,32,256]{3,2,1,0:T(8,128)(2,1)}, bf16[2,3,32,256]{3,2,1,0:T(8,128)(2,1)S(1)}, u32[]{:S(2)}, u32[]{:S(2)}) %collective-permute-start.4) | collective-permute-done | bytes 98336 | tf_op jit(solution)/shard_map/ppermute | solution.py:657
  43.8 3.7 %collective-permute-done.3.prev_ref = bf16[2,3,32,256]{3,2,1,0:T(8,128)(2,1)S(1)} collective-permute-done((bf16[2,3,32,256]{3,2,1,0:T(8,128)(2,1)S(1)}, bf16[2,3,32,256]{3,2,1,0:T(8,128)(2,1)S(1)}, u32[]{:S(2)}, u32[]{:S(2)}) %collective-permute-start.3) | collective-permute-done | bytes 98336 | tf_op jit(solution)/shard_map/ppermute | solution.py:656
  47.5 0.6 copy-done.7
  48.1 3.1 %all-to-all-done.pieces_ref = bf16[4,32,16,256]{3,2,1,0:T(8,128)(2,1)S(1)} async-done(((bf16[4,32,16,256]{3,2,1,0:T(8,128)(2,1)}), bf16[4,32,16,256]{3,2,1,0:T(8,128)(2,1)S(1)}, u32[]{:S(2)}, u32[]{:S(2)}) %all-to-all-start) | async-done | bytes 1048608 | tf_op jit(solution)/shard_map/all_to_all | solution.py:655
  51.2 0.1 added.1
  51.4 17.3 %all_to_all.15 = bf16[32,16,256]{2,1,0:T(8,128)(2,1)S(1)} all-to-all(bf16[32,16,256]{2,1,0:T(8,128)(2,1)S(1)} %added.1), channel_id=1, replica_groups={{0,1,2,3,4,5,6,7,8,9,10,11,12,13,14,15,128,129,130,131,132,133,134,135,..., dimensions={0} | all-to-all | bytes 524288 | tf_op jit(solution)/shard_map/all_to_all | solution.py:660
  68.7 0.7 broadcast_in_dim.12
  69.3 5.5 %all-to-all-start.2 = ((bf16[16,16,256]{2,1,0:T(8,128)(2,1)}), bf16[16,16,256]{2,1,0:T(8,128)(2,1)S(1)}, u32[]{:S(2)}, u32[]{:S(2)}) async-start(bf16[16,16,256]{2,1,0:T(8,128)(2,1)} %broadcast_in_dim.12), calls=%async_computation.2 | async-start | bytes 262144 | tf_op jit(solution)/shard_map/all_to_all | solution.py:665
  74.8 0.9 %copy-done.8 = bf16[2,3,32,256]{3,2,1,0:T(8,128)(2,1)S(1)} copy-done((bf16[2,3,32,256]{3,2,1,0:T(8,128)(2,1)S(1)}, bf16[2,3,32,256]{3,2,1,0:T(8,128)(2,1)}, u32[]{:S(2)}) %copy-start.8) | copy-done | bytes 98328
  75.7 4.3 %fields.1 = bf16[2,32,32,256]{3,2,1,0:T(8,128)(2,1)} custom-call(s32[4,16]{1,0:T(4,128)S(1)} %bitcast.24, s32[4,16]{1,0:T(4,128)S(1)} %bitcast.26, bf16[2,1024,256]{2,1,0:T(8,128)(2,1)S(1)} %copy-done.5, bf16[2,3,32,256]{3,2,1,0:T(8,128)(2,1)S(1)} %copy-done.6, bf16[2,3,32,256]{3,2,1,0:T(8,128)(2,1)S(1)} %copy-done.8, ...), custom_call_target="tpu_custom_call" | custom-call | flops 2415919104 | bytes 4194304 | tf_op jit(solution)/shard_map/fields/pallas_call | solution.py:546
  80.0 2.5 %all-to-all-done.2.whole_ref = bf16[16,16,256]{2,1,0:T(8,128)(2,1)S(1)} async-done(((bf16[16,16,256]{2,1,0:T(8,128)(2,1)}), bf16[16,16,256]{2,1,0:T(8,128)(2,1)S(1)}, u32[]{:S(2)}, u32[]{:S(2)}) %all-to-all-start.2) | async-done | bytes 131104 | tf_op jit(solution)/shard_map/all_to_all | solution.py:665
  82.4 0.7 finish.1
  (23 shorter events, 0.1 us)
Async XLA Ops:
  0.6 1.2 %copy-start = (bf16[1,1,2,32,32,256]{5,4,3,2,1,0:T(8,128)(2,1)S(1)}, bf16[1,1,2,32,32,256]{5,4,3,2,1,0:T(8,128)(2,1)}, u32[]{:S(2)}) copy-start(bf16[1,1,2,32,32,256]{5,4,3,2,1,0:T(8,128)(2,1)} %param.11) | copy-start | bytes 3145732
  2.0 12.8 %collective-permute-start = (bf16[2,3,32,256]{3,2,1,0:T(8,128)(2,1)S(1)}, bf16[2,3,32,256]{3,2,1,0:T(8,128)(2,1)S(1)}, u32[]{:S(2)}, u32[]{:S(2)}) collective-permute-start(bf16[2,3,32,256]{3,2,1,0:T(8,128)(2,1)S(1)} %get-tuple-element.31), channel_id=1, source_target_pairs={{0,1},{1,2},{2,3},{3,4},{4,5},{5,6},{6,7},{7,8},{8,9},{9,10},{10,1... | collective-permute-start | bytes 294920 | tf_op jit(solution)/shard_map/ppermute | solution.py:633
  4.5 10.3 %collective-permute-start.1 = (bf16[2,3,32,256]{3,2,1,0:T(8,128)(2,1)S(1)}, bf16[2,3,32,256]{3,2,1,0:T(8,128)(2,1)S(1)}, u32[]{:S(2)}, u32[]{:S(2)}) collective-permute-start(bf16[2,3,32,256]{3,2,1,0:T(8,128)(2,1)S(1)} %get-tuple-element.32), channel_id=1, source_target_pairs={{1,0},{2,1},{3,2},{4,3},{5,4},{6,5},{7,6},{8,7},{9,8},{10,9},{11,1... | collective-permute-start | bytes 294920 | tf_op jit(solution)/shard_map/ppermute | solution.py:634
  14.8 0.6 copy-start.9
  14.8 0.6 copy-start.10
  30.4 3.9 %copy-start.2 = (bf16[4,32,16,256]{3,2,1,0:T(8,128)(2,1)S(1)}, bf16[4,32,16,256]{3,2,1,0:T(8,128)(2,1)}, u32[]{:S(2)}) copy-start(bf16[4,32,16,256]{3,2,1,0:T(8,128)(2,1)} %get-tuple-element.33.left_ref) | copy-start | bytes 3145732
  30.4 3.9 %collective-permute-start.2 = (bf16[4,32,16,256]{3,2,1,0:T(8,128)(2,1)}, bf16[4,32,16,256]{3,2,1,0:T(8,128)(2,1)S(1)}, u32[]{:S(2)}, u32[]{:S(2)}) collective-permute-start(bf16[4,32,16,256]{3,2,1,0:T(8,128)(2,1)} %get-tuple-element.34), channel_id=1, source_target_pairs={{0,16},{16,0},{1,17},{17,1},{2,18},{18,2},{3,19},{19,3},{4,20},{20... | collective-permute-start | bytes 3145736 | tf_op jit(solution)/shard_map/ppermute | solution.py:651
  34.3 7.2 %copy-start.6 = (bf16[2,3,32,256]{3,2,1,0:T(8,128)(2,1)S(1)}, bf16[2,3,32,256]{3,2,1,0:T(8,128)(2,1)}, u32[]{:S(2)}) copy-start(bf16[2,3,32,256]{3,2,1,0:T(8,128)(2,1)} %get-tuple-element.39.own_ref) | copy-start | bytes 294916
  35.5 39.3 %copy-start.1 = (bf16[9,256,256]{2,1,0:T(8,128)(2,1)S(1)}, bf16[9,256,256]{2,1,0:T(8,128)(2,1)}, u32[]{:S(2)}) copy-start(bf16[9,256,256]{2,1,0:T(8,128)(2,1)} %param.15) | copy-start | bytes 3538948
  35.5 39.3 %copy-start.3 = (s32[16,4]{0,1:T(4,128)S(1)}, s32[16,4]{0,1:T(4,128)}, u32[]{:S(2)}) copy-start(s32[16,4]{0,1:T(4,128)} %param.20) | copy-start | bytes 772
  35.5 39.3 %copy-start.4 = (s32[16,4]{0,1:T(4,128)S(1)}, s32[16,4]{0,1:T(4,128)}, u32[]{:S(2)}) copy-start(s32[16,4]{0,1:T(4,128)} %param.21) | copy-start | bytes 772
  35.5 39.3 %copy-start.5 = (bf16[2,1024,256]{2,1,0:T(8,128)(2,1)S(1)}, bf16[2,1024,256]{2,1,0:T(8,128)(2,1)}, u32[]{:S(2)}) copy-start(bf16[2,1024,256]{2,1,0:T(8,128)(2,1)} %get-tuple-element.35.part_conv_ref) | copy-start | bytes 3145732
  35.5 15.7 %all-to-all-start = ((bf16[4,32,16,256]{3,2,1,0:T(8,128)(2,1)}), bf16[4,32,16,256]{3,2,1,0:T(8,128)(2,1)S(1)}, u32[]{:S(2)}, u32[]{:S(2)}) async-start(bf16[4,32,16,256]{3,2,1,0:T(8,128)(2,1)} %pair.1), calls=%async_computation | async-start | bytes 2097152 | tf_op jit(solution)/shard_map/all_to_all | solution.py:655
  39.4 4.4 %collective-permute-start.4 = (bf16[2,3,32,256]{3,2,1,0:T(8,128)(2,1)}, bf16[2,3,32,256]{3,2,1,0:T(8,128)(2,1)S(1)}, u32[]{:S(2)}, u32[]{:S(2)}) collective-permute-start(bf16[2,3,32,256]{3,2,1,0:T(8,128)(2,1)} %get-tuple-element.40), channel_id=1, source_target_pairs={{1,0},{2,1},{3,2},{4,3},{5,4},{6,5},{7,6},{8,7},{9,8},{10,9},{11,1... | collective-permute-start | bytes 294920 | tf_op jit(solution)/shard_map/ppermute | solution.py:657
  41.6 5.9 %collective-permute-start.3 = (bf16[2,3,32,256]{3,2,1,0:T(8,128)(2,1)S(1)}, bf16[2,3,32,256]{3,2,1,0:T(8,128)(2,1)S(1)}, u32[]{:S(2)}, u32[]{:S(2)}) collective-permute-start(bf16[2,3,32,256]{3,2,1,0:T(8,128)(2,1)S(1)} %copy-done.6), channel_id=1, source_target_pairs={{0,1},{1,2},{2,3},{3,4},{4,5},{5,6},{6,7},{7,8},{8,9},{9,10},{10,1... | collective-permute-start | bytes 294920 | tf_op jit(solution)/shard_map/ppermute | solution.py:656
  47.5 0.6 copy-start.7
  69.3 13.1 %all-to-all-start.2 = ((bf16[16,16,256]{2,1,0:T(8,128)(2,1)}), bf16[16,16,256]{2,1,0:T(8,128)(2,1)S(1)}, u32[]{:S(2)}, u32[]{:S(2)}) async-start(bf16[16,16,256]{2,1,0:T(8,128)(2,1)} %broadcast_in_dim.12), calls=%async_computation.2 | async-start | bytes 262144 | tf_op jit(solution)/shard_map/all_to_all | solution.py:665
  74.8 0.9 %copy-start.8 = (bf16[2,3,32,256]{3,2,1,0:T(8,128)(2,1)S(1)}, bf16[2,3,32,256]{3,2,1,0:T(8,128)(2,1)}, u32[]{:S(2)}) copy-start(bf16[2,3,32,256]{3,2,1,0:T(8,128)(2,1)} %copy-done.7) | copy-start | bytes 294916

commit v8 on v7

--- a/solution.py
+++ b/solution.py
@@ -524,19 +524,27 @@
     )(left, right)
 
 
-def added_kernel(pieces_ref, out_ref):
-    total = pieces_ref[0].astype(F32)
-    for k in range(1, pieces_ref.shape[0]):
-        total = total + pieces_ref[k].astype(F32)
-    out_ref[...] = total.astype(BF)
+def added_kernel(pieces_ref, out, out_ref, sems):
+    stores = []
+    for k in range(4):
+        rows = pl.ds(8 * k, 8)
+        total = pieces_ref[0, rows].astype(F32)
+        for piece in range(1, pieces_ref.shape[0]):
+            total = total + pieces_ref[piece, rows].astype(F32)
+        out_ref[rows] = total.astype(BF)
+        stores.append(pltpu.make_async_copy(out_ref.at[rows], out.at[rows], sems.at[k]))
+        stores[k].start()
+    for store in stores:
+        store.wait()
 
 
 def added_call(pieces):
     return pl.pallas_call(
         added_kernel,
-        out_shape=shape((32, 16, C)),
+        out_shape=shape(pieces.shape[1:]),
         in_specs=[in_vmem()],
-        out_specs=in_vmem(),
+        out_specs=pl.BlockSpec(memory_space=pl.ANY),
+        scratch_shapes=[pltpu.VMEM(pieces.shape[1:], BF), pltpu.SemaphoreType.DMA((4,))],
         compiler_params=params(8),
         name="added",
     )(pieces)
@@ -657,13 +665,12 @@
     following = lax.ppermute(out_prev, belt, BACK)
     held, prev, following = lax.optimization_barrier((held, prev, following))
     held = added_call(held)
+    grad_fields = fields_call(*seams, part_conv, out_next, prev, following, conv)
     held = lax.all_to_all(held, EVERY, 0, 0, axis_index_groups=SECOND, tiled=True)
-    held, prev, following = lax.optimization_barrier((held, prev, following))
     held = added(held).astype(BF)
-    grad_fields = fields_call(*seams, part_conv, out_next, prev, following, conv)
+    held, grad_fields = lax.optimization_barrier((held, grad_fields))
     whole = jnp.broadcast_to(held[None], (16, 16, C))
     whole = lax.all_to_all(whole, dp, 0, 0, tiled=True)
-    whole, grad_fields = lax.optimization_barrier((whole, grad_fields))
     grad_conv, grad_update, grad_reset, grad_candidate, grad_head = finish_call(whole)
     return (
         grad_fields[None, None],

time: 83.6 us -> 83.6 us (level)
  blocking collectives: 17.3 us -> 12.9 us
  waiting for transfers between devices: 11.5 us -> 15.5 us
    all_to_all x1, blocking collectives: 17.3 us -> 12.9 us  [body(): whole = lax.all_to_all(whole, dp, 0, 0, tiled=True)]
    all_to_all x1, waiting for transfers between devices: 2.46 us -> 6.49 us  [body(): lax.all_to_all(held, EVERY, 0, 0, axis_index_groups=SECOND, tiled=True)]
where the time goes in v8:
time: 83.6 us; the launch traced here: 83.2 us
  Pallas kernels  30 us (36%)
  starting transfers between devices  20.4 us (24%)
  waiting for transfers between devices  15.5 us (19%)
  blocking collectives  12.9 us (15%)
  local copies, waits for them, and re-layouts  3.44 us (4%)
    pallas_call x1, Pallas kernels, main_call(): pl.pallas_call(main_kernel, out_shape=(shape((CELLS, C), F32), shape((STE...  14.9 us
    all_to_all x1, blocking collectives, body(): whole = lax.all_to_all(whole, dp, 0, 0, tiled=True)  12.9 us
    all_to_all x1, waiting for transfers between devices, body(): lax.all_to_all(held, EVERY, 0, 0, axis_index_groups=SECOND, tiled=True)  6.49 us
    all_to_all x1, starting transfers between devices, body(): lax.all_to_all(held, EVERY, 0, 0, axis_index_groups=SECOND, tiled=True)  5.77 us
    pallas_call x1, Pallas kernels, early_call(): pl.pallas_call(early_kernel, out_shape=shape(raw, F32), in_specs=[anywher...  5.29 us
    ppermute x1, starting transfers between devices, body(): following = lax.ppermute(to_prev, belt, BACK)  4.96 us
    pallas_call x1, Pallas kernels, fields_call(): pl.pallas_call(fields_kernel, out_shape=shape((STEPS, SIDE, SIDE, C)), in...  4.26 us
    all_to_all x1, starting transfers between devices, body(): lax.all_to_all(held, EVERY, 0, 0, axis_index_groups=FIRST, tiled=True)  3.87 us
  transfers between devices with their start and end apart: 7, of which 4 were waited for; matrix products, arithmetic and copies ran while one was open for 0% of the time, Pallas kernels for 15%

profile of v8, /device:TPU:1, one launch (start us, length us, event | category | flops | bytes accessed | tf_op | source)
XLA Modules:
  0.0 83.2 jit_solution(10679514695633159561)
XLA Ops:
  0.6 1.2 %copy-done = bf16[1,1,2,32,32,256]{5,4,3,2,1,0:T(8,128)(2,1)S(1)} copy-done((bf16[1,1,2,32,32,256]{5,4,3,2,1,0:T(8,128)(2,1)S(1)}, bf16[1,1,2,32,32,256]{5,4,3,2,1,0:T(8,128)(2,1)}, u32[]{:S(2)}) %copy-start) | copy-done | bytes 1048600
  1.9 0.1 edges.1
  2.0 2.5 %collective-permute-start = (bf16[2,3,32,256]{3,2,1,0:T(8,128)(2,1)S(1)}, bf16[2,3,32,256]{3,2,1,0:T(8,128)(2,1)S(1)}, u32[]{:S(2)}, u32[]{:S(2)}) collective-permute-start(bf16[2,3,32,256]{3,2,1,0:T(8,128)(2,1)S(1)} %get-tuple-element.28), channel_id=1, source_target_pairs={{0,1},{1,2},{2,3},{3,4},{4,5},{5,6},{6,7},{7,8},{8,9},{9,10},{10,1... | collective-permute-start | bytes 294920 | tf_op jit(solution)/shard_map/ppermute | solution.py:641
  4.5 5.0 %collective-permute-start.1 = (bf16[2,3,32,256]{3,2,1,0:T(8,128)(2,1)S(1)}, bf16[2,3,32,256]{3,2,1,0:T(8,128)(2,1)S(1)}, u32[]{:S(2)}, u32[]{:S(2)}) collective-permute-start(bf16[2,3,32,256]{3,2,1,0:T(8,128)(2,1)S(1)} %get-tuple-element.29), channel_id=1, source_target_pairs={{1,0},{2,1},{3,2},{4,3},{5,4},{6,5},{7,6},{8,7},{9,8},{10,9},{11,1... | collective-permute-start | bytes 294920 | tf_op jit(solution)/shard_map/ppermute | solution.py:642
  9.5 5.3 %early.1 = f32[2,1024,256]{2,1,0:T(8,128)} custom-call(bf16[2,32,32,256]{3,2,1,0:T(8,128)(2,1)} %bitcast.101, bf16[2304,256]{1,0:T(8,128)(2,1)} %bitcast.104), custom_call_target="tpu_custom_call" | custom-call | flops 2415919104 | bytes 5242880 | tf_op jit(solution)/shard_map/early/pallas_call | solution.py:439
  14.8 0.6 copy-done.9
  15.4 14.9 %steps.1 = (f32[1024,256]{1,0:T(8,128)}, bf16[2,1024,256]{2,1,0:T(8,128)(2,1)}, bf16[4,32,16,256]{3,2,1,0:T(8,128)(2,1)}, bf16[4,32,16,256]{3,2,1,0:T(8,128)(2,1)}) custom-call(s32[4,16]{1,0:T(4,128)} %bitcast.108, s32[4,16]{1,0:T(4,128)} %bitcast.110, bf16[2,32,32,256]{3,2,1,0:T(8,128)(2,1)} %bitcast.102, bf16[2,3,32,256]{3,2,1,0:T(8,128)(2,1)} %copy-done.9, ...), custom_call_target="tpu_custom_call" | custom-call | tf_op jit(solution)/shard_map/steps/pallas_call | solution.py:461
  30.4 1.1 %collective-permute-start.2 = (bf16[4,32,16,256]{3,2,1,0:T(8,128)(2,1)}, bf16[4,32,16,256]{3,2,1,0:T(8,128)(2,1)S(1)}, u32[]{:S(2)}, u32[]{:S(2)}) collective-permute-start(bf16[4,32,16,256]{3,2,1,0:T(8,128)(2,1)} %get-tuple-element.31), channel_id=1, source_target_pairs={{0,16},{16,0},{1,17},{17,1},{2,18},{18,2},{3,19},{19,3},{4,20},{20... | collective-permute-start | bytes 3145736 | tf_op jit(solution)/shard_map/ppermute | solution.py:659
  31.5 2.9 %outside.1 = (bf16[2,3,32,256]{3,2,1,0:T(8,128)(2,1)}, bf16[2,3,32,256]{3,2,1,0:T(8,128)(2,1)}) custom-call(bf16[2,32,32,256]{3,2,1,0:T(8,128)(2,1)} %bitcast.112, bf16[2304,256]{1,0:T(8,128)(2,1)} %bitcast.106), custom_call_target="tpu_custom_call" | custom-call | flops 1073741824 | bytes 3145728 | tf_op jit(solution)/shard_map/outside/pallas_call | solution.py:491
  34.4 1.1 %pair.1 = bf16[4,32,16,256]{3,2,1,0:T(8,128)(2,1)} custom-call(bf16[4,32,16,256]{3,2,1,0:T(8,128)(2,1)S(1)} %copy-done.2, bf16[4,32,16,256]{3,2,1,0:T(8,128)(2,1)S(1)} %collective-permute-done.2.right_ref), custom_call_target="tpu_custom_call" | custom-call | tf_op jit(solution)/shard_map/pair/pallas_call | solution.py:513
  35.5 3.9 %all-to-all-start = ((bf16[4,32,16,256]{3,2,1,0:T(8,128)(2,1)}), bf16[4,32,16,256]{3,2,1,0:T(8,128)(2,1)S(1)}, u32[]{:S(2)}, u32[]{:S(2)}) async-start(bf16[4,32,16,256]{3,2,1,0:T(8,128)(2,1)} %pair.1), calls=%async_computation | async-start | bytes 2097152 | tf_op jit(solution)/shard_map/all_to_all | solution.py:663
  39.4 2.2 %collective-permute-start.4 = (bf16[2,3,32,256]{3,2,1,0:T(8,128)(2,1)}, bf16[2,3,32,256]{3,2,1,0:T(8,128)(2,1)S(1)}, u32[]{:S(2)}, u32[]{:S(2)}) collective-permute-start(bf16[2,3,32,256]{3,2,1,0:T(8,128)(2,1)} %get-tuple-element.37), channel_id=1, source_target_pairs={{1,0},{2,1},{3,2},{4,3},{5,4},{6,5},{7,6},{8,7},{9,8},{10,9},{11,1... | collective-permute-start | bytes 294920 | tf_op jit(solution)/shard_map/ppermute | solution.py:665
  41.6 2.2 %collective-permute-done.4.next_ref = bf16[2,3,32,256]{3,2,1,0:T(8,128)(2,1)S(1)} collective-permute-done((bf16[2,3,32,256]{3,2,1,0:T(8,128)(2,1)}, bf16[2,3,32,256]{3,2,1,0:T(8,128)(2,1)S(1)}, u32[]{:S(2)}, u32[]{:S(2)}) %collective-permute-start.4) | collective-permute-done | bytes 98336 | tf_op jit(solution)/shard_map/ppermute | solution.py:665
  43.8 3.7 %collective-permute-done.3.prev_ref = bf16[2,3,32,256]{3,2,1,0:T(8,128)(2,1)S(1)} collective-permute-done((bf16[2,3,32,256]{3,2,1,0:T(8,128)(2,1)S(1)}, bf16[2,3,32,256]{3,2,1,0:T(8,128)(2,1)S(1)}, u32[]{:S(2)}, u32[]{:S(2)}) %collective-permute-start.3) | collective-permute-done | bytes 98336 | tf_op jit(solution)/shard_map/ppermute | solution.py:664
  47.5 0.6 copy-done.7
  48.1 3.1 %all-to-all-done.pieces_ref = bf16[4,32,16,256]{3,2,1,0:T(8,128)(2,1)S(1)} async-done(((bf16[4,32,16,256]{3,2,1,0:T(8,128)(2,1)}), bf16[4,32,16,256]{3,2,1,0:T(8,128)(2,1)S(1)}, u32[]{:S(2)}, u32[]{:S(2)}) %all-to-all-start) | async-done | bytes 1048608 | tf_op jit(solution)/shard_map/all_to_all | solution.py:663
  51.2 0.8 added.1
  52.0 5.8 %all-to-all-start.1 = ((bf16[32,16,256]{2,1,0:T(8,128)(2,1)}), bf16[32,16,256]{2,1,0:T(8,128)(2,1)S(1)}, u32[]{:S(2)}, u32[]{:S(2)}) async-start(bf16[32,16,256]{2,1,0:T(8,128)(2,1)} %added.1), calls=%async_computation.1 | async-start | bytes 524288 | tf_op jit(solution)/shard_map/all_to_all | solution.py:669
  57.8 0.9 %copy-done.8 = bf16[2,3,32,256]{3,2,1,0:T(8,128)(2,1)S(1)} copy-done((bf16[2,3,32,256]{3,2,1,0:T(8,128)(2,1)S(1)}, bf16[2,3,32,256]{3,2,1,0:T(8,128)(2,1)}, u32[]{:S(2)}) %copy-start.8) | copy-done | bytes 98328
  58.7 4.3 %fields.1 = bf16[2,32,32,256]{3,2,1,0:T(8,128)(2,1)} custom-call(s32[4,16]{1,0:T(4,128)S(1)} %bitcast.109, s32[4,16]{1,0:T(4,128)S(1)} %bitcast.111, bf16[2,1024,256]{2,1,0:T(8,128)(2,1)S(1)} %copy-done.5, bf16[2,3,32,256]{3,2,1,0:T(8,128)(2,1)S(1)} %copy-done.6, bf16[2,3,32,256]{3,2,1,0:T(8,128)(2,1)S(1)} %copy-done.8, ...), custom_call_target="tpu_custom_call" | custom-call | flops 2415919104 | bytes 4194304 | tf_op jit(solution)/shard_map/fields/pallas_call | solution.py:554
  63.0 6.5 %all-to-all-done.1 = bf16[32,16,256]{2,1,0:T(8,128)(2,1)S(1)} async-done(((bf16[32,16,256]{2,1,0:T(8,128)(2,1)}), bf16[32,16,256]{2,1,0:T(8,128)(2,1)S(1)}, u32[]{:S(2)}, u32[]{:S(2)}) %all-to-all-start.1) | async-done | bytes 262176 | tf_op jit(solution)/shard_map/all_to_all | solution.py:669
  69.5 0.1 fusion
  69.6 12.9 %all_to_all.15.whole_ref = bf16[16,16,256]{2,1,0:T(8,128)(2,1)S(1)} all-to-all(bf16[16,16,256]{2,1,0:T(8,128)(2,1)S(1)} %broadcast_in_dim.10), channel_id=1, replica_groups=mesh['x_hi'=2,'y'=4,'core'=2,'x_lo'=2,'z'=8] {'x_hi','y','core'}, dimensions={0} | all-to-all | bytes 262144 | tf_op jit(solution)/shard_map/all_to_all | solution.py:673
  82.5 0.7 finish.1
  (23 shorter events, 0.1 us)
Async XLA Ops:
  0.6 1.2 %copy-start = (bf16[1,1,2,32,32,256]{5,4,3,2,1,0:T(8,128)(2,1)S(1)}, bf16[1,1,2,32,32,256]{5,4,3,2,1,0:T(8,128)(2,1)}, u32[]{:S(2)}) copy-start(bf16[1,1,2,32,32,256]{5,4,3,2,1,0:T(8,128)(2,1)} %param.11) | copy-start | bytes 3145732
  2.0 12.8 %collective-permute-start = (bf16[2,3,32,256]{3,2,1,0:T(8,128)(2,1)S(1)}, bf16[2,3,32,256]{3,2,1,0:T(8,128)(2,1)S(1)}, u32[]{:S(2)}, u32[]{:S(2)}) collective-permute-start(bf16[2,3,32,256]{3,2,1,0:T(8,128)(2,1)S(1)} %get-tuple-element.28), channel_id=1, source_target_pairs={{0,1},{1,2},{2,3},{3,4},{4,5},{5,6},{6,7},{7,8},{8,9},{9,10},{10,1... | collective-permute-start | bytes 294920 | tf_op jit(solution)/shard_map/ppermute | solution.py:641
  4.5 10.3 %collective-permute-start.1 = (bf16[2,3,32,256]{3,2,1,0:T(8,128)(2,1)S(1)}, bf16[2,3,32,256]{3,2,1,0:T(8,128)(2,1)S(1)}, u32[]{:S(2)}, u32[]{:S(2)}) collective-permute-start(bf16[2,3,32,256]{3,2,1,0:T(8,128)(2,1)S(1)} %get-tuple-element.29), channel_id=1, source_target_pairs={{1,0},{2,1},{3,2},{4,3},{5,4},{6,5},{7,6},{8,7},{9,8},{10,9},{11,1... | collective-permute-start | bytes 294920 | tf_op jit(solution)/shard_map/ppermute | solution.py:642
  14.8 0.6 copy-start.9
  14.8 0.6 copy-start.10
  30.4 3.9 %copy-start.2 = (bf16[4,32,16,256]{3,2,1,0:T(8,128)(2,1)S(1)}, bf16[4,32,16,256]{3,2,1,0:T(8,128)(2,1)}, u32[]{:S(2)}) copy-start(bf16[4,32,16,256]{3,2,1,0:T(8,128)(2,1)} %get-tuple-element.30.left_ref) | copy-start | bytes 3145732
  30.4 3.9 %collective-permute-start.2 = (bf16[4,32,16,256]{3,2,1,0:T(8,128)(2,1)}, bf16[4,32,16,256]{3,2,1,0:T(8,128)(2,1)S(1)}, u32[]{:S(2)}, u32[]{:S(2)}) collective-permute-start(bf16[4,32,16,256]{3,2,1,0:T(8,128)(2,1)} %get-tuple-element.31), channel_id=1, source_target_pairs={{0,16},{16,0},{1,17},{17,1},{2,18},{18,2},{3,19},{19,3},{4,20},{20... | collective-permute-start | bytes 3145736 | tf_op jit(solution)/shard_map/ppermute | solution.py:659
  34.3 7.2 %copy-start.6 = (bf16[2,3,32,256]{3,2,1,0:T(8,128)(2,1)S(1)}, bf16[2,3,32,256]{3,2,1,0:T(8,128)(2,1)}, u32[]{:S(2)}) copy-start(bf16[2,3,32,256]{3,2,1,0:T(8,128)(2,1)} %get-tuple-element.36.own_ref) | copy-start | bytes 294916
  35.5 22.3 %copy-start.1 = (bf16[9,256,256]{2,1,0:T(8,128)(2,1)S(1)}, bf16[9,256,256]{2,1,0:T(8,128)(2,1)}, u32[]{:S(2)}) copy-start(bf16[9,256,256]{2,1,0:T(8,128)(2,1)} %param.15) | copy-start | bytes 3538948
  35.5 22.3 %copy-start.3 = (s32[16,4]{0,1:T(4,128)S(1)}, s32[16,4]{0,1:T(4,128)}, u32[]{:S(2)}) copy-start(s32[16,4]{0,1:T(4,128)} %param.20) | copy-start | bytes 772
  35.5 22.3 %copy-start.4 = (s32[16,4]{0,1:T(4,128)S(1)}, s32[16,4]{0,1:T(4,128)}, u32[]{:S(2)}) copy-start(s32[16,4]{0,1:T(4,128)} %param.21) | copy-start | bytes 772
  35.5 22.3 %copy-start.5 = (bf16[2,1024,256]{2,1,0:T(8,128)(2,1)S(1)}, bf16[2,1024,256]{2,1,0:T(8,128)(2,1)}, u32[]{:S(2)}) copy-start(bf16[2,1024,256]{2,1,0:T(8,128)(2,1)} %get-tuple-element.32.part_conv_ref) | copy-start | bytes 3145732
  35.5 15.7 %all-to-all-start = ((bf16[4,32,16,256]{3,2,1,0:T(8,128)(2,1)}), bf16[4,32,16,256]{3,2,1,0:T(8,128)(2,1)S(1)}, u32[]{:S(2)}, u32[]{:S(2)}) async-start(bf16[4,32,16,256]{3,2,1,0:T(8,128)(2,1)} %pair.1), calls=%async_computation | async-start | bytes 2097152 | tf_op jit(solution)/shard_map/all_to_all | solution.py:663
  39.4 4.4 %collective-permute-start.4 = (bf16[2,3,32,256]{3,2,1,0:T(8,128)(2,1)}, bf16[2,3,32,256]{3,2,1,0:T(8,128)(2,1)S(1)}, u32[]{:S(2)}, u32[]{:S(2)}) collective-permute-start(bf16[2,3,32,256]{3,2,1,0:T(8,128)(2,1)} %get-tuple-element.37), channel_id=1, source_target_pairs={{1,0},{2,1},{3,2},{4,3},{5,4},{6,5},{7,6},{8,7},{9,8},{10,9},{11,1... | collective-permute-start | bytes 294920 | tf_op jit(solution)/shard_map/ppermute | solution.py:665
  41.6 5.9 %collective-permute-start.3 = (bf16[2,3,32,256]{3,2,1,0:T(8,128)(2,1)S(1)}, bf16[2,3,32,256]{3,2,1,0:T(8,128)(2,1)S(1)}, u32[]{:S(2)}, u32[]{:S(2)}) collective-permute-start(bf16[2,3,32,256]{3,2,1,0:T(8,128)(2,1)S(1)} %copy-done.6), channel_id=1, source_target_pairs={{0,1},{1,2},{2,3},{3,4},{4,5},{5,6},{6,7},{7,8},{8,9},{9,10},{10,1... | collective-permute-start | bytes 294920 | tf_op jit(solution)/shard_map/ppermute | solution.py:664
  47.5 0.6 copy-start.7
  52.0 17.5 %all-to-all-start.1 = ((bf16[32,16,256]{2,1,0:T(8,128)(2,1)}), bf16[32,16,256]{2,1,0:T(8,128)(2,1)S(1)}, u32[]{:S(2)}, u32[]{:S(2)}) async-start(bf16[32,16,256]{2,1,0:T(8,128)(2,1)} %added.1), calls=%async_computation.1 | async-start | bytes 524288 | tf_op jit(solution)/shard_map/all_to_all | solution.py:669
  57.8 0.9 %copy-start.8 = (bf16[2,3,32,256]{3,2,1,0:T(8,128)(2,1)S(1)}, bf16[2,3,32,256]{3,2,1,0:T(8,128)(2,1)}, u32[]{:S(2)}) copy-start(bf16[2,3,32,256]{3,2,1,0:T(8,128)(2,1)} %copy-done.7) | copy-start | bytes 294916

commit v9 on v7

--- a/solution.py
+++ b/solution.py
@@ -542,6 +542,30 @@
     )(pieces)
 
 
+def spread_kernel(pieces_ref, out, total_ref, sems):
+    total = pieces_ref[0].astype(F32)
+    for k in range(1, pieces_ref.shape[0]):
+        total = total + pieces_ref[k].astype(F32)
+    total_ref[...] = total.astype(BF)
+    stores = [pltpu.make_async_copy(total_ref, out.at[k], sems.at[k]) for k in range(16)]
+    for store in stores:
+        store.start()
+    for store in stores:
+        store.wait()
+
+
+def spread_call(pieces):
+    return pl.pallas_call(
+        spread_kernel,
+        out_shape=shape((16, 16, C)),
+        in_specs=[in_vmem()],
+        out_specs=pl.BlockSpec(memory_space=pl.ANY),
+        scratch_shapes=[pltpu.VMEM((16, C), BF), pltpu.SemaphoreType.DMA((16,))],
+        compiler_params=params(8),
+        name="spread",
+    )(pieces)
+
+
 def fields_call(*args):
     return pl.pallas_call(
         fields_kernel,
@@ -583,13 +607,6 @@
         compiler_params=params(8),
         name="finish",
     )(whole)
-
-
-def added(pieces):
-    total = pieces[0].astype(F32)
-    for k in range(1, pieces.shape[0]):
-        total = total + pieces[k].astype(F32)
-    return total
 
 
 EVERY = ("x_hi", "y", "core", "x_lo", "z")
@@ -659,9 +676,8 @@
     held = added_call(held)
     held = lax.all_to_all(held, EVERY, 0, 0, axis_index_groups=SECOND, tiled=True)
     held, prev, following = lax.optimization_barrier((held, prev, following))
-    held = added(held).astype(BF)
     grad_fields = fields_call(*seams, part_conv, out_next, prev, following, conv)
-    whole = jnp.broadcast_to(held[None], (16, 16, C))
+    whole = spread_call(held)
     whole = lax.all_to_all(whole, dp, 0, 0, tiled=True)
     whole, grad_fields = lax.optimization_barrier((whole, grad_fields))
     grad_conv, grad_update, grad_reset, grad_candidate, grad_head = finish_call(whole)

time: 83.6 us -> 83.7 us (level)
    pallas_call x0 -> x1, Pallas kernels: none -> 0.84 us  [spread_call(): pl.pallas_call(spread_kernel, out_shape=shape((16, 16, C)), in_specs=[in_...]
where the time goes in v9:
time: 83.7 us; the launch traced here: 83.3 us
  Pallas kernels  30.2 us (36%)
  starting transfers between devices  20.1 us (24%)
  blocking collectives  17.3 us (21%)
  waiting for transfers between devices  11.5 us (14%)
  local copies, waits for them, and re-layouts  3.42 us (4%)
    all_to_all x1, blocking collectives, body(): lax.all_to_all(held, EVERY, 0, 0, axis_index_groups=SECOND, tiled=True)  17.3 us
    pallas_call x1, Pallas kernels, main_call(): pl.pallas_call(main_kernel, out_shape=(shape((CELLS, C), F32), shape((STE...  14.9 us
    all_to_all x1, starting transfers between devices, body(): whole = lax.all_to_all(whole, dp, 0, 0, tiled=True)  5.46 us
    pallas_call x1, Pallas kernels, early_call(): pl.pallas_call(early_kernel, out_shape=shape(raw, F32), in_specs=[anywher...  5.29 us
    ppermute x1, starting transfers between devices, body(): following = lax.ppermute(to_prev, belt, BACK)  4.96 us
    pallas_call x1, Pallas kernels, fields_call(): pl.pallas_call(fields_kernel, out_shape=shape((STEPS, SIDE, SIDE, C)), in...  4.26 us
    all_to_all x1, starting transfers between devices, body(): lax.all_to_all(held, EVERY, 0, 0, axis_index_groups=FIRST, tiled=True)  3.87 us
    ppermute x1, waiting for transfers between devices, body(): prev = lax.ppermute(out_next, belt, RING)  3.68 us
  transfers between devices with their start and end apart: 7, of which 4 were waited for; matrix products, arithmetic and copies ran while one was open for 0% of the time, Pallas kernels for 15%

profile of v9, /device:TPU:1, one launch (start us, length us, event | category | flops | bytes accessed | tf_op | source)
XLA Modules:
  0.0 83.3 jit_solution(14754416021287287515)
XLA Ops:
  0.6 1.2 %copy-done = bf16[1,1,2,32,32,256]{5,4,3,2,1,0:T(8,128)(2,1)S(1)} copy-done((bf16[1,1,2,32,32,256]{5,4,3,2,1,0:T(8,128)(2,1)S(1)}, bf16[1,1,2,32,32,256]{5,4,3,2,1,0:T(8,128)(2,1)}, u32[]{:S(2)}) %copy-start) | copy-done | bytes 1048600
  1.9 0.1 edges.1
  2.0 2.5 %collective-permute-start = (bf16[2,3,32,256]{3,2,1,0:T(8,128)(2,1)S(1)}, bf16[2,3,32,256]{3,2,1,0:T(8,128)(2,1)S(1)}, u32[]{:S(2)}, u32[]{:S(2)}) collective-permute-start(bf16[2,3,32,256]{3,2,1,0:T(8,128)(2,1)S(1)} %get-tuple-element.31), channel_id=1, source_target_pairs={{0,1},{1,2},{2,3},{3,4},{4,5},{5,6},{6,7},{7,8},{8,9},{9,10},{10,1... | collective-permute-start | bytes 294920 | tf_op jit(solution)/shard_map/ppermute | solution.py:650
  4.5 5.0 %collective-permute-start.1 = (bf16[2,3,32,256]{3,2,1,0:T(8,128)(2,1)S(1)}, bf16[2,3,32,256]{3,2,1,0:T(8,128)(2,1)S(1)}, u32[]{:S(2)}, u32[]{:S(2)}) collective-permute-start(bf16[2,3,32,256]{3,2,1,0:T(8,128)(2,1)S(1)} %get-tuple-element.32), channel_id=1, source_target_pairs={{1,0},{2,1},{3,2},{4,3},{5,4},{6,5},{7,6},{8,7},{9,8},{10,9},{11,1... | collective-permute-start | bytes 294920 | tf_op jit(solution)/shard_map/ppermute | solution.py:651
  9.5 5.3 %early.1 = f32[2,1024,256]{2,1,0:T(8,128)} custom-call(bf16[2,32,32,256]{3,2,1,0:T(8,128)(2,1)} %bitcast.14, bf16[2304,256]{1,0:T(8,128)(2,1)} %bitcast.17), custom_call_target="tpu_custom_call" | custom-call | flops 2415919104 | bytes 5242880 | tf_op jit(solution)/shard_map/early/pallas_call | solution.py:439
  14.8 0.6 copy-done.9
  15.4 14.9 %steps.1 = (f32[1024,256]{1,0:T(8,128)}, bf16[2,1024,256]{2,1,0:T(8,128)(2,1)}, bf16[4,32,16,256]{3,2,1,0:T(8,128)(2,1)}, bf16[4,32,16,256]{3,2,1,0:T(8,128)(2,1)}) custom-call(s32[4,16]{1,0:T(4,128)} %bitcast.21, s32[4,16]{1,0:T(4,128)} %bitcast.23, bf16[2,32,32,256]{3,2,1,0:T(8,128)(2,1)} %bitcast.15, bf16[2,3,32,256]{3,2,1,0:T(8,128)(2,1)} %copy-done.9, ...), custom_call_target="tpu_custom_call" | custom-call | tf_op jit(solution)/shard_map/steps/pallas_call | solution.py:461
  30.4 1.1 %collective-permute-start.2 = (bf16[4,32,16,256]{3,2,1,0:T(8,128)(2,1)}, bf16[4,32,16,256]{3,2,1,0:T(8,128)(2,1)S(1)}, u32[]{:S(2)}, u32[]{:S(2)}) collective-permute-start(bf16[4,32,16,256]{3,2,1,0:T(8,128)(2,1)} %get-tuple-element.34), channel_id=1, source_target_pairs={{0,16},{16,0},{1,17},{17,1},{2,18},{18,2},{3,19},{19,3},{4,20},{20... | collective-permute-start | bytes 3145736 | tf_op jit(solution)/shard_map/ppermute | solution.py:668
  31.5 2.9 %outside.1 = (bf16[2,3,32,256]{3,2,1,0:T(8,128)(2,1)}, bf16[2,3,32,256]{3,2,1,0:T(8,128)(2,1)}) custom-call(bf16[2,32,32,256]{3,2,1,0:T(8,128)(2,1)} %bitcast.25, bf16[2304,256]{1,0:T(8,128)(2,1)} %bitcast.19), custom_call_target="tpu_custom_call" | custom-call | flops 1073741824 | bytes 3145728 | tf_op jit(solution)/shard_map/outside/pallas_call | solution.py:491
  34.4 1.1 %pair.1 = bf16[4,32,16,256]{3,2,1,0:T(8,128)(2,1)} custom-call(bf16[4,32,16,256]{3,2,1,0:T(8,128)(2,1)S(1)} %copy-done.2, bf16[4,32,16,256]{3,2,1,0:T(8,128)(2,1)S(1)} %collective-permute-done.2.right_ref), custom_call_target="tpu_custom_call" | custom-call | tf_op jit(solution)/shard_map/pair/pallas_call | solution.py:513
  35.5 3.9 %all-to-all-start = ((bf16[4,32,16,256]{3,2,1,0:T(8,128)(2,1)}), bf16[4,32,16,256]{3,2,1,0:T(8,128)(2,1)S(1)}, u32[]{:S(2)}, u32[]{:S(2)}) async-start(bf16[4,32,16,256]{3,2,1,0:T(8,128)(2,1)} %pair.1), calls=%async_computation | async-start | bytes 2097152 | tf_op jit(solution)/shard_map/all_to_all | solution.py:672
  39.4 2.2 %collective-permute-start.4 = (bf16[2,3,32,256]{3,2,1,0:T(8,128)(2,1)}, bf16[2,3,32,256]{3,2,1,0:T(8,128)(2,1)S(1)}, u32[]{:S(2)}, u32[]{:S(2)}) collective-permute-start(bf16[2,3,32,256]{3,2,1,0:T(8,128)(2,1)} %get-tuple-element.40), channel_id=1, source_target_pairs={{1,0},{2,1},{3,2},{4,3},{5,4},{6,5},{7,6},{8,7},{9,8},{10,9},{11,1... | collective-permute-start | bytes 294920 | tf_op jit(solution)/shard_map/ppermute | solution.py:674
  41.6 2.2 %collective-permute-done.4.next_ref = bf16[2,3,32,256]{3,2,1,0:T(8,128)(2,1)S(1)} collective-permute-done((bf16[2,3,32,256]{3,2,1,0:T(8,128)(2,1)}, bf16[2,3,32,256]{3,2,1,0:T(8,128)(2,1)S(1)}, u32[]{:S(2)}, u32[]{:S(2)}) %collective-permute-start.4) | collective-permute-done | bytes 98336 | tf_op jit(solution)/shard_map/ppermute | solution.py:674
  43.8 3.7 %collective-permute-done.3.prev_ref = bf16[2,3,32,256]{3,2,1,0:T(8,128)(2,1)S(1)} collective-permute-done((bf16[2,3,32,256]{3,2,1,0:T(8,128)(2,1)S(1)}, bf16[2,3,32,256]{3,2,1,0:T(8,128)(2,1)S(1)}, u32[]{:S(2)}, u32[]{:S(2)}) %collective-permute-start.3) | collective-permute-done | bytes 98336 | tf_op jit(solution)/shard_map/ppermute | solution.py:673
  47.5 0.6 copy-done.7
  48.1 3.1 %all-to-all-done.pieces_ref = bf16[4,32,16,256]{3,2,1,0:T(8,128)(2,1)S(1)} async-done(((bf16[4,32,16,256]{3,2,1,0:T(8,128)(2,1)}), bf16[4,32,16,256]{3,2,1,0:T(8,128)(2,1)S(1)}, u32[]{:S(2)}, u32[]{:S(2)}) %all-to-all-start) | async-done | bytes 1048608 | tf_op jit(solution)/shard_map/all_to_all | solution.py:672
  51.2 0.1 added.1
  51.4 17.3 %all_to_all.15.pieces_ref = bf16[32,16,256]{2,1,0:T(8,128)(2,1)S(1)} all-to-all(bf16[32,16,256]{2,1,0:T(8,128)(2,1)S(1)} %added.1), channel_id=1, replica_groups={{0,1,2,3,4,5,6,7,8,9,10,11,12,13,14,15,128,129,130,131,132,133,134,135,..., dimensions={0} | all-to-all | bytes 524288 | tf_op jit(solution)/shard_map/all_to_all | solution.py:677
  68.6 0.8 %spread.1 = bf16[16,16,256]{2,1,0:T(8,128)(2,1)} custom-call(bf16[32,16,256]{2,1,0:T(8,128)(2,1)S(1)} %all_to_all.15.pieces_ref), custom_call_target="tpu_custom_call" | custom-call | tf_op jit(solution)/shard_map/spread/pallas_call | solution.py:558
  69.5 5.5 %all-to-all-start.2 = ((bf16[16,16,256]{2,1,0:T(8,128)(2,1)}), bf16[16,16,256]{2,1,0:T(8,128)(2,1)S(1)}, u32[]{:S(2)}, u32[]{:S(2)}) async-start(bf16[16,16,256]{2,1,0:T(8,128)(2,1)} %spread.1), calls=%async_computation.2 | async-start | bytes 262144 | tf_op jit(solution)/shard_map/all_to_all | solution.py:681
  75.0 0.9 %copy-done.8 = bf16[2,3,32,256]{3,2,1,0:T(8,128)(2,1)S(1)} copy-done((bf16[2,3,32,256]{3,2,1,0:T(8,128)(2,1)S(1)}, bf16[2,3,32,256]{3,2,1,0:T(8,128)(2,1)}, u32[]{:S(2)}) %copy-start.8) | copy-done | bytes 98328
  75.9 4.3 %fields.1 = bf16[2,32,32,256]{3,2,1,0:T(8,128)(2,1)} custom-call(s32[4,16]{1,0:T(4,128)S(1)} %bitcast.22, s32[4,16]{1,0:T(4,128)S(1)} %bitcast.24, bf16[2,1024,256]{2,1,0:T(8,128)(2,1)S(1)} %copy-done.5, bf16[2,3,32,256]{3,2,1,0:T(8,128)(2,1)S(1)} %copy-done.6, bf16[2,3,32,256]{3,2,1,0:T(8,128)(2,1)S(1)} %copy-done.8, ...), custom_call_target="tpu_custom_call" | custom-call | flops 2415919104 | bytes 4194304 | tf_op jit(solution)/shard_map/fields/pallas_call | solution.py:570
  80.1 2.5 %all-to-all-done.2.whole_ref = bf16[16,16,256]{2,1,0:T(8,128)(2,1)S(1)} async-done(((bf16[16,16,256]{2,1,0:T(8,128)(2,1)}), bf16[16,16,256]{2,1,0:T(8,128)(2,1)S(1)}, u32[]{:S(2)}, u32[]{:S(2)}) %all-to-all-start.2) | async-done | bytes 131104 | tf_op jit(solution)/shard_map/all_to_all | solution.py:681
  82.6 0.7 finish.1
  (22 shorter events, 0.1 us)
Async XLA Ops:
  0.6 1.2 %copy-start = (bf16[1,1,2,32,32,256]{5,4,3,2,1,0:T(8,128)(2,1)S(1)}, bf16[1,1,2,32,32,256]{5,4,3,2,1,0:T(8,128)(2,1)}, u32[]{:S(2)}) copy-start(bf16[1,1,2,32,32,256]{5,4,3,2,1,0:T(8,128)(2,1)} %param.11) | copy-start | bytes 3145732
  2.0 12.8 %collective-permute-start = (bf16[2,3,32,256]{3,2,1,0:T(8,128)(2,1)S(1)}, bf16[2,3,32,256]{3,2,1,0:T(8,128)(2,1)S(1)}, u32[]{:S(2)}, u32[]{:S(2)}) collective-permute-start(bf16[2,3,32,256]{3,2,1,0:T(8,128)(2,1)S(1)} %get-tuple-element.31), channel_id=1, source_target_pairs={{0,1},{1,2},{2,3},{3,4},{4,5},{5,6},{6,7},{7,8},{8,9},{9,10},{10,1... | collective-permute-start | bytes 294920 | tf_op jit(solution)/shard_map/ppermute | solution.py:650
  4.5 10.3 %collective-permute-start.1 = (bf16[2,3,32,256]{3,2,1,0:T(8,128)(2,1)S(1)}, bf16[2,3,32,256]{3,2,1,0:T(8,128)(2,1)S(1)}, u32[]{:S(2)}, u32[]{:S(2)}) collective-permute-start(bf16[2,3,32,256]{3,2,1,0:T(8,128)(2,1)S(1)} %get-tuple-element.32), channel_id=1, source_target_pairs={{1,0},{2,1},{3,2},{4,3},{5,4},{6,5},{7,6},{8,7},{9,8},{10,9},{11,1... | collective-permute-start | bytes 294920 | tf_op jit(solution)/shard_map/ppermute | solution.py:651
  14.8 0.6 copy-start.9
  14.8 0.6 copy-start.10
  30.4 3.9 %copy-start.2 = (bf16[4,32,16,256]{3,2,1,0:T(8,128)(2,1)S(1)}, bf16[4,32,16,256]{3,2,1,0:T(8,128)(2,1)}, u32[]{:S(2)}) copy-start(bf16[4,32,16,256]{3,2,1,0:T(8,128)(2,1)} %get-tuple-element.33.left_ref) | copy-start | bytes 3145732
  30.4 3.9 %collective-permute-start.2 = (bf16[4,32,16,256]{3,2,1,0:T(8,128)(2,1)}, bf16[4,32,16,256]{3,2,1,0:T(8,128)(2,1)S(1)}, u32[]{:S(2)}, u32[]{:S(2)}) collective-permute-start(bf16[4,32,16,256]{3,2,1,0:T(8,128)(2,1)} %get-tuple-element.34), channel_id=1, source_target_pairs={{0,16},{16,0},{1,17},{17,1},{2,18},{18,2},{3,19},{19,3},{4,20},{20... | collective-permute-start | bytes 3145736 | tf_op jit(solution)/shard_map/ppermute | solution.py:668
  34.3 7.2 %copy-start.6 = (bf16[2,3,32,256]{3,2,1,0:T(8,128)(2,1)S(1)}, bf16[2,3,32,256]{3,2,1,0:T(8,128)(2,1)}, u32[]{:S(2)}) copy-start(bf16[2,3,32,256]{3,2,1,0:T(8,128)(2,1)} %get-tuple-element.39.own_ref) | copy-start | bytes 294916
  35.5 39.5 %copy-start.1 = (bf16[9,256,256]{2,1,0:T(8,128)(2,1)S(1)}, bf16[9,256,256]{2,1,0:T(8,128)(2,1)}, u32[]{:S(2)}) copy-start(bf16[9,256,256]{2,1,0:T(8,128)(2,1)} %param.15) | copy-start | bytes 3538948
  35.5 39.5 %copy-start.3 = (s32[16,4]{0,1:T(4,128)S(1)}, s32[16,4]{0,1:T(4,128)}, u32[]{:S(2)}) copy-start(s32[16,4]{0,1:T(4,128)} %param.20) | copy-start | bytes 772
  35.5 39.5 %copy-start.4 = (s32[16,4]{0,1:T(4,128)S(1)}, s32[16,4]{0,1:T(4,128)}, u32[]{:S(2)}) copy-start(s32[16,4]{0,1:T(4,128)} %param.21) | copy-start | bytes 772
  35.5 39.5 %copy-start.5 = (bf16[2,1024,256]{2,1,0:T(8,128)(2,1)S(1)}, bf16[2,1024,256]{2,1,0:T(8,128)(2,1)}, u32[]{:S(2)}) copy-start(bf16[2,1024,256]{2,1,0:T(8,128)(2,1)} %get-tuple-element.35.part_conv_ref) | copy-start | bytes 3145732
  35.5 15.7 %all-to-all-start = ((bf16[4,32,16,256]{3,2,1,0:T(8,128)(2,1)}), bf16[4,32,16,256]{3,2,1,0:T(8,128)(2,1)S(1)}, u32[]{:S(2)}, u32[]{:S(2)}) async-start(bf16[4,32,16,256]{3,2,1,0:T(8,128)(2,1)} %pair.1), calls=%async_computation | async-start | bytes 2097152 | tf_op jit(solution)/shard_map/all_to_all | solution.py:672
  39.4 4.4 %collective-permute-start.4 = (bf16[2,3,32,256]{3,2,1,0:T(8,128)(2,1)}, bf16[2,3,32,256]{3,2,1,0:T(8,128)(2,1)S(1)}, u32[]{:S(2)}, u32[]{:S(2)}) collective-permute-start(bf16[2,3,32,256]{3,2,1,0:T(8,128)(2,1)} %get-tuple-element.40), channel_id=1, source_target_pairs={{1,0},{2,1},{3,2},{4,3},{5,4},{6,5},{7,6},{8,7},{9,8},{10,9},{11,1... | collective-permute-start | bytes 294920 | tf_op jit(solution)/shard_map/ppermute | solution.py:674
  41.6 5.9 %collective-permute-start.3 = (bf16[2,3,32,256]{3,2,1,0:T(8,128)(2,1)S(1)}, bf16[2,3,32,256]{3,2,1,0:T(8,128)(2,1)S(1)}, u32[]{:S(2)}, u32[]{:S(2)}) collective-permute-start(bf16[2,3,32,256]{3,2,1,0:T(8,128)(2,1)S(1)} %copy-done.6), channel_id=1, source_target_pairs={{0,1},{1,2},{2,3},{3,4},{4,5},{5,6},{6,7},{7,8},{8,9},{9,10},{10,1... | collective-permute-start | bytes 294920 | tf_op jit(solution)/shard_map/ppermute | solution.py:673
  47.5 0.6 copy-start.7
  69.5 13.1 %all-to-all-start.2 = ((bf16[16,16,256]{2,1,0:T(8,128)(2,1)}), bf16[16,16,256]{2,1,0:T(8,128)(2,1)S(1)}, u32[]{:S(2)}, u32[]{:S(2)}) async-start(bf16[16,16,256]{2,1,0:T(8,128)(2,1)} %spread.1), calls=%async_computation.2 | async-start | bytes 262144 | tf_op jit(solution)/shard_map/all_to_all | solution.py:681
  75.0 0.9 %copy-start.8 = (bf16[2,3,32,256]{3,2,1,0:T(8,128)(2,1)S(1)}, bf16[2,3,32,256]{3,2,1,0:T(8,128)(2,1)}, u32[]{:S(2)}) copy-start(bf16[2,3,32,256]{3,2,1,0:T(8,128)(2,1)} %copy-done.7) | copy-start | bytes 294916
